TPU v7x, 32 devices: a whole 2x2x4 slice. The times are simulated.
32 devices in a mesh: shard: 4 (over z), ctx: 4 (over y, core), tp: 2 (over x).
Axes of the slice: x: 2, y: 2, z: 4, core: 2. Of those that a mesh axis runs over, the one named last changes fastest.
Arguments:
- activations: bfloat16 [12, 1024, 2048], P('shard', 'ctx'), may hold values from -6 to 6
- segments: int32 [12, 1024], P('shard'), may hold values from 0 to 3, as said below
- query_weight: bfloat16 [2048, 2048], P('shard', 'tp'), may hold values from -0.125 to 0.125
- key_weight: bfloat16 [2048, 256], P('shard', 'tp'), may hold values from -0.125 to 0.125
- value_weight: bfloat16 [2048, 256], P('shard', 'tp'), may hold values from -0.125 to 0.125
- output_weight: bfloat16 [2048, 2048], P('tp', 'shard'), may hold values from -2 to 2
- gate_weight: bfloat16 [2048, 5632], P('shard', 'tp'), may hold values from -0.125 to 0.125
- up_weight: bfloat16 [2048, 5632], P('shard', 'tp'), may hold values from -0.125 to 0.125
- down_weight: bfloat16 [5632, 2048], P('tp', 'shard'), may hold values from -0.078125 to 0.078125
- attn_gain: bfloat16 [2048], P('shard'), may hold values from 0.099609375 to 1.8984375
- ffn_gain: bfloat16 [2048], P('shard'), may hold values from 0.099609375 to 1.8984375
- cotangent: bfloat16 [12, 1024, 2048], P('shard', 'ctx'), may hold values from -6 to 6
Outputs:
- block_out: bfloat16 [12, 1024, 2048], P('shard', 'ctx')
- input_grad: float32 [12, 1024, 2048], P('shard', 'ctx')
- query_grad: float32 [2048, 2048], P('shard', 'tp')
- key_grad: float32 [2048, 256], P('shard', 'tp')
- value_grad: float32 [2048, 256], P('shard', 'tp')
- output_grad: float32 [2048, 2048], P('tp', 'shard')
- gate_grad: float32 [2048, 5632], P('shard', 'tp')
- up_grad: float32 [2048, 5632], P('shard', 'tp')
- down_grad: float32 [5632, 2048], P('tp', 'shard')
- attn_gain_grad: float32 [2048], P('shard')
- ffn_gain_grad: float32 [2048], P('shard')
Inputs may be any that keep to these rules, and one draw needn't show every extreme that they name: Along each sequence the numbers start at 0 and rise by one at each new document (the last segment may be padding). In each aligned group of 3 sequences exactly one is all 0; each other sequence has exactly 4 segments.
All inputs are finite; a program needn't handle non-finite values.
Results may differ from a plain program's by a relative error of at most 0.013.
Values may be sent and summed in bfloat16 or wider, within the bound.
No kernel may reach another device: no remote copies, remote signals or barrier semaphores. Data moves between devices by JAX's collectives and lax.ppermute only.
A program may use at most 384 MiB of HBM per device.

v0:
```python
import jax
import jax.numpy as jnp
from jax import lax
from jax.sharding import PartitionSpec as P

HEAD = 64


epsilon = 1e-05
rope_base = 10000.0
masked_value = -1e30


def rope_tables(positions):
    half_dim = HEAD // 2
    frequency = jnp.power(rope_base, -jnp.arange(half_dim, dtype=jnp.float32) / half_dim)
    angles = positions.astype(jnp.float32)[..., None] * frequency
    return (jnp.cos(angles)[..., None, :], jnp.sin(angles)[..., None, :])


def rotate(values, cosine, sine_table):
    half_dim = HEAD // 2
    first_half = values[..., :half_dim]
    second_half = values[..., half_dim:]
    return jnp.concatenate(
        [
            first_half * cosine - second_half * sine_table,
            second_half * cosine + first_half * sine_table,
        ],
        -1,
    )


def rotate_back(values, cosine, sine_table):
    half_dim = HEAD // 2
    first_half = values[..., :half_dim]
    second_half = values[..., half_dim:]
    return jnp.concatenate(
        [
            first_half * cosine + second_half * sine_table,
            second_half * cosine - first_half * sine_table,
        ],
        -1,
    )


def contract_rows(left_side, right_side):
    return lax.dot_general(
        left_side, right_side, (((0,), (0,)), ((), ())), preferred_element_type=jnp.float32
    )


def contract_cols(left_side, right_side):
    return lax.dot_general(
        left_side, right_side, (((1,), (1,)), ((), ())), preferred_element_type=jnp.float32
    )


def tp_total(partial_sum):
    return lax.psum(partial_sum, "tp")


def grad_slices(lefts, rights, gain_terms):
    blocks = [contract_rows(left_side, right_side) for left_side, right_side in zip(lefts, rights)]
    summed = lax.psum_scatter(jnp.concatenate(blocks, 1), "shard", scatter_dimension=0, tiled=True)
    return lax.psum((summed, gain_terms), "ctx")


def body(
    activations,
    segments,
    query_weight,
    key_weight,
    value_weight,
    output_weight,
    gate_weight,
    up_weight,
    down_weight,
    attn_gain,
    ffn_gain,
    cotangent,
):
    seq_here, block_len, model_width = activations.shape
    seq_len = segments.shape[1]
    row_total = seq_here * block_len
    query_cols = query_weight.shape[1]
    kv_width = key_weight.shape[1]
    query_heads = query_cols // HEAD
    kv_heads = kv_width // HEAD
    group_size = query_heads // kv_heads
    hidden_width = gate_weight.shape[1]
    inputs = activations.reshape(row_total, model_width).astype(jnp.float32)
    inv_one = lax.rsqrt(jnp.mean(inputs * inputs, -1, keepdims=True) + epsilon)
    unit_one = inputs * inv_one
    key_index = jnp.arange(seq_len, dtype=jnp.int32)
    previous = jnp.concatenate([segments[:, :1], segments[:, :-1]], 1)
    starts_at = jnp.where(segments != previous, key_index[None, :], 0)
    doc_pos = key_index[None, :] - lax.cummax(starts_at, axis=1)
    offset = lax.axis_index("ctx") * block_len
    query_pos = lax.dynamic_slice_in_dim(doc_pos, offset, block_len, 1)
    query_seg = lax.dynamic_slice_in_dim(segments, offset, block_len, 1)
    query_index = offset + jnp.arange(block_len, dtype=jnp.int32)
    cosine, sine_table = rope_tables(query_pos)
    gain_piece = lax.all_gather(attn_gain, "shard", axis=0, tiled=True)
    query_piece = lax.all_gather(query_weight, "shard", axis=0, tiled=True)
    key_piece = lax.all_gather(key_weight, "shard", axis=0, tiled=True)
    value_piece = lax.all_gather(value_weight, "shard", axis=0, tiled=True)
    columns = unit_one
    normed_piece = (columns * gain_piece.astype(jnp.float32)[None, :]).astype(jnp.bfloat16)
    queries = jnp.dot(normed_piece, query_piece, preferred_element_type=jnp.float32)
    key_proj = jnp.dot(normed_piece, key_piece, preferred_element_type=jnp.float32)
    values = jnp.dot(normed_piece, value_piece, preferred_element_type=jnp.float32)
    normed = normed_piece
    gain_full = gain_piece
    queries, key_proj, values, normed_one, gain_one = (queries, key_proj, values, normed, gain_full)
    query_round = (
        rotate(queries.reshape(seq_here, block_len, query_heads, HEAD), cosine, sine_table)
        * HEAD ** (-0.5)
    ).astype(jnp.bfloat16)
    key_round = (
        rotate(key_proj.reshape(seq_here, block_len, kv_heads, HEAD), cosine, sine_table)
        .astype(jnp.bfloat16)
        .reshape(seq_here, block_len, kv_width)
    )
    value_round = values.astype(jnp.bfloat16).reshape(seq_here, block_len, kv_width)
    keys_all, values_all = (
        lax.all_gather(key_round, "ctx", axis=1, tiled=True),
        lax.all_gather(value_round, "ctx", axis=1, tiled=True),
    )
    query_group = query_round.reshape(seq_here, block_len, kv_heads, group_size, HEAD)

    def scores_of(query_block, key_block, segment_row, seg_block):
        allowed = (seg_block[:, None] == segment_row[None, :]) & (
            query_index[:, None] >= key_index[None, :]
        )
        scores = jnp.einsum(
            "ighd,jgd->ghij",
            query_block,
            key_block.reshape(seq_len, kv_heads, HEAD),
            preferred_element_type=jnp.float32,
        )
        return (jnp.where(allowed, scores, masked_value), allowed)

    def attend(entries):
        query_block, key_block, value_block, segment_row, seg_block = entries
        masked, allowed = scores_of(query_block, key_block, segment_row, seg_block)
        row_max = jnp.max(masked, -1, keepdims=True)
        exp_terms = jnp.where(allowed, jnp.exp(masked - row_max), 0.0)
        totals = jnp.sum(exp_terms, -1, keepdims=True)
        weights_round = (exp_terms / totals).astype(jnp.bfloat16)
        attended = jnp.einsum(
            "ghij,jgd->ighd",
            weights_round,
            value_block.reshape(seq_len, kv_heads, HEAD),
            preferred_element_type=jnp.float32,
        )
        return (attended.reshape(block_len, query_cols), row_max[..., 0] + jnp.log(totals[..., 0]))

    mixed_all, log_sums = lax.map(attend, (query_group, keys_all, values_all, segments, query_seg))
    mixed_round = mixed_all.reshape(row_total, query_cols).astype(jnp.bfloat16)
    residual = inputs + tp_total(
        jnp.dot(
            mixed_round,
            lax.all_gather(output_weight, "shard", axis=1, tiled=True),
            preferred_element_type=jnp.float32,
        )
    )
    inv_two = lax.rsqrt(jnp.mean(residual * residual, -1, keepdims=True) + epsilon)
    unit_two = residual * inv_two
    gain_piece = lax.all_gather(ffn_gain, "shard", axis=0, tiled=True)
    gate_piece = lax.all_gather(gate_weight, "shard", axis=0, tiled=True)
    up_piece = lax.all_gather(up_weight, "shard", axis=0, tiled=True)
    columns = unit_two
    normed_piece = (columns * gain_piece.astype(jnp.float32)[None, :]).astype(jnp.bfloat16)
    gate_proj = jnp.dot(normed_piece, gate_piece, preferred_element_type=jnp.float32)
    up_value = jnp.dot(normed_piece, up_piece, preferred_element_type=jnp.float32)
    normed = normed_piece
    gain_full = gain_piece
    gate_proj, up_value, normed_two, gain_two = (gate_proj, up_value, normed, gain_full)
    sigmoid_gate = jax.nn.sigmoid(gate_proj)
    silu_gate = gate_proj * sigmoid_gate
    hidden = (silu_gate * up_value).astype(jnp.bfloat16)
    ffn_branch = tp_total(
        jnp.dot(
            hidden,
            lax.all_gather(down_weight, "shard", axis=1, tiled=True),
            preferred_element_type=jnp.float32,
        )
    )
    block_out = (
        (residual + ffn_branch).astype(jnp.bfloat16).reshape(seq_here, block_len, model_width)
    )
    grad_out = cotangent.reshape(row_total, model_width)
    residual_delta = grad_out.astype(jnp.float32)
    columns = grad_out
    hidden_delta = contract_cols(columns, lax.all_gather(down_weight, "shard", axis=1, tiled=True))
    gate_delta = (
        hidden_delta * up_value * sigmoid_gate * (1.0 + gate_proj * (1.0 - sigmoid_gate))
    ).astype(jnp.bfloat16)
    up_delta = (hidden_delta * silu_gate).astype(jnp.bfloat16)
    gate_piece = lax.all_gather(gate_weight, "shard", axis=0, tiled=True)
    up_piece = lax.all_gather(up_weight, "shard", axis=0, tiled=True)
    column_block = contract_cols(gate_delta, gate_piece) + contract_cols(up_delta, up_piece)
    normed_two_delta = tp_total(column_block)
    ffn_gain_term = jnp.sum(normed_two_delta * unit_two, 0)
    scaled_two = normed_two_delta * gain_two.astype(jnp.float32)
    residual_delta = residual_delta + inv_two * (
        scaled_two - unit_two * jnp.mean(scaled_two * unit_two, -1, keepdims=True)
    )
    ffn_lefts = (normed_two, normed_two, grad_out)
    ffn_rights = (gate_delta, up_delta, hidden)
    ffn_slices, ffn_gain_sum = grad_slices(ffn_lefts, ffn_rights, ffn_gain_term)
    residual_round = residual_delta.astype(jnp.bfloat16)
    columns = residual_round
    mixed_delta = contract_cols(columns, lax.all_gather(output_weight, "shard", axis=1, tiled=True))
    mixed_delta_round = mixed_delta.astype(jnp.bfloat16).reshape(
        seq_here, block_len, kv_heads, group_size, HEAD
    )

    def attend_back(entries):
        query_block, key_block, value_block, segment_row, seg_block, log_block, delta_block = (
            entries
        )
        masked, allowed = scores_of(query_block, key_block, segment_row, seg_block)
        probs_full = jnp.where(allowed, jnp.exp(masked - log_block[..., None]), 0.0)
        probs_delta = jnp.einsum(
            "ighd,jgd->ghij",
            delta_block,
            value_block.reshape(seq_len, kv_heads, HEAD),
            preferred_element_type=jnp.float32,
        )
        inner_sum = jnp.sum(probs_full * probs_delta, -1, keepdims=True)
        score_delta = (probs_full * (probs_delta - inner_sum)).astype(jnp.bfloat16)
        query_part = jnp.einsum(
            "ghij,jgd->ighd",
            score_delta,
            key_block.reshape(seq_len, kv_heads, HEAD),
            preferred_element_type=jnp.float32,
        )
        return (
            query_part.reshape(block_len, query_cols),
            score_delta,
            probs_full.astype(jnp.bfloat16),
        )

    query_parts, score_deltas, probs_round = lax.map(
        attend_back,
        (query_group, keys_all, values_all, segments, query_seg, log_sums, mixed_delta_round),
    )
    row_count = lax.axis_size("ctx") * block_len
    key_part = jnp.einsum(
        "sghij,sighd->jsgd", score_deltas, query_group, preferred_element_type=jnp.float32
    )
    value_part = jnp.einsum(
        "sghij,sighd->jsgd", probs_round, mixed_delta_round, preferred_element_type=jnp.float32
    )
    kv_deltas = jnp.transpose(
        lax.psum_scatter(
            jnp.concatenate(
                [
                    key_part.reshape(row_count, seq_here, kv_width),
                    value_part.reshape(row_count, seq_here, kv_width),
                ],
                2,
            ),
            "ctx",
            scatter_dimension=0,
            tiled=True,
        ),
        (1, 0, 2),
    )
    key_delta = (
        rotate_back(
            kv_deltas[:, :, :kv_width].reshape(seq_here, block_len, kv_heads, HEAD),
            cosine,
            sine_table,
        )
        .astype(jnp.bfloat16)
        .reshape(row_total, kv_width)
    )
    value_delta = kv_deltas[:, :, kv_width:].astype(jnp.bfloat16).reshape(row_total, kv_width)
    query_delta = (
        rotate_back(
            query_parts.reshape(seq_here, block_len, query_heads, HEAD) * HEAD ** (-0.5),
            cosine,
            sine_table,
        )
        .astype(jnp.bfloat16)
        .reshape(row_total, query_cols)
    )
    query_piece = lax.all_gather(query_weight, "shard", axis=0, tiled=True)
    key_piece = lax.all_gather(key_weight, "shard", axis=0, tiled=True)
    value_piece = lax.all_gather(value_weight, "shard", axis=0, tiled=True)
    column_block = (
        contract_cols(query_delta, query_piece)
        + contract_cols(key_delta, key_piece)
        + contract_cols(value_delta, value_piece)
    )
    normed_one_delta = tp_total(column_block)
    attn_gain_term = jnp.sum(normed_one_delta * unit_one, 0)
    scaled_one = normed_one_delta * gain_one.astype(jnp.float32)
    input_grad = residual_delta + inv_one * (
        scaled_one - unit_one * jnp.mean(scaled_one * unit_one, -1, keepdims=True)
    )
    attn_lefts = (normed_one, normed_one, normed_one, residual_round)
    attn_rights = (query_delta, key_delta, value_delta, mixed_round)
    attn_slices, attn_gain_sum = grad_slices(attn_lefts, attn_rights, attn_gain_term)
    attn_gain_grad, ffn_gain_grad = (
        lax.psum_scatter(attn_gain_sum, "shard", scatter_dimension=0, tiled=True),
        lax.psum_scatter(ffn_gain_sum, "shard", scatter_dimension=0, tiled=True),
    )
    query_grad = attn_slices[:, :query_cols]
    key_grad = attn_slices[:, query_cols : query_cols + kv_width]
    value_grad = attn_slices[:, query_cols + kv_width : query_cols + 2 * kv_width]
    output_grad = jnp.transpose(attn_slices[:, query_cols + 2 * kv_width :])
    gate_grad = ffn_slices[:, :hidden_width]
    up_grad = ffn_slices[:, hidden_width : 2 * hidden_width]
    down_grad = jnp.transpose(ffn_slices[:, 2 * hidden_width :])
    return (
        block_out,
        input_grad.reshape(seq_here, block_len, model_width),
        query_grad,
        key_grad,
        value_grad,
        output_grad,
        gate_grad,
        up_grad,
        down_grad,
        attn_gain_grad,
        ffn_gain_grad,
    )


def solution(mesh):
    return jax.shard_map(
        body,
        mesh=mesh,
        in_specs=(
            P("shard", "ctx", None),
            P("shard", None),
            P("shard", "tp"),
            P("shard", "tp"),
            P("shard", "tp"),
            P("tp", "shard"),
            P("shard", "tp"),
            P("shard", "tp"),
            P("tp", "shard"),
            P("shard"),
            P("shard"),
            P("shard", "ctx", None),
        ),
        out_specs=(
            P("shard", "ctx", None),
            P("shard", "ctx", None),
            P("shard", "tp"),
            P("shard", "tp"),
            P("shard", "tp"),
            P("tp", "shard"),
            P("shard", "tp"),
            P("shard", "tp"),
            P("tp", "shard"),
            P("shard"),
            P("shard"),
        ),
        check_vma=False,
    )
```

profile of v0, /device:TPU:1, one launch (start us, length us, event | category | flops | bytes accessed | tf_op | source)
XLA Modules:
  0.0 3541.0 jit_solution(8347071439219005526)
XLA Ops:
  26.4 20.9 all_gather.41
  48.5 12.7 all_gather.42
  61.2 22.0 all_gather.43
  122.3 86.0 %while.28 = (s32[]{:T(128)}, bf16[3,256,1024]{2,1,0:T(8,128)(2,1)}, f32[3,2,8,256]{3,2,1,0:T(8,128)}, bf16[3,1024,128]{1,2,0:T(8,128)(2,1)}, s32[3,256]{1,0:T(4,...) while((s32[]{:T(128)}, bf16[3,256,1024]{2,1,0:T(8,128)(2,1)}, ...), condition=%wide.region_6.7_spmd.clone, body=%wide.region_3.6_spmd.clone.sunk | while | flops 1120661760 | bytes 56247432 | solution.py:159
  229.2 140.2 %all-reduce.12.cloned.1.call-done = f32[768,2048]{1,0:T(8,128)} async-done(((f32[768,2048]{1,0:T(8,128)}), f32[768,2048]{1,0:T(8,128)}) %all-reduce.12.cloned.1.call-update) | async-done | bytes 6291472 | tf_op jit(solution)/shard_map/psum | solution.py:60
  376.4 195.8 %all-gather.12.cloned.1.call-done = bf16[2048,2816]{1,0:T(8,128)(2,1)} async-done(((bf16[512,2816]{1,0:T(8,128)(2,1)}), bf16[2048,2816]{1,0:T(8,128)(2,1)}) %all-gather.12.cloned.1.call-update) | async-done | bytes 11534352 | tf_op jit(solution)/shard_map/all_gather | solution.py:171
  572.2 14.8 fusion.64
  587.0 186.0 %all-gather.14.cloned.1.call-done = bf16[2048,2816]{1,0:T(8,128)(2,1)} async-done(((bf16[512,2816]{1,0:T(8,128)(2,1)}), bf16[2048,2816]{1,0:T(8,128)(2,1)}) %all-gather.14.cloned.1.call-update) | async-done | bytes 11534352 | tf_op jit(solution)/shard_map/all_gather | solution.py:172
  773.0 15.7 fusion.65
  788.7 185.1 %all-gather.16.cloned.1.call-done = bf16[2816,2048]{1,0:T(8,128)(2,1)} async-done(((bf16[2816,512]{1,0:T(8,128)(2,1)}), bf16[2816,2048]{1,0:T(8,128)(2,1)}) %all-gather.16.cloned.1.call-update) | async-done | bytes 11534352 | tf_op jit(solution)/shard_map/all_gather | solution.py:186
  973.8 20.5 multiply_convert_fusion
  994.3 13.4 fusion.67
  1007.7 13.8 convolution_add_fusion
  1021.6 151.2 %all-reduce.14.cloned.1.call-done = f32[768,2048]{1,0:T(8,128)} async-done(((f32[768,2048]{1,0:T(8,128)}), f32[768,2048]{1,0:T(8,128)}) %all-reduce.14.cloned.1.call-update) | async-done | bytes 6291472 | tf_op jit(solution)/shard_map/psum | solution.py:60
  1196.7 112.1 %while.29 = (s32[]{:T(128)}, f32[3,256,1024]{1,2,0:T(8,128)}, bf16[3,2,8,256,1024]{3,4,2,1,0:T(8,128)(2,1)}, bf16[3,2,8,256,1024]{3,4,2,1,0:T(8,128)(2,1)}, bf16...) while((s32[]{:T(128)}, f32[3,256,1024]{1,2,0:T(8,128)}, ...), condition=%wide.region_14.15_spmd.clone, body=%wide.region_12.14_spmd.clone.sunk | while | flops 1661726976 | bytes 124372128 | solution.py:246
  1211.5 16.7 bitcast_dynamic-update-slice_fusion.5
  1248.8 16.7 bitcast_dynamic-update-slice_fusion.5
  1286.0 16.7 bitcast_dynamic-update-slice_fusion.5
  1308.8 13.6 fusion.70
  1322.3 13.6 fusion.69
  1357.0 20.5 reduce-scatter.6.cloned.1.call-done
  1394.4 14.9 convolution_bitcast_fusion
  1409.3 14.8 fusion.73
  1424.1 14.6 fusion.72
  1438.7 44.8 %pad_maximum_fusion = f32[2048,8448]{1,0:T(8,128)} fusion(f32[2048,2816]{1,0:T(8,128)} %convolution_bitcast_fusion, f32[2048,2816]{1,0:T(8,128)} %fusion.73, f32[2048,2816]{1,0:T(8,128)} %fusion.72), kind=kLoop, calls=%fused_computation.55 | loop fusion | flops 34603008 | bytes 138412032 | tf_op jit(solution)/shard_map/concatenate | solution.py:65
  1483.7 15.1 fusion.66
  1513.4 193.0 %reduce-scatter.8.cloned.1.call-done = f32[512,2304]{0,1:T(8,128)} async-done(((f32[2048,2304]{0,1:T(8,128)}), f32[512,2304]{0,1:T(8,128)}) %reduce-scatter.8.cloned.1.call-update) | async-done | bytes 4718608 | tf_op jit(solution)/shard_map/reduce_scatter | solution.py:65
  1706.3 1131.9 %reduce-scatter.10.cloned.1.call-done = f32[512,8448]{1,0:T(8,128)} async-done(((f32[2048,8448]{1,0:T(8,128)}), f32[512,8448]{1,0:T(8,128)}) %reduce-scatter.10.cloned.1.call-update) | async-done | bytes 17301520
  2840.1 290.8 %all-reduce.18.cloned.1.call-done = (f32[768,2048]{1,0:T(8,128)}, f32[768,2048]{1,0:T(8,128)}) async-done(((f32[768,2048]{1,0:T(8,128)}, f32[768,2048]{1,0:T(8,128)}), (f32[768,2048]{1,0:T(8,128)}, f32[768,2048]{1,0:T(8,128)})) %all-reduce.18.cloned.1.call-update) | async-done | bytes 12582928 | tf_op jit(solution)/shard_map/psum | solution.py:60
  3135.4 15.0 all-reduce.5
  3175.8 330.7 %all-reduce.16.cloned.1.call-done = (f32[512,2304]{0,1:T(8,128)}, f32[512,8448]{1,0:T(8,128)}) async-done(((f32[512,2304]{0,1:T(8,128)}, f32[512,8448]{1,0:T(8,128)}), (f32[512,2304]{0,1:T(8,128)}, f32[512,8448]{1,0:T(8,128)})) %all-reduce.16.cloned.1.call-update) | async-done | bytes 22020112 | tf_op jit(solution)/shard_map/psum | solution.py:66
  3515.0 12.7 slice_bitcast_fusion
  (265 shorter events, 356.2 us)
Async XLA Ops:
  7.2 15.9 copy-start.1
  7.2 102.0 %all-gather.8.cloned.1.call-start = ((), (), s32[]{:S(2)}) async-start(), calls=%async_computation.3 | async-start | bytes 5242880 | tf_op jit(solution)/shard_map/all_gather | solution.py:105
  7.9 200.4 %all-gather.10.cloned.1.call-start = ((), (), s32[]{:S(2)}) async-start(), calls=%async_computation.4 | async-start | bytes 5242880 | tf_op jit(solution)/shard_map/all_gather | solution.py:164
  8.7 360.7 %all-reduce.12.cloned.1.call-start = ((), (), s32[]{:S(2)}) async-start(), calls=%async_computation.5 | async-start | bytes 12582912 | tf_op jit(solution)/shard_map/psum | solution.py:60
  25.6 35.6 %copy-start.27 = (s32[3,1024]{1,0:T(4,128)S(1)}, s32[3,1024]{1,0:T(4,128)}, u32[]{:S(2)}) copy-start(s32[3,1024]{1,0:T(4,128)} %param.17) | copy-start | bytes 36868
  26.4 60.3 %copy-start.4 = (bf16[3,256,2048]{2,1,0:T(8,128)(2,1)S(1)}, bf16[3,256,2048]{2,1,0:T(8,128)(2,1)}, u32[]{:S(2)}) copy-start(bf16[3,256,2048]{2,1,0:T(8,128)(2,1)} %fusion.49) | copy-start | bytes 9437188
  48.5 40.5 %copy-start.36 = (f32[32]{0:T(128)S(1)}, f32[32]{0:T(128)}, u32[]{:S(2)}) copy-start(f32[32]{0:T(128)} %multiply_power_fusion) | copy-start | bytes 388
  89.4 31.7 copy-start.19
  89.4 31.7 copy-start.21
  208.3 9.4 copy-start.6
  208.3 9.4 copy-start.33
  217.7 151.7 %copy-start.2 = (bf16[3,256,2048]{2,1,0:T(8,128)(2,1)S(1)}, bf16[3,256,2048]{2,1,0:T(8,128)(2,1)}, u32[]{:S(2)}) copy-start(bf16[3,256,2048]{2,1,0:T(8,128)(2,1)} %param.16) | copy-start | bytes 9437188
  217.7 354.5 %all-gather.12.cloned.1.call-start = ((), (), s32[]{:S(2)}) async-start(), calls=%async_computation.6 | async-start | bytes 14417920 | tf_op jit(solution)/shard_map/all_gather | solution.py:171
  218.3 554.7 %all-gather.14.cloned.1.call-start = ((), (), s32[]{:S(2)}) async-start(), calls=%async_computation.7 | async-start | bytes 14417920 | tf_op jit(solution)/shard_map/all_gather | solution.py:172
  218.9 754.9 %all-gather.16.cloned.1.call-start = ((), (), s32[]{:S(2)}) async-start(), calls=%async_computation.8 | async-start | bytes 14417920 | tf_op jit(solution)/shard_map/all_gather | solution.py:186
  219.5 953.4 %all-reduce.14.cloned.1.call-start = ((), (), s32[]{:S(2)}) async-start(), calls=%async_computation.9 | async-start | bytes 12582912 | tf_op jit(solution)/shard_map/psum | solution.py:60
  376.4 195.9 %copy-start.17 = (bf16[768,2048]{1,0:T(8,128)(2,1)}, bf16[768,2048]{1,0:T(8,128)(2,1)S(1)}, u32[]{:S(2)}) copy-start(bf16[768,2048]{1,0:T(8,128)(2,1)S(1)} %multiply_convert_fusion.3) | copy-start | bytes 9437188
  587.0 386.8 %copy-start.15 = (bf16[3,256,2048]{2,1,0:T(8,128)(2,1)S(1)}, bf16[3,256,2048]{2,1,0:T(8,128)(2,1)}, u32[]{:S(2)}) copy-start(bf16[3,256,2048]{2,1,0:T(8,128)(2,1)} %param.27) | copy-start | bytes 9437188
  994.3 13.4 copy-start.40
  1021.5 355.9 %reduce-scatter.6.cloned.1.call-start = ((), (), s32[]{:S(2)}) async-start(), calls=%async_computation.10 | async-start | bytes 3932160 | tf_op jit(solution)/shard_map/reduce_scatter | solution.py:258
  1322.3 13.6 copy-start.12
  1339.4 366.9 %reduce-scatter.8.cloned.1.call-start = ((), (), s32[]{:S(2)}) async-start(), calls=%async_computation.11 | async-start | bytes 23592960 | tf_op jit(solution)/shard_map/reduce_scatter | solution.py:65
  1392.5 1445.7 %reduce-scatter.10.cloned.1.call-start = ((), (), s32[]{:S(2)}) async-start(), calls=%async_computation.12 | async-start | bytes 86507520
  1394.4 14.9 copy-start.18
  1483.5 15.3 copy-start.26
  1483.5 1647.5 %all-reduce.18.cloned.1.call-start = ((), (), s32[]{:S(2)}) async-start(), calls=%async_computation.14 | async-start | bytes 25165824 | tf_op jit(solution)/shard_map/psum | solution.py:60
  1483.7 15.1 copy-start.14
  1513.3 1993.1 %all-reduce.16.cloned.1.call-start = ((), (), s32[]{:S(2)}) async-start(), calls=%async_computation.13 | async-start | bytes 44040192 | tf_op jit(solution)/shard_map/psum | solution.py:66
  2838.2 292.7 %copy-start.3 = (bf16[3,256,2048]{2,1,0:T(8,128)(2,1)S(1)}, bf16[3,256,2048]{2,1,0:T(8,128)(2,1)}, u32[]{:S(2)}) copy-start(bf16[3,256,2048]{2,1,0:T(8,128)(2,1)} %param.16) | copy-start | bytes 9437188
  2838.2 292.7 %copy-start.29 = (f32[4,1,512]{2,1,0:T(1,128)S(1)}, f32[4,1,512]{2,1,0:T(1,128)}, u32[]{:S(2)}) copy-start(f32[4,1,512]{2,1,0:T(1,128)} %copy-done.28) | copy-start | bytes 24580
  2838.2 292.7 %copy-start.32 = (f32[768]{0:T(1024)S(1)}, f32[768]{0:T(1024)}, u32[]{:S(2)}) copy-start(f32[768]{0:T(1024)} %copy-done.31) | copy-start | bytes 9220
  2838.2 297.1 %copy-start.34 = (f32[2048]{0:T(1024)S(1)}, f32[2048]{0:T(1024)}, u32[]{:S(2)}) copy-start(f32[2048]{0:T(1024)} %get-tuple-element.257) | copy-start | bytes 24580
  (25 other events, 100.8 us)
Sparse Core Ops, SparseCore 0:
  9.6 99.5 all-gather.7
  110.7 79.2 all-gather.9
  217.8 151.4 all-reduce.11
  370.9 201.2 all-gather.11
  573.7 199.2 all-gather.13
  774.5 199.2 all-gather.15
  1021.7 151.1 all-reduce.13
  1339.5 37.9 reduce-scatter.5
  1392.7 313.6 reduce-scatter.7
  1708.5 1129.6 reduce-scatter.9
  2840.7 290.1 all-reduce.17
  3133.4 372.9 all-reduce.15
where the time goes:
time: 3550 us; the launch traced here: 3540 us
  waiting for transfers between devices  2840 us (80%)
  matrix products  307 us (9%)
  other arithmetic  186 us (5%)
  blocking collectives  110 us (3%)
  local copies, waits for them, and re-layouts  80.9 us (2%)
    unnamed x13, waiting for transfers between devices  1130 us
    psum x3, waiting for transfers between devices, tp_total(): return lax.psum(partial_sum, 'tp')  582 us
    psum x1, waiting for transfers between devices, grad_slices(): return lax.psum((summed, gain_terms), 'ctx')  331 us
    all_gather x1, waiting for transfers between devices, body(): gate_piece = lax.all_gather(gate_weight, 'shard', axis=0, tiled=True)  196 us
    reduce_scatter x1, waiting for transfers between devices, grad_slices(): lax.psum_scatter(jnp.concatenate(blocks, 1), 'shard', scatter_dimension=0...  193 us
    all_gather x1, waiting for transfers between devices, body(): up_piece = lax.all_gather(up_weight, 'shard', axis=0, tiled=True)  186 us
    all_gather x1, waiting for transfers between devices, body(): lax.all_gather(down_weight, 'shard', axis=1, tiled=True)  185 us
  transfers between devices with their start and end apart: 12, of which 11 were waited for; matrix products, arithmetic and copies ran while one was open for 9% of the time, Pallas kernels for 0%

commit v1 on v0

v1 whole, which is shorter than its diff:
```python
import jax
import jax.numpy as jnp
from jax import lax
from jax.experimental import pallas as pl
from jax.experimental.pallas import tpu as pltpu
from jax.sharding import PartitionSpec as P

HEAD = 64
HALF = HEAD // 2
epsilon = 1e-05
rope_base = 10000.0
masked_value = -1e30
bf16 = jnp.bfloat16
f32 = jnp.float32

SWAP_LOW = [(0, 1), (1, 0), (2, 3), (3, 2)]
SWAP_HIGH = [(0, 2), (2, 0), (1, 3), (3, 1)]
SWAP_TP = [(0, 1), (1, 0)]


def low_swap(value):
    return lax.ppermute(value, "ctx", SWAP_LOW)


def high_swap(value):
    return lax.ppermute(value, "ctx", SWAP_HIGH)


def dot(left, right, left_dim, right_dim):
    return lax.dot_general(
        left, right, (((left_dim,), (right_dim,)), ((), ())), preferred_element_type=f32
    )


def tp_sum(partial_sum):
    mine = partial_sum.astype(bf16)
    return mine.astype(f32) + lax.ppermute(mine, "tp", SWAP_TP).astype(f32)


def ring(shards, step):
    return [(i, (i - step) % shards) for i in range(shards)]


def fetch(weight, ctx, me, shards, direct):
    rows = weight.shape[0] // 4
    mine = lax.dynamic_slice_in_dim(weight, ctx * rows, rows, 0)
    if direct:
        own = [lax.ppermute(mine, "shard", ring(shards, r))[None] for r in range(1, shards)]
        high = [high_swap(piece) for piece in own]
        low = [low_swap(piece) for piece in own]
        both = [low_swap(piece) for piece in high]
        return own, low, high, both
    gathered = lax.all_gather(mine, "shard", axis=0, tiled=False)
    own = jnp.concatenate(
        [
            lax.dynamic_slice_in_dim(gathered, (me + r) % shards, 1, 0)
            for r in range(1, shards)
        ],
        0,
    )
    high = high_swap(own)
    return [own], [low_swap(own)], [high], [low_swap(high)]


def place(weight, pieces, ctx, me, shards, along_rows):
    height, width = weight.shape
    rows = height // 4
    count = len(pieces[0])
    each = pieces[0][0].shape[0]

    def kernel(where, local, *refs):
        parts, out = refs[:-1], refs[-1]
        step = pl.program_id(0)

        def put(slot, value):
            if along_rows:
                out[0, slot] = value
            else:
                out[pl.ds(pl.multiple_of(slot * rows, 16), rows), :] = value

        @pl.when(step == 0)
        def _():
            for slot in range(4):
                put(slot, local[slot])

        for i in range(count):

            @pl.when(step >= 1 if count == 1 else step == i + 1)
            def _():
                for k in range(4):
                    put(jnp.bitwise_xor(where[0], k), parts[k * count + i][0])

    if each == 1:
        piece_spec = pl.BlockSpec((1, rows, width), lambda r, where: (0, 0, 0))
    else:
        piece_spec = pl.BlockSpec(
            (1, rows, width), lambda r, where: (jnp.maximum(r - 1, 0), 0, 0)
        )
    if along_rows:
        out_shape = (shards, 4, rows, width)
        out_spec = pl.BlockSpec(
            (1, 4, rows, width), lambda r, where: (lax.rem(where[1] + r, shards), 0, 0, 0)
        )
    else:
        out_shape = (height, shards * width)
        out_spec = pl.BlockSpec((height, width), lambda r, where: (0, lax.rem(where[1] + r, shards)))
    out = pl.pallas_call(
        kernel,
        out_shape=jax.ShapeDtypeStruct(out_shape, weight.dtype),
        grid_spec=pltpu.PrefetchScalarGridSpec(
            num_scalar_prefetch=1,
            grid=(shards,),
            in_specs=[pl.BlockSpec((4, rows, width), lambda r, where: (0, 0, 0))]
            + [piece_spec] * (4 * count),
            out_specs=out_spec,
        ),
        compiler_params=pltpu.CompilerParams(vmem_limit_bytes=56 * 2**20),
        cost_estimate=pl.CostEstimate(
            flops=0, bytes_accessed=4 * shards * height * width, transcendentals=0
        ),
        name="place",
    )(jnp.stack([ctx, me]), weight.reshape(4, rows, width), *sum(pieces, []))
    return out.reshape(shards * height, width) if along_rows else out


def block_bias(start_row, key_first, diagonal):
    size = start_row.shape[1]
    keys = lax.broadcasted_iota(jnp.int32, (size, size), 0)
    allowed = keys + key_first >= start_row
    if diagonal:
        queries = lax.broadcasted_iota(jnp.int32, (size, size), 1)
        allowed = allowed & (keys <= queries)
    return jnp.where(allowed, 0.0, masked_value).astype(f32)


def turned(block):
    return jnp.transpose(block.astype(f32)).astype(bf16)


def attend_kernel(group, info, q_ref, k_ref, v_ref, start_ref, o_ref, lse_ref, acc, top):
    here, first = info[0], info[1]
    size = q_ref.shape[1]

    def step(block, diagonal):
        keys = turned(k_ref[block])
        values = jnp.concatenate([v_ref[block], jnp.ones((16, size), bf16)], 0)
        bias = block_bias(start_ref[...], block * size, diagonal)
        for h in range(group):
            scores = dot(keys, q_ref[h * HEAD : (h + 1) * HEAD, :], 1, 0) + bias
            block_top = jnp.max(scores, 0, keepdims=True)
            if diagonal:
                weights = jnp.exp(scores - block_top).astype(bf16)
                acc[h] = dot(values, weights, 1, 0)
                top[h] = block_top
            else:
                new_top = jnp.maximum(top[h], block_top)
                weights = jnp.exp(scores - new_top).astype(bf16)
                acc[h] = acc[h] * jnp.exp(top[h] - new_top) + dot(values, weights, 1, 0)
                top[h] = new_top

    step(here, True)

    @pl.loop(first, here)
    def _(block):
        step(block, False)

    for h in range(group):
        total = acc[h, HEAD : HEAD + 1, :]
        o_ref[h * HEAD : (h + 1) * HEAD, :] = (acc[h, :HEAD, :] / total).astype(bf16)
        lse_ref[0, h : h + 1, :] = top[h] + jnp.log(total)


def attend(info, query_t, keyval, start_row, kv_heads, seq):
    blocks, kv_rows, _ = keyval.shape
    size = start_row.shape[1]
    group = query_t.shape[0] // HEAD // kv_heads
    rows = group * HEAD
    return pl.pallas_call(
        lambda *refs: attend_kernel(group, *refs),
        out_shape=(
            jax.ShapeDtypeStruct((query_t.shape[0], size), bf16),
            jax.ShapeDtypeStruct((kv_heads, group, size), f32),
        ),
        grid_spec=pltpu.PrefetchScalarGridSpec(
            num_scalar_prefetch=1,
            grid=(kv_heads,),
            in_specs=[
                pl.BlockSpec((rows, size), lambda g, _: (g, seq)),
                pl.BlockSpec((blocks, HEAD, size), lambda g, _: (0, g, seq)),
                pl.BlockSpec((blocks, HEAD, size), lambda g, _: (0, kv_heads + g, seq)),
                pl.BlockSpec((1, size), lambda g, _: (0, 0)),
            ],
            out_specs=(
                pl.BlockSpec((rows, size), lambda g, _: (g, 0)),
                pl.BlockSpec((1, group, size), lambda g, _: (g, 0, 0)),
            ),
            scratch_shapes=[
                pltpu.VMEM((group, HEAD + 16, size), f32),
                pltpu.VMEM((group, 1, size), f32),
            ],
        ),
        compiler_params=pltpu.CompilerParams(vmem_limit_bytes=48 * 2**20),
        cost_estimate=pl.CostEstimate(
            flops=2 * 2 * query_t.shape[0] * size * size * blocks * 4,
            bytes_accessed=4 * query_t.shape[0] * size,
            transcendentals=0,
        ),
        name="attend",
    )(info, query_t, keyval, keyval, start_row)


def attend_back_kernel(
    group, info, q_ref, k_ref, v_ref, start_ref, d_ref, o_ref, lse_ref, cos_ref, sin_ref,
    dq_ref, dk_ref, dv_ref, acc, inner,
):
    here, first = info[0], info[1]
    size = q_ref.shape[1]
    rows = [slice(h * HEAD, (h + 1) * HEAD) for h in range(group)]
    for h in range(group):
        product = d_ref[rows[h], :].astype(f32) * o_ref[rows[h], :].astype(f32)
        inner[h] = jnp.sum(product, 0, keepdims=True)

    def step(block, diagonal):
        key_block = k_ref[block]
        keys = turned(key_block)
        values = turned(v_ref[block])
        bias = block_bias(start_ref[...], block * size, diagonal)
        key_sum = jnp.zeros((HEAD, size), f32)
        value_sum = jnp.zeros((HEAD, size), f32)
        for h in range(group):
            query, delta = q_ref[rows[h], :], d_ref[rows[h], :]
            scores = dot(keys, query, 1, 0) + bias
            probs = jnp.exp(scores - lse_ref[0, h : h + 1, :])
            probs_delta = dot(values, delta, 1, 0)
            score_delta = (probs * (probs_delta - inner[h])).astype(bf16)
            part = dot(key_block, score_delta, 1, 0)
            if diagonal:
                acc[rows[h], :] = part
            else:
                acc[rows[h], :] += part
            key_sum += dot(query, score_delta, 1, 1)
            value_sum += dot(delta, probs.astype(bf16), 1, 1)
        dk_ref[block] = key_sum.astype(bf16)
        dv_ref[block] = value_sum.astype(bf16)

    step(here, True)

    @pl.loop(first, here)
    def _(block):
        step(block, False)

    def clear(block):
        dk_ref[block] = jnp.zeros((HEAD, size), bf16)
        dv_ref[block] = jnp.zeros((HEAD, size), bf16)

    pl.loop(0, first)(clear)
    pl.loop(here + 1, k_ref.shape[0])(clear)

    cosine, sine = cos_ref[...], sin_ref[...]
    for h in range(group):
        upper = acc[h * HEAD : h * HEAD + HALF, :]
        lower = acc[h * HEAD + HALF : (h + 1) * HEAD, :]
        scale = HEAD ** (-0.5)
        dq_ref[h * HEAD : h * HEAD + HALF, :] = (
            (upper * cosine + lower * sine) * scale
        ).astype(bf16)
        dq_ref[h * HEAD + HALF : (h + 1) * HEAD, :] = (
            (lower * cosine - upper * sine) * scale
        ).astype(bf16)


def attend_back(
    info, query_t, keyval, start_row, delta_t, mixed_t, log_sums, cosine, sine, kv_heads, seq
):
    blocks = keyval.shape[0]
    size = start_row.shape[1]
    group = query_t.shape[0] // HEAD // kv_heads
    rows = group * HEAD
    kv_out = jax.ShapeDtypeStruct((blocks, kv_heads * HEAD, size), bf16)
    kv_spec = pl.BlockSpec((blocks, HEAD, size), lambda g, _: (0, g, 0))
    return pl.pallas_call(
        lambda *refs: attend_back_kernel(group, *refs),
        out_shape=(jax.ShapeDtypeStruct((query_t.shape[0], size), bf16), kv_out, kv_out),
        grid_spec=pltpu.PrefetchScalarGridSpec(
            num_scalar_prefetch=1,
            grid=(kv_heads,),
            in_specs=[
                pl.BlockSpec((rows, size), lambda g, _: (g, seq)),
                pl.BlockSpec((blocks, HEAD, size), lambda g, _: (0, g, seq)),
                pl.BlockSpec((blocks, HEAD, size), lambda g, _: (0, kv_heads + g, seq)),
                pl.BlockSpec((1, size), lambda g, _: (0, 0)),
                pl.BlockSpec((rows, size), lambda g, _: (g, seq)),
                pl.BlockSpec((rows, size), lambda g, _: (g, 0)),
                pl.BlockSpec((1, group, size), lambda g, _: (g, 0, 0)),
                pl.BlockSpec((HALF, size), lambda g, _: (0, seq)),
                pl.BlockSpec((HALF, size), lambda g, _: (0, seq)),
            ],
            out_specs=(pl.BlockSpec((rows, size), lambda g, _: (g, 0)), kv_spec, kv_spec),
            scratch_shapes=[
                pltpu.VMEM((rows, size), f32),
                pltpu.VMEM((group, 1, size), f32),
            ],
        ),
        compiler_params=pltpu.CompilerParams(vmem_limit_bytes=48 * 2**20),
        cost_estimate=pl.CostEstimate(
            flops=5 * 2 * query_t.shape[0] * size * size * blocks * 4,
            bytes_accessed=8 * query_t.shape[0] * size,
            transcendentals=0,
        ),
        name="attend_back",
    )(info, query_t, keyval, keyval, start_row, delta_t, mixed_t, log_sums, cosine, sine)


def rotate_t(values, cosine, sine):
    heads = values.reshape(-1, 2, HALF, values.shape[1])
    first, second = heads[:, 0], heads[:, 1]
    return jnp.stack([first * cosine - second * sine, second * cosine + first * sine], 1).reshape(
        values.shape
    )


def pick(index, when_zero, when_one):
    return jnp.where(index == 0, when_zero, when_one)


def block_products(lefts, rights, came, high, shards, left_rows, right_rows, left_cut):
    cut_side, whole_side = (lefts, rights) if left_cut else (rights, lefts)
    whole_rows = right_rows if left_cut else left_rows
    tokens, model_width = cut_side[0].shape
    part = model_width // shards // 2
    whole = whole_side[0].shape[1 - whole_rows]
    tile = whole // 2 if whole > 1408 else whole
    steps = whole // tile
    cut_spec = pl.BlockSpec((tokens, part), lambda j, s, where: (0, s * 2 + where[0]))
    if whole_rows == 0:
        whole_spec = pl.BlockSpec((tokens, tile), lambda j, s, where: (0, j))
    else:
        whole_spec = pl.BlockSpec((tile, tokens), lambda j, s, where: (j, 0))
    left_spec, right_spec = (cut_spec, whole_spec) if left_cut else (whole_spec, cut_spec)
    if left_cut:
        out_shape = (shards, part, whole)
        out_spec = pl.BlockSpec((1, part, tile), lambda j, s, where: (s, 0, j))
    else:
        out_shape = (shards, whole, part)
        out_spec = pl.BlockSpec((1, tile, part), lambda j, s, where: (s, j, 0))

    def kernel(where, *refs):
        total = dot(refs[0][...], refs[2][...], left_rows, right_rows)
        total += dot(refs[1][...], refs[3][...], left_rows, right_rows)
        if came is not None:
            total += refs[4][0].astype(f32)
        refs[-1][0] = total.astype(bf16)

    extra = [] if came is None else [came]
    return pl.pallas_call(
        kernel,
        out_shape=jax.ShapeDtypeStruct(out_shape, bf16),
        grid_spec=pltpu.PrefetchScalarGridSpec(
            num_scalar_prefetch=1,
            grid=(steps, shards),
            in_specs=[left_spec] * 2 + [right_spec] * 2 + [out_spec] * len(extra),
            out_specs=out_spec,
        ),
        compiler_params=pltpu.CompilerParams(vmem_limit_bytes=56 * 2**20),
        cost_estimate=pl.CostEstimate(
            flops=4 * tokens * shards * part * whole,
            bytes_accessed=4 * tokens * (shards * part + whole) + 2 * shards * part * whole,
            transcendentals=0,
        ),
        name="block_products",
    )(high.reshape(1), *lefts, *rights, *extra)


def column_half(values, which, shards):
    tokens, width = values.shape
    part = width // shards // 2
    return lax.dynamic_slice_in_dim(values.reshape(tokens, shards, 2, part), which, 1, 2)[:, :, 0]


def plain_products(lefts, rights, came, high, shards, left_rows, right_rows, left_cut):
    left = jnp.concatenate(lefts, left_rows)
    right = jnp.concatenate(rights, right_rows)
    if left_cut:
        total = jnp.einsum(
            "tsp,tn->spn" if right_rows == 0 else "tsp,nt->spn",
            column_half(left, high, shards), right, preferred_element_type=f32,
        )
    else:
        total = jnp.einsum(
            "tn,tsp->snp" if left_rows == 0 else "nt,tsp->snp",
            left, column_half(right, high, shards), preferred_element_type=f32,
        )
    return (total if came is None else total + came.astype(f32)).astype(bf16)


def reduced(lefts, rights, high, shards, left_rows, right_rows, left_cut):
    width = (lefts if left_cut else rights)[0].shape[1]
    products = block_products if width // shards // 2 % 128 == 0 else plain_products
    other = products(lefts, rights, None, 1 - high, shards, left_rows, right_rows, left_cut)
    came = high_swap(other)
    total = products(lefts, rights, came, high, shards, left_rows, right_rows, left_cut)
    return lax.psum_scatter(total, "shard", scatter_dimension=0, tiled=True)[0]


def halves(high, own, axis):
    came = high_swap(own)
    return jnp.concatenate([pick(high, own, came), pick(high, came, own)], axis)


def body(
    activations,
    segments,
    query_weight,
    key_weight,
    value_weight,
    output_weight,
    gate_weight,
    up_weight,
    down_weight,
    attn_gain,
    ffn_gain,
    cotangent,
):
    seq_here, block_len, model_width = activations.shape
    seq_len = segments.shape[1]
    tokens = seq_here * block_len
    query_cols = query_weight.shape[1]
    kv_width = key_weight.shape[1]
    kv_heads = kv_width // HEAD
    shards = lax.axis_size("shard")
    ctx = lax.axis_index("ctx")
    low, high = ctx % 2, ctx // 2

    me = lax.axis_index("shard")
    small = shards <= 4

    def whole(weight, along_rows, direct):
        pieces = fetch(weight, ctx, me, shards, direct and small)
        return place(weight, pieces, ctx, me, shards, along_rows)

    qkv_local = jnp.concatenate([query_weight, key_weight, value_weight], 1)
    qkv_weight = whole(qkv_local, True, False)
    gain_one = lax.all_gather(jnp.stack([attn_gain, ffn_gain]), "shard", axis=1, tiled=True)
    gain_one, gain_two = gain_one[0].astype(f32), gain_one[1].astype(f32)
    out_weight = whole(output_weight, False, False)
    down_full = whole(down_weight, False, False)
    gate_full = whole(gate_weight, True, False)
    up_full = whole(up_weight, True, True)

    index = jnp.arange(seq_len, dtype=jnp.int32)[None, :]
    doc_start = jnp.zeros_like(segments)
    for number in range(1, 4):
        before = jnp.sum((segments < number).astype(jnp.int32), 1, keepdims=True)
        doc_start = jnp.where(segments == number, before, doc_start)
    offset = ctx * block_len
    start_here = lax.dynamic_slice_in_dim(doc_start, offset, block_len, 1)
    position = lax.dynamic_slice_in_dim(index, offset, block_len, 1) - start_here
    frequency = jnp.power(rope_base, -jnp.arange(HALF, dtype=f32) / HALF)
    angles = frequency[:, None] * position.reshape(1, tokens).astype(f32)
    cosine, sine = jnp.cos(angles), jnp.sin(angles)
    first_block = start_here[:, 0] // block_len

    inputs = activations.reshape(tokens, model_width).astype(f32)
    grad_out = cotangent.reshape(tokens, model_width)
    inv_one = lax.rsqrt(jnp.mean(inputs * inputs, -1, keepdims=True) + epsilon)
    unit_one = inputs * inv_one
    normed_one = (unit_one * gain_one[None, :]).astype(bf16)

    projected = dot(qkv_weight, normed_one, 0, 1)
    query_t = (rotate_t(projected[:query_cols], cosine, sine) * HEAD ** (-0.5)).astype(bf16)
    key_t = rotate_t(projected[query_cols : query_cols + kv_width], cosine, sine).astype(bf16)
    value_t = projected[query_cols + kv_width :].astype(bf16)
    keyval = lax.all_gather(jnp.concatenate([key_t, value_t], 0), "ctx", axis=0, tiled=False)

    mixed, log_sums, residual, infos = [], [], [], []
    for s in range(seq_here):
        infos.append(jnp.stack([ctx, first_block[s]]).astype(jnp.int32))
        mixed_s, log_s = attend(infos[s], query_t, keyval, start_here[s : s + 1], kv_heads, s)
        mixed.append(mixed_s)
        log_sums.append(log_s)
        residual.append(tp_sum(dot(mixed_s, out_weight, 0, 0)))
    residual = inputs + jnp.concatenate(residual, 0)
    mixed_t = jnp.concatenate(mixed, 1)

    inv_two = lax.rsqrt(jnp.mean(residual * residual, -1, keepdims=True) + epsilon)
    unit_two = residual * inv_two
    normed_two = (unit_two * gain_two[None, :]).astype(bf16)
    gate_proj = dot(normed_two, gate_full, 1, 0)
    up_value = dot(normed_two, up_full, 1, 0)
    sigmoid_gate = jax.nn.sigmoid(gate_proj)
    silu_gate = gate_proj * sigmoid_gate
    hidden = (silu_gate * up_value).astype(bf16)

    hidden_delta = dot(grad_out, down_full, 1, 1)
    gate_delta = (
        hidden_delta * up_value * sigmoid_gate * (1.0 + gate_proj * (1.0 - sigmoid_gate))
    ).astype(bf16)
    up_delta = (hidden_delta * silu_gate).astype(bf16)
    chunk = model_width // 4
    parts = []
    for i in range(4):
        rows = slice(i * chunk, (i + 1) * chunk)
        parts.append(tp_sum(dot(gate_delta, gate_full[rows], 1, 1) + dot(up_delta, up_full[rows], 1, 1)))
    normed_two_delta = jnp.concatenate(parts, 1)
    ffn_branch = tp_sum(dot(hidden, down_full, 1, 0))
    block_out = (residual + ffn_branch).astype(bf16).reshape(activations.shape)

    ffn_gain_term = jnp.sum(normed_two_delta * unit_two, 0)
    scaled_two = normed_two_delta * gain_two[None, :]
    residual_delta = grad_out.astype(f32) + inv_two * (
        scaled_two - unit_two * jnp.mean(scaled_two * unit_two, -1, keepdims=True)
    )
    residual_round = residual_delta.astype(bf16)

    kept = pick(low, gate_delta, up_delta)
    given = pick(low, up_delta, gate_delta)
    normed_pair = (normed_two, low_swap(normed_two))
    gate_up = reduced(normed_pair, (kept, low_swap(given)), high, shards, 0, 0, True)
    gate_up = halves(high, gate_up, 0)
    gate_up_other = low_swap(gate_up)
    gate_grad = pick(low, gate_up, gate_up_other).astype(f32)
    up_grad = pick(low, gate_up_other, gate_up).astype(f32)

    part = hidden.shape[1] // 2
    hidden_kept = lax.dynamic_slice_in_dim(hidden, low * part, part, 1)
    hidden_given = lax.dynamic_slice_in_dim(hidden, (1 - low) * part, part, 1)
    hidden_pair = (hidden_kept, low_swap(hidden_given))
    cotangent_pair = (grad_out, low_swap(grad_out))
    down = reduced(hidden_pair, cotangent_pair, high, shards, 0, 0, False)
    down = halves(high, down, 1)
    down_other = low_swap(down)
    down_grad = jnp.concatenate([pick(low, down, down_other), pick(low, down_other, down)], 0)
    down_grad = down_grad.astype(f32)

    delta_t = dot(out_weight, residual_round, 1, 1).astype(bf16)

    half_rows = query_cols // 2
    mixed_kept = lax.dynamic_slice_in_dim(mixed_t, low * half_rows, half_rows, 0)
    mixed_given = lax.dynamic_slice_in_dim(mixed_t, (1 - low) * half_rows, half_rows, 0)
    mixed_pair = (mixed_kept, low_swap(mixed_given))
    residual_pair = (residual_round, low_swap(residual_round))
    output = reduced(mixed_pair, residual_pair, high, shards, 1, 0, False)
    output = halves(high, output, 1)
    output_other = low_swap(output)
    output_grad = jnp.concatenate(
        [pick(low, output, output_other), pick(low, output_other, output)], 0
    ).astype(f32)

    deltas, normed_one_delta = [], []
    for s in range(seq_here):
        query_delta, key_part, value_part = attend_back(
            infos[s], query_t, keyval, start_here[s : s + 1], delta_t, mixed[s], log_sums[s],
            cosine, sine, kv_heads, s,
        )
        part_sum = jnp.concatenate([key_part, value_part], 1).reshape(2, 2, 2 * kv_width, block_len)
        sent = lax.dynamic_index_in_dim(part_sum, 1 - high, 0, False)
        kept = lax.dynamic_index_in_dim(part_sum, high, 0, False)
        kept = kept.astype(f32) + high_swap(sent).astype(f32)
        sent = lax.dynamic_index_in_dim(kept, 1 - low, 0, False).astype(bf16)
        kept = lax.dynamic_index_in_dim(kept, low, 0, False)
        keyval_delta = kept + low_swap(sent).astype(f32)
        cols = slice(s * block_len, (s + 1) * block_len)
        key_delta = rotate_t(keyval_delta[:kv_width], cosine[:, cols], -sine[:, cols])
        delta = jnp.concatenate(
            [query_delta, key_delta.astype(bf16), keyval_delta[kv_width:].astype(bf16)], 0
        )
        deltas.append(delta)
        normed_one_delta.append(tp_sum(dot(delta, qkv_weight, 0, 1)))
    delta_all = jnp.concatenate(deltas, 1)
    normed_one_delta = jnp.concatenate(normed_one_delta, 0)

    attn_gain_term = jnp.sum(normed_one_delta * unit_one, 0)
    scaled_one = normed_one_delta * gain_one[None, :]
    input_grad = residual_delta + inv_one * (
        scaled_one - unit_one * jnp.mean(scaled_one * unit_one, -1, keepdims=True)
    )

    half_rows = delta_all.shape[0] // 2
    delta_kept = lax.dynamic_slice_in_dim(delta_all, low * half_rows, half_rows, 0)
    delta_given = lax.dynamic_slice_in_dim(delta_all, (1 - low) * half_rows, half_rows, 0)
    delta_pair = (delta_kept.T, low_swap(delta_given).T)
    normed_pair_one = (normed_one, low_swap(normed_one))
    qkv = reduced(normed_pair_one, delta_pair, high, shards, 0, 0, True)
    qkv = halves(high, qkv, 0)
    qkv_other = low_swap(qkv)
    qkv_grad = jnp.concatenate([pick(low, qkv, qkv_other), pick(low, qkv_other, qkv)], 1)
    qkv_grad = qkv_grad.astype(f32)

    gain_terms = jnp.stack([attn_gain_term, ffn_gain_term])
    gain_terms = gain_terms + low_swap(gain_terms)
    gain_terms = gain_terms + high_swap(gain_terms)
    gain_terms = gain_terms.reshape(2, shards, model_width // shards)
    gain_grads = lax.dynamic_index_in_dim(gain_terms, me, 1, False)
    for k in range(1, shards):
        block = lax.dynamic_index_in_dim(gain_terms, (me + k) % shards, 1, False)
        gain_grads = gain_grads + lax.ppermute(
            block, "shard", [(i, (i + k) % shards) for i in range(shards)]
        )

    return (
        block_out,
        input_grad.reshape(activations.shape),
        qkv_grad[:, :query_cols],
        qkv_grad[:, query_cols : query_cols + kv_width],
        qkv_grad[:, query_cols + kv_width :],
        output_grad,
        gate_grad,
        up_grad,
        down_grad,
        gain_grads[0],
        gain_grads[1],
    )


def solution(mesh):
    return jax.shard_map(
        body,
        mesh=mesh,
        in_specs=(
            P("shard", "ctx", None),
            P("shard", None),
            P("shard", "tp"),
            P("shard", "tp"),
            P("shard", "tp"),
            P("tp", "shard"),
            P("shard", "tp"),
            P("shard", "tp"),
            P("tp", "shard"),
            P("shard"),
            P("shard"),
            P("shard", "ctx", None),
        ),
        out_specs=(
            P("shard", "ctx", None),
            P("shard", "ctx", None),
            P("shard", "tp"),
            P("shard", "tp"),
            P("shard", "tp"),
            P("tp", "shard"),
            P("shard", "tp"),
            P("shard", "tp"),
            P("tp", "shard"),
            P("shard"),
            P("shard"),
        ),
        check_vma=False,
    )
```

time: 3550 us -> 1140 us (0.32)
  waiting for transfers between devices: 2840 us -> 504 us
  matrix products: 307 us -> 116 us
  Pallas kernels: 0 us -> 185 us
  starting transfers between devices: 1.37 us -> 120 us
  blocking collectives: 110 us -> 10.6 us
  other arithmetic: 186 us -> 95.3 us
    unnamed x13 -> x9, waiting for transfers between devices: 1130 us -> 0.15 us
    psum x4 -> x0, waiting for transfers between devices: 913 us -> none  [the longest x3 582 us: tp_total(): return lax.psum(partial_sum, 'tp')]
    all_gather x5, waiting for transfers between devices: 577 us -> 40.9 us  [the longest x1 24.9 us: body(): lax.all_gather(jnp.concatenate([key_t, value_t], 0), 'ctx', axis=0, tiled...]
    ppermute x0 -> x66, waiting for transfers between devices: none -> 463 us  [the longest x19 233 us: high_swap(): return lax.ppermute(value, 'ctx', SWAP_HIGH)]
    reduce_scatter x2 -> x4, waiting for transfers between devices: 213 us -> 0.01 us  [reduced(): return lax.psum_scatter(total, 'shard', scatter_dimension=0, tiled=True)[0]]
    dot_general x38 -> x20, matrix products: 307 us -> 116 us  [dot(): lax.dot_general(left, right, (((left_dim,), (right_dim,)), ((), ())), pre...]
    pallas_call x0 -> x19, Pallas kernels: none -> 185 us  [the longest x8 76.8 us: block_products(): pl.pallas_call(kernel, out_shape=jax.ShapeDtypeStruct(out_shape, bf16), g...]
    ppermute x0 -> x66, starting transfers between devices: none -> 119 us  [the longest x30 63.8 us: low_swap(): return lax.ppermute(value, 'ctx', SWAP_LOW)]
  transfers between devices with their start and end apart: 12 -> 75, of which waited for: 11 -> 27; matrix products, arithmetic and copies ran while one was open for 9% -> 23% of each run, Pallas kernels for 0% -> 17%
where the time goes in v1:
time: 1140 us; the launch traced here: 1120 us
  waiting for transfers between devices  504 us (44%)
  Pallas kernels  185 us (16%)
  starting transfers between devices  120 us (11%)
  matrix products  116 us (10%)
  other arithmetic  95.3 us (8%)
  local copies, waits for them, and re-layouts  75.2 us (7%)
  between operations  16 us (1%)
    ppermute x19, waiting for transfers between devices, high_swap(): return lax.ppermute(value, 'ctx', SWAP_HIGH)  233 us
    ppermute x11, waiting for transfers between devices, tp_sum(): return mine.astype(f32) + lax.ppermute(mine, 'tp', SWAP_TP).astype(f32)  143 us
    dot_general x20, matrix products, dot(): lax.dot_general(left, right, (((left_dim,), (right_dim,)), ((), ())), pre...  116 us
    ppermute x3, waiting for transfers between devices, fetch(): lax.ppermute(mine, 'shard', ring(shards, r))[None]  85.8 us
    pallas_call x8, Pallas kernels, block_products(): pl.pallas_call(kernel, out_shape=jax.ShapeDtypeStruct(out_shape, bf16), g...  76.8 us
    ppermute x30, starting transfers between devices, low_swap(): return lax.ppermute(value, 'ctx', SWAP_LOW)  63.8 us
    pallas_call x5, Pallas kernels, place(): pl.pallas_call(kernel, out_shape=jax.ShapeDtypeStruct(out_shape, weight.d...  42.5 us
    ppermute x19, starting transfers between devices, high_swap(): return lax.ppermute(value, 'ctx', SWAP_HIGH)  36.9 us
  transfers between devices with their start and end apart: 75, of which 27 were waited for; matrix products, arithmetic and copies ran while one was open for 23% of the time, Pallas kernels for 17%

profile of v1, /device:TPU:1, one launch (start us, length us, event | category | flops | bytes accessed | tf_op | source)
XLA Modules:
  0.0 1122.4 jit_solution(3483160385146717498)
XLA Ops:
  26.7 27.5 %collective-permute-done.12 = bf16[128,2816]{1,0:T(8,128)(2,1)} collective-permute-done((bf16[128,2816]{1,0:T(8,128)(2,1)}, bf16[128,2816]{1,0:T(8,128)(2,1)}, u32[]{:S(2)}, u32[]{:S(2)}) %collective-permute-start.12) | collective-permute-done | bytes 720928 | tf_op jit(solution)/shard_map/ppermute | solution.py:48
  55.4 58.3 %collective-permute-done.13 = bf16[128,2816]{1,0:T(8,128)(2,1)} collective-permute-done((bf16[128,2816]{1,0:T(8,128)(2,1)}, bf16[128,2816]{1,0:T(8,128)(2,1)}, u32[]{:S(2)}, u32[]{:S(2)}) %collective-permute-start.13) | collective-permute-done | bytes 720928 | tf_op jit(solution)/shard_map/ppermute | solution.py:48
  125.8 10.6 all_gather.35
  141.3 13.0 %collective-permute-start.21 = (bf16[1,128,2816]{2,1,0:T(8,128)(2,1)}, bf16[1,128,2816]{2,1,0:T(8,128)(2,1)}, u32[]{:S(2)}, u32[]{:S(2)}) collective-permute-start(bf16[1,128,2816]{2,1,0:T(8,128)(2,1)} %collective-permute-done.18.refs_6_), channel_id=1, source_target_pairs={{0,2},{2,0},{4,6},{6,4},{1,3},{3,1},{5,7},{7,5},{8,10},{10,8},{12,... | collective-permute-start | bytes 2162696 | tf_op jit(solution)/shard_map/ppermute | solution.py:22
  228.2 15.9 %all-gather.19.cloned.1.call-done = bf16[2816,512]{1,0:T(8,128)(2,1)} async-done(((bf16[704,512]{1,0:T(8,128)(2,1)}), bf16[2816,512]{1,0:T(8,128)(2,1)}) %all-gather.19.cloned.1.call-update) | async-done | bytes 2883600 | tf_op jit(solution)/shard_map/all_gather | solution.py:53
  248.6 24.9 %all-gather.13.cloned.1.call-done = bf16[1024,768]{1,0:T(8,128)(2,1)} async-done(((bf16[256,768]{1,0:T(8,128)(2,1)}), bf16[1024,768]{1,0:T(8,128)(2,1)}) %all-gather.13.cloned.1.call-update) | async-done | bytes 1572880 | tf_op jit(solution)/shard_map/all_gather | solution.py:473
  299.2 10.5 attend.5
  314.0 20.1 %collective-permute-done.7 = bf16[256,2048]{1,0:T(8,128)(2,1)S(1)} collective-permute-done((bf16[256,2048]{1,0:T(8,128)(2,1)S(1)}, bf16[256,2048]{1,0:T(8,128)(2,1)S(1)}, u32[]{:S(2)}, u32[]{:S(2)}) %collective-permute-start.7) | collective-permute-done | bytes 1048608 | tf_op jit(solution)/shard_map/ppermute | solution.py:37
  335.1 17.2 %collective-permute-done.8 = bf16[256,2048]{1,0:T(8,128)(2,1)S(1)} collective-permute-done((bf16[256,2048]{1,0:T(8,128)(2,1)S(1)}, bf16[256,2048]{1,0:T(8,128)(2,1)S(1)}, u32[]{:S(2)}, u32[]{:S(2)}) %collective-permute-start.8) | collective-permute-done | bytes 1048608 | tf_op jit(solution)/shard_map/ppermute | solution.py:37
  385.2 13.2 %fusion.56 = f32[768,2816]{1,0:T(8,128)} fusion(bf16[768,2048]{1,0:T(8,128)(2,1)} %bitcast.236, bf16[2048,2816]{1,0:T(8,128)(2,1)S(1)} %bitcast.208), kind=kOutput, calls=%fused_computation.229 | convolution fusion | flops 8858370048 | bytes 23330816 | tf_op jit(solution)/shard_map/dot_general | solution.py:30
  398.4 15.3 %multiply_convert_fusion = (bf16[768,2816]{1,0:T(8,128)(2,1)}, f32[768,2816]{1,0:T(8,128)}) fusion(f32[768,2816]{1,0:T(8,128)} %fusion.56, bf16[768,2048]{1,0:T(8,128)(2,1)} %bitcast.237, bf16[2048,2816]{1,0:T(8,128)(2,1)S(1)} %bitcast.207), kind=kOutput, calls=%fused_computation.6 | convolution fusion | flops 8871346176 | bytes 36306944 | tf_op jit(solution)/shard_map/dot_general | solution.py:30
  423.9 23.3 %broadcast_select_fusion = (bf16[768,2816]{1,0:T(8,128)(2,1)}, bf16[768,2816]{1,0:T(8,128)(2,1)}, bf16[768,2816]{1,0:T(8,128)(2,1)}) fusion(pred[]{:T(512)S(6)} %eq.51, f32[768,2816]{1,0:T(8,128)} %fusion.56, f32[768,2816]{1,0:T(8,128)} %get-tuple-element.133, bf16[2816,2048]{1,0:T(8,128)(2,1)} %place.9, bf16[768,2048]{1,0:T(8,128)(2,1)} %bitcast.218), kind=kOutput, calls=%fused_computation.41 | convolution fusion | flops 8888647680 | bytes 44957696 | tf_op jit(solution)/shard_map/dot_general | solution.py:30
  474.3 16.6 %collective-permute-done.29 = bf16[768,512]{1,0:T(8,128)(2,1)S(1)} collective-permute-done((bf16[768,512]{1,0:T(8,128)(2,1)S(1)}, bf16[768,512]{1,0:T(8,128)(2,1)S(1)}, u32[]{:S(2)}, u32[]{:S(2)}) %collective-permute-start.29) | collective-permute-done | bytes 786464 | tf_op jit(solution)/shard_map/ppermute | solution.py:37
  491.2 16.6 %collective-permute-done.30 = bf16[768,512]{1,0:T(8,128)(2,1)S(1)} collective-permute-done((bf16[768,512]{1,0:T(8,128)(2,1)S(1)}, bf16[768,512]{1,0:T(8,128)(2,1)S(1)}, u32[]{:S(2)}, u32[]{:S(2)}) %collective-permute-start.30) | collective-permute-done | bytes 786464 | tf_op jit(solution)/shard_map/ppermute | solution.py:37
  508.0 16.6 %collective-permute-done.31 = bf16[768,512]{1,0:T(8,128)(2,1)S(1)} collective-permute-done((bf16[768,512]{1,0:T(8,128)(2,1)S(1)}, bf16[768,512]{1,0:T(8,128)(2,1)S(1)}, u32[]{:S(2)}, u32[]{:S(2)}) %collective-permute-start.31) | collective-permute-done | bytes 786464 | tf_op jit(solution)/shard_map/ppermute | solution.py:37
  528.1 13.6 %multiply_convert_fusion.1 = (bf16[768,2048]{1,0:T(8,128)(2,1)}, bf16[768,2048]{1,0:T(8,128)(2,1)}, bf16[768,2048]{1,0:T(8,128)(2,1)}) fusion(f32[2048]{0:T(1024)S(1)} %bitcast.271, f32[768]{0:T(1024)S(1)} %rsqrt.26, bf16[3,256,2048]{2,1,0:T(8,128)(2,1)} %param.12, f32[256,2048]{1,0:T(8,128)} %copy-done.44, f32[256,2048]{1,0:T(8,128)} %copy-done.42, ...), kind=kLoop, calls=%fused_computation.36 | loop fusion | flops 31457280 | bytes 28337152 | tf_op jit(solution)/shard_map/convert_element_type | solution.py:487
  549.8 11.8 %attend_back.3 = (bf16[1024,256]{1,0:T(8,128)(2,1)S(1)}, bf16[4,128,256]{2,1,0:T(8,128)(2,1)S(1)}, bf16[4,128,256]{2,1,0:T(8,128)(2,1)S(1)}) custom-call(s32[2]{0:T(128)S(1)} %copy-done.25, bf16[1024,768]{1,0:T(8,128)(2,1)S(1)} %bitcast.182, bf16[4,256,768]{2,1,0:T(8,128)(2,1)S(1)} %bitcast.191, bf16[4,256,768]{2,1,0:T(8,128)(2,1)S(1)} %bitcast.192, ...), custom_call_target="tpu_custom_call" | custom-call | flops 10737418240 | bytes 2097152 | tf_op jit(solution)/shard_map/attend_back/pallas_call | solution.py:281
  564.6 19.2 %collective-permute-start.32 = (bf16[2,256,256]{1,2,0:T(8,128)(2,1)}, bf16[2,256,256]{1,2,0:T(8,128)(2,1)}, u32[]{:S(2)}, u32[]{:S(2)}) collective-permute-start(bf16[2,256,256]{1,2,0:T(8,128)(2,1)} %dynamic-slice_bitcast_fusion.3), channel_id=1, source_target_pairs={{0,4},{4,0},{2,6},{6,2},{1,5},{5,1},{3,7},{7,3},{8,12},{12,8},{10,... | collective-permute-start | bytes 786440 | tf_op jit(solution)/shard_map/ppermute | solution.py:26
  585.2 12.0 %attend_back.4 = (bf16[1024,256]{1,0:T(8,128)(2,1)S(1)}, bf16[4,128,256]{2,1,0:T(8,128)(2,1)S(1)}, bf16[4,128,256]{2,1,0:T(8,128)(2,1)S(1)}) custom-call(s32[2]{0:T(128)S(1)} %copy-done.23, bf16[1024,768]{1,0:T(8,128)(2,1)S(1)} %bitcast.183, bf16[4,256,768]{2,1,0:T(8,128)(2,1)S(1)} %bitcast.193, bf16[4,256,768]{2,1,0:T(8,128)(2,1)S(1)} %bitcast.194, ...), custom_call_target="tpu_custom_call" | custom-call | flops 10737418240 | bytes 2097152 | tf_op jit(solution)/shard_map/attend_back/pallas_call | solution.py:281
  600.4 11.8 %attend_back.5 = (bf16[1024,256]{1,0:T(8,128)(2,1)S(1)}, bf16[4,128,256]{2,1,0:T(8,128)(2,1)S(1)}, bf16[4,128,256]{2,1,0:T(8,128)(2,1)S(1)}) custom-call(s32[2]{0:T(128)S(1)} %copy-done.32, bf16[1024,768]{1,0:T(8,128)(2,1)S(1)} %bitcast.184, bf16[4,256,768]{2,1,0:T(8,128)(2,1)S(1)} %bitcast.195, bf16[4,256,768]{2,1,0:T(8,128)(2,1)S(1)} %bitcast.196, ...), custom_call_target="tpu_custom_call" | custom-call | flops 10737418240 | bytes 2097152 | tf_op jit(solution)/shard_map/attend_back/pallas_call | solution.py:281
  651.4 18.5 %collective-permute-done.48.refs_4_ = bf16[4,512,256]{2,1,0:T(8,128)(2,1)S(1)} collective-permute-done((bf16[4,512,256]{2,1,0:T(8,128)(2,1)}, bf16[4,512,256]{2,1,0:T(8,128)(2,1)S(1)}, u32[]{:S(2)}, u32[]{:S(2)}) %collective-permute-start.48) | collective-permute-done | bytes 1048608 | tf_op jit(solution)/shard_map/ppermute | solution.py:26
  693.4 19.3 %collective-permute-done.43.refs_4_ = bf16[4,256,640]{2,1,0:T(8,128)(2,1)S(1)} collective-permute-done((bf16[4,256,640]{2,1,0:T(8,128)(2,1)}, bf16[4,256,640]{2,1,0:T(8,128)(2,1)S(1)}, u32[]{:S(2)}, u32[]{:S(2)}) %collective-permute-start.43) | collective-permute-done | bytes 1310752 | tf_op jit(solution)/shard_map/ppermute | solution.py:26
  725.2 16.7 %block_products.12 = bf16[4,256,2816]{2,1,0:T(8,128)(2,1)} custom-call(s32[1]{0:T(128)} %bitcast.69.where, bf16[768,2048]{1,0:T(8,128)(2,1)} %get-tuple-element.61.refs_0_, bf16[768,2048]{1,0:T(8,128)(2,1)} %collective-permute-done.51.refs_1_, bf16[768,2816]{1,0:T(8,128)(2,1)} %broadcast_select_fusion.1.refs_2_, ...), custom_call_target="tpu_custom_call" | custom-call | flops 8858370048 | bytes 17563648 | tf_op jit(solution)/shard_map/block_products/pallas_call | solution.py:355
  743.3 31.2 %collective-permute-done.58.refs_4_ = bf16[4,1408,256]{2,1,0:T(8,128)(2,1)S(1)} collective-permute-done((bf16[4,1408,256]{2,1,0:T(8,128)(2,1)}, bf16[4,1408,256]{2,1,0:T(8,128)(2,1)S(1)}, u32[]{:S(2)}, u32[]{:S(2)}) %collective-permute-start.58) | collective-permute-done | bytes 2883616 | tf_op jit(solution)/shard_map/ppermute | solution.py:26
  785.6 112.6 %collective-permute-done.53.refs_4_ = bf16[4,256,2816]{2,1,0:T(8,128)(2,1)} collective-permute-done((bf16[4,256,2816]{2,1,0:T(8,128)(2,1)}, bf16[4,256,2816]{2,1,0:T(8,128)(2,1)}, u32[]{:S(2)}, u32[]{:S(2)}) %collective-permute-start.53) | collective-permute-done | bytes 5767200 | tf_op jit(solution)/shard_map/ppermute | solution.py:26
  898.2 17.5 %block_products.13 = bf16[4,256,2816]{2,1,0:T(8,128)(2,1)} custom-call(s32[1]{0:T(128)} %bitcast.66.where, bf16[768,2048]{1,0:T(8,128)(2,1)} %get-tuple-element.61.refs_0_, bf16[768,2048]{1,0:T(8,128)(2,1)} %collective-permute-done.51.refs_1_, bf16[768,2816]{1,0:T(8,128)(2,1)} %broadcast_select_fusion.1.refs_2_, ...), custom_call_target="tpu_custom_call" | custom-call | flops 8858370048 | bytes 17563648 | tf_op jit(solution)/shard_map/block_products/pallas_call | solution.py:355
  930.6 13.5 %collective-permute-done.34 = bf16[256,2048]{1,0:T(8,128)(2,1)} collective-permute-done((bf16[256,2048]{1,0:T(8,128)(2,1)S(1)}, bf16[256,2048]{1,0:T(8,128)(2,1)}, u32[]{:S(2)}, u32[]{:S(2)}) %collective-permute-start.34) | collective-permute-done | bytes 1048608 | tf_op jit(solution)/shard_map/ppermute | solution.py:37
  945.6 20.9 %collective-permute-done.37 = bf16[256,2048]{1,0:T(8,128)(2,1)S(1)} collective-permute-done((bf16[256,2048]{1,0:T(8,128)(2,1)}, bf16[256,2048]{1,0:T(8,128)(2,1)S(1)}, u32[]{:S(2)}, u32[]{:S(2)}) %collective-permute-start.37) | collective-permute-done | bytes 1048608 | tf_op jit(solution)/shard_map/ppermute | solution.py:37
  968.1 20.9 %collective-permute-done.40 = bf16[256,2048]{1,0:T(8,128)(2,1)S(1)} collective-permute-done((bf16[256,2048]{1,0:T(8,128)(2,1)S(1)}, bf16[256,2048]{1,0:T(8,128)(2,1)S(1)}, u32[]{:S(2)}, u32[]{:S(2)}) %collective-permute-start.40) | collective-permute-done | bytes 1048608 | tf_op jit(solution)/shard_map/ppermute | solution.py:37
  996.2 14.3 %convolution_convert_fusion = bf16[768,2048]{1,0:T(8,128)(2,1)} fusion(bf16[768,2816]{1,0:T(8,128)(2,1)} %get-tuple-element.132, bf16[2816,2048]{1,0:T(8,128)(2,1)} %place.9), kind=kOutput, calls=%fused_computation.43 | convolution fusion | flops 8859942912 | bytes 19005440 | tf_op jit(solution)/shard_map/dot_general | solution.py:30
  1018.6 12.6 %fusion.17 = f32[3,256,2048]{2,1,0:T(8,128)} fusion(bf16[3,256,2048]{2,1,0:T(8,128)(2,1)S(1)} %copy-done.36, bf16[3,256,2048]{2,1,0:T(8,128)(2,1)} %param.23, f32[3,256,2048]{2,1,0:T(8,128)} %bitcast.204, f32[3,256]{1,0:T(4,128)S(1)} %broadcast_multiply_fusion, f32[3,256]{1,0:T(4,128)S(1)} %copy-done.92, f32[2048]{0:T(1024)S(1)} %bitcast.272, ...), kind=kLoop, calls=%fused_computation.30 | loop fusion | flops 28311552 | bytes 31485952 | tf_op jit(solution)/shard_map/add | solution.py:574
  1066.2 24.7 %collective-permute-done.54 = bf16[256,2816]{1,0:T(8,128)(2,1)S(1)} collective-permute-done((bf16[256,2816]{1,0:T(8,128)(2,1)}, bf16[256,2816]{1,0:T(8,128)(2,1)S(1)}, u32[]{:S(2)}, u32[]{:S(2)}) %collective-permute-start.54) | collective-permute-done | bytes 1441824 | tf_op jit(solution)/shard_map/ppermute | solution.py:26
  (532 shorter events, 415.5 us)
Async XLA Ops:
  7.2 108.0 %all-gather.11.cloned.1.call-start = ((), (), s32[]{:S(2)}) async-start(), calls=%async_computation.8 | async-start | bytes 1638400 | tf_op jit(solution)/shard_map/all_gather | solution.py:53
  11.2 157.7 %all-gather.15.cloned.1.call-start = ((), (), s32[]{:S(2)}) async-start(), calls=%async_computation.10 | async-start | bytes 1310720 | tf_op jit(solution)/shard_map/all_gather | solution.py:53
  13.3 210.4 %all-gather.17.cloned.1.call-start = ((), (), s32[]{:S(2)}) async-start(), calls=%async_computation.11 | async-start | bytes 3604480 | tf_op jit(solution)/shard_map/all_gather | solution.py:53
  15.6 228.6 %all-gather.19.cloned.1.call-start = ((), (), s32[]{:S(2)}) async-start(), calls=%async_computation.12 | async-start | bytes 3604480 | tf_op jit(solution)/shard_map/all_gather | solution.py:53
  21.8 91.9 %collective-permute-start.13 = (bf16[128,2816]{1,0:T(8,128)(2,1)}, bf16[128,2816]{1,0:T(8,128)(2,1)}, u32[]{:S(2)}, u32[]{:S(2)}) collective-permute-start(bf16[128,2816]{1,0:T(8,128)(2,1)} %constant_dynamic-slice_fusion.13), channel_id=1, source_target_pairs={{0,16},{8,24},{16,0},{24,8},{1,17},{9,25},{17,1},{25,9},{2,18},{10... | collective-permute-start | bytes 2162696 | tf_op jit(solution)/shard_map/ppermute | solution.py:48
  21.8 93.0 %collective-permute-start.14 = (bf16[128,2816]{1,0:T(8,128)(2,1)}, bf16[128,2816]{1,0:T(8,128)(2,1)}, u32[]{:S(2)}, u32[]{:S(2)}) collective-permute-start(bf16[128,2816]{1,0:T(8,128)(2,1)} %constant_dynamic-slice_fusion.13), channel_id=1, source_target_pairs={{0,8},{8,16},{16,24},{24,0},{1,9},{9,17},{17,25},{25,1},{2,10},{10... | collective-permute-start | bytes 2162696 | tf_op jit(solution)/shard_map/ppermute | solution.py:48
  24.3 249.2 %all-gather.13.cloned.1.call-start = ((), (), s32[]{:S(2)}) async-start(), calls=%async_computation.9 | async-start | bytes 1966080 | tf_op jit(solution)/shard_map/all_gather | solution.py:473
  54.3 71.0 %collective-permute-start.18 = (bf16[1,128,2816]{2,1,0:T(8,128)(2,1)}, bf16[1,128,2816]{2,1,0:T(8,128)(2,1)}, u32[]{:S(2)}, u32[]{:S(2)}) collective-permute-start(bf16[1,128,2816]{2,1,0:T(8,128)(2,1)} %bitcast.23.refs_0_), channel_id=1, source_target_pairs={{0,4},{4,0},{2,6},{6,2},{1,5},{5,1},{3,7},{7,3},{8,12},{12,8},{10,... | collective-permute-start | bytes 2162696 | tf_op jit(solution)/shard_map/ppermute | solution.py:26
  116.6 45.8 %collective-permute-start.1 = (bf16[3,128,1280]{2,1,0:T(8,128)(2,1)S(1)}, bf16[3,128,1280]{2,1,0:T(8,128)(2,1)S(1)}, u32[]{:S(2)}, u32[]{:S(2)}) collective-permute-start(bf16[3,128,1280]{2,1,0:T(8,128)(2,1)S(1)} %pad_maximum_fusion.7.refs_0_), channel_id=1, source_target_pairs={{0,4},{4,0},{2,6},{6,2},{1,5},{5,1},{3,7},{7,3},{8,12},{12,8},{10,... | collective-permute-start | bytes 2949128 | tf_op jit(solution)/shard_map/ppermute | solution.py:26
  206.1 825.0 %reduce-scatter.7.cloned.1.call-start = ((), (), s32[]{:S(2)}) async-start(), calls=%async_computation.5 | async-start | bytes 1310720 | tf_op jit(solution)/shard_map/reduce_scatter | solution.py:402
  226.9 107.5 %collective-permute-start.10 = (bf16[3,128,2816]{2,1,0:T(8,128)(2,1)}, bf16[3,128,2816]{2,1,0:T(8,128)(2,1)}, u32[]{:S(2)}, u32[]{:S(2)}) collective-permute-start(bf16[3,128,2816]{2,1,0:T(8,128)(2,1)} %pad_maximum_fusion.4.refs_0_), channel_id=1, source_target_pairs={{0,4},{4,0},{2,6},{6,2},{1,5},{5,1},{3,7},{7,3},{8,12},{12,8},{10,... | collective-permute-start | bytes 6488072 | tf_op jit(solution)/shard_map/ppermute | solution.py:26
  228.0 135.2 %collective-permute-start.9 = (bf16[3,128,2816]{2,1,0:T(8,128)(2,1)}, bf16[3,128,2816]{2,1,0:T(8,128)(2,1)}, u32[]{:S(2)}, u32[]{:S(2)}) collective-permute-start(bf16[3,128,2816]{2,1,0:T(8,128)(2,1)} %pad_maximum_fusion.4.refs_0_), channel_id=1, source_target_pairs={{0,2},{2,0},{4,6},{6,4},{1,3},{3,1},{5,7},{7,5},{8,10},{10,8},{12,... | collective-permute-start | bytes 6488072 | tf_op jit(solution)/shard_map/ppermute | solution.py:22
  247.4 87.6 %collective-permute-start.25 = (bf16[3,704,512]{2,1,0:T(8,128)(2,1)}, bf16[3,704,512]{2,1,0:T(8,128)(2,1)}, u32[]{:S(2)}, u32[]{:S(2)}) collective-permute-start(bf16[3,704,512]{2,1,0:T(8,128)(2,1)} %pad_maximum_fusion.5.refs_0_), channel_id=1, source_target_pairs={{0,4},{4,0},{2,6},{6,2},{1,5},{5,1},{3,7},{7,3},{8,12},{12,8},{10,... | collective-permute-start | bytes 6488072 | tf_op jit(solution)/shard_map/ppermute | solution.py:26
  334.0 79.6 %collective-permute-start.24 = (bf16[3,704,512]{2,1,0:T(8,128)(2,1)}, bf16[3,704,512]{2,1,0:T(8,128)(2,1)}, u32[]{:S(2)}, u32[]{:S(2)}) collective-permute-start(bf16[3,704,512]{2,1,0:T(8,128)(2,1)} %pad_maximum_fusion.5.refs_0_), channel_id=1, source_target_pairs={{0,2},{2,0},{4,6},{6,4},{1,3},{3,1},{5,7},{7,5},{8,10},{10,8},{12,... | collective-permute-start | bytes 6488072 | tf_op jit(solution)/shard_map/ppermute | solution.py:22
  334.4 304.5 %collective-permute-start.46 = (bf16[512,768]{1,0:T(8,128)(2,1)}, bf16[512,768]{1,0:T(8,128)(2,1)}, u32[]{:S(2)}, u32[]{:S(2)}) collective-permute-start(bf16[512,768]{1,0:T(8,128)(2,1)} %get-tuple-element.82), channel_id=1, source_target_pairs={{0,2},{2,0},{4,6},{6,4},{1,3},{3,1},{5,7},{7,5},{8,10},{10,8},{12,... | collective-permute-start | bytes 2359304 | tf_op jit(solution)/shard_map/ppermute | solution.py:22
  352.3 61.4 %collective-permute-start.26 = (bf16[3,704,512]{2,1,0:T(8,128)(2,1)}, bf16[3,704,512]{2,1,0:T(8,128)(2,1)}, u32[]{:S(2)}, u32[]{:S(2)}) collective-permute-start(bf16[3,704,512]{2,1,0:T(8,128)(2,1)} %collective-permute-done.25.refs_2_), channel_id=1, source_target_pairs={{0,2},{2,0},{4,6},{6,4},{1,3},{3,1},{5,7},{7,5},{8,10},{10,8},{12,... | collective-permute-start | bytes 6488072 | tf_op jit(solution)/shard_map/ppermute | solution.py:22
  473.0 51.7 %collective-permute-start.31 = (bf16[768,512]{1,0:T(8,128)(2,1)S(1)}, bf16[768,512]{1,0:T(8,128)(2,1)S(1)}, u32[]{:S(2)}, u32[]{:S(2)}) collective-permute-start(bf16[768,512]{1,0:T(8,128)(2,1)S(1)} %add_convert_fusion.1), channel_id=1, source_target_pairs={{0,1},{1,0},{2,3},{3,2},{4,5},{5,4},{6,7},{7,6},{8,9},{9,8},{10,11... | collective-permute-start | bytes 2359304 | tf_op jit(solution)/shard_map/ppermute | solution.py:37
  548.4 90.8 %collective-permute-start.47 = (bf16[768,2048]{1,0:T(8,128)(2,1)}, bf16[768,2048]{1,0:T(8,128)(2,1)}, u32[]{:S(2)}, u32[]{:S(2)}) collective-permute-start(bf16[768,2048]{1,0:T(8,128)(2,1)} %get-tuple-element.62.refs_2_), channel_id=1, source_target_pairs={{0,2},{2,0},{4,6},{6,4},{1,3},{3,1},{5,7},{7,5},{8,10},{10,8},{12,... | collective-permute-start | bytes 9437192 | tf_op jit(solution)/shard_map/ppermute | solution.py:22
  564.6 55.8 %collective-permute-start.32 = (bf16[2,256,256]{1,2,0:T(8,128)(2,1)}, bf16[2,256,256]{1,2,0:T(8,128)(2,1)}, u32[]{:S(2)}, u32[]{:S(2)}) collective-permute-start(bf16[2,256,256]{1,2,0:T(8,128)(2,1)} %dynamic-slice_bitcast_fusion.3), channel_id=1, source_target_pairs={{0,4},{4,0},{2,6},{6,2},{1,5},{5,1},{3,7},{7,3},{8,12},{12,8},{10,... | collective-permute-start | bytes 786440 | tf_op jit(solution)/shard_map/ppermute | solution.py:26
  620.3 56.4 %collective-permute-start.41 = (bf16[768,2048]{1,0:T(8,128)(2,1)}, bf16[768,2048]{1,0:T(8,128)(2,1)}, u32[]{:S(2)}, u32[]{:S(2)}) collective-permute-start(bf16[768,2048]{1,0:T(8,128)(2,1)} %get-tuple-element.69.refs_0_), channel_id=1, source_target_pairs={{0,2},{2,0},{4,6},{6,4},{1,3},{3,1},{5,7},{7,5},{8,10},{10,8},{12,... | collective-permute-start | bytes 9437192 | tf_op jit(solution)/shard_map/ppermute | solution.py:22
  638.9 86.2 %collective-permute-start.52 = (bf16[768,2816]{1,0:T(8,128)(2,1)}, bf16[768,2816]{1,0:T(8,128)(2,1)}, u32[]{:S(2)}, u32[]{:S(2)}) collective-permute-start(bf16[768,2816]{1,0:T(8,128)(2,1)} %get-tuple-element.48), channel_id=1, source_target_pairs={{0,2},{2,0},{4,6},{6,4},{1,3},{3,1},{5,7},{7,5},{8,10},{10,8},{12,... | collective-permute-start | bytes 12976136 | tf_op jit(solution)/shard_map/ppermute | solution.py:22
  670.0 55.2 %collective-permute-start.51 = (bf16[768,2048]{1,0:T(8,128)(2,1)}, bf16[768,2048]{1,0:T(8,128)(2,1)}, u32[]{:S(2)}, u32[]{:S(2)}) collective-permute-start(bf16[768,2048]{1,0:T(8,128)(2,1)} %get-tuple-element.61.refs_0_), channel_id=1, source_target_pairs={{0,2},{2,0},{4,6},{6,4},{1,3},{3,1},{5,7},{7,5},{8,10},{10,8},{12,... | collective-permute-start | bytes 9437192 | tf_op jit(solution)/shard_map/ppermute | solution.py:22
  676.6 356.5 %reduce-scatter.5.cloned.1.call-start = ((), (), s32[]{:S(2)}) async-start(), calls=%async_computation.4 | async-start | bytes 1638400 | tf_op jit(solution)/shard_map/reduce_scatter | solution.py:402
  693.4 81.2 %collective-permute-start.58 = (bf16[4,1408,256]{2,1,0:T(8,128)(2,1)}, bf16[4,1408,256]{2,1,0:T(8,128)(2,1)S(1)}, u32[]{:S(2)}, u32[]{:S(2)}) collective-permute-start(bf16[4,1408,256]{2,1,0:T(8,128)(2,1)} %block_products.14), channel_id=1, source_target_pairs={{0,4},{4,0},{2,6},{6,2},{1,5},{5,1},{3,7},{7,3},{8,12},{12,8},{10,... | collective-permute-start | bytes 8650760 | tf_op jit(solution)/shard_map/ppermute | solution.py:26
  720.4 312.8 %reduce-scatter.11.cloned.1.call-start = ((), (), s32[]{:S(2)}) async-start(), calls=%async_computation.7 | async-start | bytes 3604480 | tf_op jit(solution)/shard_map/reduce_scatter | solution.py:402
  741.8 156.4 %collective-permute-start.53 = (bf16[4,256,2816]{2,1,0:T(8,128)(2,1)}, bf16[4,256,2816]{2,1,0:T(8,128)(2,1)}, u32[]{:S(2)}, u32[]{:S(2)}) collective-permute-start(bf16[4,256,2816]{2,1,0:T(8,128)(2,1)} %block_products.12), channel_id=1, source_target_pairs={{0,4},{4,0},{2,6},{6,2},{1,5},{5,1},{3,7},{7,3},{8,12},{12,8},{10,... | collective-permute-start | bytes 17301512 | tf_op jit(solution)/shard_map/ppermute | solution.py:26
  785.5 249.1 %reduce-scatter.9.cloned.1.call-start = ((), (), s32[]{:S(2)}) async-start(), calls=%async_computation.6 | async-start | bytes 7208960 | tf_op jit(solution)/shard_map/reduce_scatter | solution.py:402
  929.1 59.9 %collective-permute-start.40 = (bf16[256,2048]{1,0:T(8,128)(2,1)S(1)}, bf16[256,2048]{1,0:T(8,128)(2,1)S(1)}, u32[]{:S(2)}, u32[]{:S(2)}) collective-permute-start(bf16[256,2048]{1,0:T(8,128)(2,1)S(1)} %convolution_convert_fusion.4), channel_id=1, source_target_pairs={{0,1},{1,0},{2,3},{3,2},{4,5},{5,4},{6,7},{7,6},{8,9},{9,8},{10,11... | collective-permute-start | bytes 3145736 | tf_op jit(solution)/shard_map/ppermute | solution.py:37
  1010.5 83.4 %collective-permute-start.27 = (bf16[768,2048]{1,0:T(8,128)(2,1)}, bf16[768,2048]{1,0:T(8,128)(2,1)}, u32[]{:S(2)}, u32[]{:S(2)}) collective-permute-start(bf16[768,2048]{1,0:T(8,128)(2,1)} %convolution_convert_fusion), channel_id=1, source_target_pairs={{0,1},{1,0},{2,3},{3,2},{4,5},{5,4},{6,7},{7,6},{8,9},{9,8},{10,11... | collective-permute-start | bytes 9437192 | tf_op jit(solution)/shard_map/ppermute | solution.py:37
  1034.6 56.3 %collective-permute-start.54 = (bf16[256,2816]{1,0:T(8,128)(2,1)}, bf16[256,2816]{1,0:T(8,128)(2,1)S(1)}, u32[]{:S(2)}, u32[]{:S(2)}) collective-permute-start(bf16[256,2816]{1,0:T(8,128)(2,1)} %bitcast.256), channel_id=1, source_target_pairs={{0,4},{4,0},{2,6},{6,2},{1,5},{5,1},{3,7},{7,3},{8,12},{12,8},{10,... | collective-permute-start | bytes 4325384 | tf_op jit(solution)/shard_map/ppermute | solution.py:26
  1039.5 60.1 %collective-permute-start.50 = (bf16[512,512]{1,0:T(8,128)(2,1)}, bf16[512,512]{1,0:T(8,128)(2,1)}, u32[]{:S(2)}, u32[]{:S(2)}) collective-permute-start(bf16[512,512]{1,0:T(8,128)(2,1)} %pad_maximum_fusion.13), channel_id=1, source_target_pairs={{0,2},{2,0},{4,6},{6,4},{1,3},{3,1},{5,7},{7,5},{8,10},{10,8},{12,... | collective-permute-start | bytes 1572872 | tf_op jit(solution)/shard_map/ppermute | solution.py:22
  1045.8 56.8 %collective-permute-start.45 = (bf16[512,640]{1,0:T(8,128)(2,1)S(1)}, bf16[512,640]{1,0:T(8,128)(2,1)}, u32[]{:S(2)}, u32[]{:S(2)}) collective-permute-start(bf16[512,640]{1,0:T(8,128)(2,1)S(1)} %pad_maximum_fusion.9), channel_id=1, source_target_pairs={{0,2},{2,0},{4,6},{6,4},{1,3},{3,1},{5,7},{7,5},{8,10},{10,8},{12,... | collective-permute-start | bytes 1966088 | tf_op jit(solution)/shard_map/ppermute | solution.py:22
  (151 other events, 3987.7 us)
Sparse Core Ops, SparseCore 0:
  11.4 75.3 all-gather.10
  88.9 33.4 all-gather.14
  124.6 60.1 all-gather.16
  186.3 57.8 all-gather.18
  246.1 27.3 all-gather.12
  676.8 25.7 reduce-scatter.6
  720.5 32.1 reduce-scatter.4
  785.7 57.1 reduce-scatter.10
  915.9 102.0 reduce-scatter.8

commit v2 on v1

--- a/solution.py
+++ b/solution.py
@@ -37,39 +37,62 @@
     return mine.astype(f32) + lax.ppermute(mine, "tp", SWAP_TP).astype(f32)
 
 
+UNREAD = pl.BlockSpec(memory_space=pl.ANY)
+
+
+def taking(microseconds):
+    return pl.CostEstimate(flops=int(microseconds * 0.05e9), bytes_accessed=int(microseconds * 0.15e6), transcendentals=0)
+
+
+def tie(value, *after):
+    def kernel(*refs):
+        pass
+
+    return pl.pallas_call(
+        kernel,
+        out_shape=jax.ShapeDtypeStruct(value.shape, value.dtype),
+        in_specs=[UNREAD] * (1 + len(after)),
+        out_specs=UNREAD,
+        input_output_aliases={0: 0},
+        name="tie",
+    )(value, *after)
+
+
 def ring(shards, step):
     return [(i, (i - step) % shards) for i in range(shards)]
 
 
-def fetch(weight, ctx, me, shards, direct):
+def quarter(weight, ctx):
     rows = weight.shape[0] // 4
-    mine = lax.dynamic_slice_in_dim(weight, ctx * rows, rows, 0)
-    if direct:
-        own = [lax.ppermute(mine, "shard", ring(shards, r))[None] for r in range(1, shards)]
-        high = [high_swap(piece) for piece in own]
-        low = [low_swap(piece) for piece in own]
-        both = [low_swap(piece) for piece in high]
-        return own, low, high, both
-    gathered = lax.all_gather(mine, "shard", axis=0, tiled=False)
-    own = jnp.concatenate(
-        [
-            lax.dynamic_slice_in_dim(gathered, (me + r) % shards, 1, 0)
-            for r in range(1, shards)
-        ],
-        0,
-    )
-    high = high_swap(own)
-    return [own], [low_swap(own)], [high], [low_swap(high)]
-
-
-def place(weight, pieces, ctx, me, shards, along_rows):
+    return lax.dynamic_slice_in_dim(weight, ctx * rows, rows, 0)
+
+
+def gathered(weight, ctx):
+    return lax.all_gather(quarter(weight, ctx), "shard", axis=0, tiled=False)
+
+
+def spread(own, *after):
+    high = [high_swap(piece) for piece in own]
+    low = [low_swap(piece) for piece in own]
+    if after:
+        high = [tie(piece, *after) for piece in high]
+    return own, low, high, [low_swap(piece) for piece in high]
+
+
+def others(everyone, me):
+    shards = everyone.shape[0]
+    steps = [lax.dynamic_slice_in_dim(everyone, (me + r) % shards, 1, 0) for r in range(1, shards)]
+    return jnp.concatenate(steps, 0)
+
+
+def place(weight, pieces, ctx, me, shards, along_rows, after=()):
     height, width = weight.shape
     rows = height // 4
     count = len(pieces[0])
     each = pieces[0][0].shape[0]
 
     def kernel(where, local, *refs):
-        parts, out = refs[:-1], refs[-1]
+        parts, out = refs[: 4 * count], refs[-1]
         step = pl.program_id(0)
 
         def put(slot, value):
@@ -111,16 +134,336 @@
             num_scalar_prefetch=1,
             grid=(shards,),
             in_specs=[pl.BlockSpec((4, rows, width), lambda r, where: (0, 0, 0))]
-            + [piece_spec] * (4 * count),
+            + [piece_spec] * (4 * count)
+            + [UNREAD] * len(after),
             out_specs=out_spec,
         ),
         compiler_params=pltpu.CompilerParams(vmem_limit_bytes=56 * 2**20),
-        cost_estimate=pl.CostEstimate(
-            flops=0, bytes_accessed=4 * shards * height * width, transcendentals=0
-        ),
+        cost_estimate=taking(8),
         name="place",
-    )(jnp.stack([ctx, me]), weight.reshape(4, rows, width), *sum(pieces, []))
+    )(jnp.stack([ctx, me]), weight.reshape(4, rows, width), *sum(pieces, []), *after)
     return out.reshape(shards * height, width) if along_rows else out
+
+
+TILE = 256
+ROOMY = pltpu.CompilerParams(vmem_limit_bytes=56 * 2**20)
+
+
+def feed_forward(normed, weights, pieces, ctx, me, shards, after=()):
+    tokens, model_width = normed.shape
+    height, width = weights[0].shape
+    rows = height // 4
+
+    def kernel(where, normed_ref, *refs):
+        hidden_ref, gate_ref, up_ref, full_ref = refs[-4:]
+        for w in range(2):
+            local, parts = refs[5 * w], refs[5 * w + 1 : 5 * w + 5]
+            for slot in range(4):
+                start = pl.multiple_of(where[1] * height + slot * rows, rows)
+                full_ref[w, pl.ds(start, rows), :] = local[slot]
+            for r in range(1, shards):
+                first = lax.rem(where[1] + r, shards) * height
+                for k in range(4):
+                    start = first + jnp.bitwise_xor(where[0], k) * rows
+                    full_ref[w, pl.ds(pl.multiple_of(start, rows), rows), :] = parts[k][r - 1]
+        gate = dot(normed_ref[...], full_ref[0], 1, 0)
+        up = dot(normed_ref[...], full_ref[1], 1, 0)
+        sigmoid = 1.0 / (1.0 + jnp.exp(-gate))
+        silu = gate * sigmoid
+        hidden_ref[...] = (silu * up).astype(bf16)
+        gate_ref[...] = (up * sigmoid * (1.0 + gate * (1.0 - sigmoid))).astype(bf16)
+        up_ref[...] = silu.astype(bf16)
+
+    weight_specs = [pl.BlockSpec((4, rows, TILE), lambda j, _: (0, 0, j))] + [
+        pl.BlockSpec((shards - 1, rows, TILE), lambda j, _: (0, 0, j))
+    ] * 4
+    token_spec = pl.BlockSpec((tokens, TILE), lambda j, _: (0, j))
+    token_shape = jax.ShapeDtypeStruct((tokens, width), bf16)
+    operands = []
+    for weight, parts in zip(weights, pieces):
+        operands += [weight.reshape(4, rows, width)] + [part[0] for part in parts]
+    return pl.pallas_call(
+        kernel,
+        out_shape=(
+            token_shape,
+            token_shape,
+            token_shape,
+            jax.ShapeDtypeStruct((2, model_width, width), bf16),
+        ),
+        grid_spec=pltpu.PrefetchScalarGridSpec(
+            num_scalar_prefetch=1,
+            grid=(width // TILE,),
+            in_specs=[pl.BlockSpec((tokens, model_width), lambda j, _: (0, 0))] + weight_specs * 2
+            + [UNREAD] * len(after),
+            out_specs=(
+                token_spec,
+                token_spec,
+                token_spec,
+                pl.BlockSpec((2, model_width, TILE), lambda j, _: (0, 0, j)),
+            ),
+        ),
+        compiler_params=ROOMY,
+        cost_estimate=taking(29),
+        name="feed_forward",
+    )(jnp.stack([ctx, me]), normed, *operands, *after)
+
+
+def feed_back(grad_out, down_full, gate_factor, up_factor, low, after=()):
+    tokens, model_width = grad_out.shape
+    width = down_full.shape[0]
+
+    def kernel(where, grad_ref, down_ref, gate_ref, up_ref, *rest):
+        kept_ref, given_ref = rest[-2:]
+        hidden_delta = dot(grad_ref[...], down_ref[...], 1, 1)
+        gate_delta = (hidden_delta * gate_ref[...].astype(f32)).astype(bf16)
+        up_delta = (hidden_delta * up_ref[...].astype(f32)).astype(bf16)
+
+        @pl.when(where[0] == 0)
+        def _():
+            kept_ref[...] = gate_delta
+            given_ref[...] = up_delta
+
+        @pl.when(where[0] != 0)
+        def _():
+            kept_ref[...] = up_delta
+            given_ref[...] = gate_delta
+
+    token_spec = pl.BlockSpec((tokens, TILE), lambda j, _: (0, j))
+    token_shape = jax.ShapeDtypeStruct((tokens, width), bf16)
+    return pl.pallas_call(
+        kernel,
+        out_shape=(token_shape, token_shape),
+        grid_spec=pltpu.PrefetchScalarGridSpec(
+            num_scalar_prefetch=1,
+            grid=(width // TILE,),
+            in_specs=[
+                pl.BlockSpec((tokens, model_width), lambda j, _: (0, 0)),
+                pl.BlockSpec((TILE, model_width), lambda j, _: (j, 0)),
+                token_spec,
+                token_spec,
+            ]
+            + [UNREAD] * len(after),
+            out_specs=(token_spec, token_spec),
+        ),
+        compiler_params=ROOMY,
+        cost_estimate=taking(19),
+        name="feed_back",
+    )(low.reshape(1), grad_out, down_full, gate_factor, up_factor, *after)
+
+
+def feed_input(kept, given, full, low, part, parts, after=()):
+    tokens, width = kept.shape
+    model_width = full.shape[1]
+    tiles = model_width // parts // TILE
+
+    def kernel(where, kept_ref, given_ref, kept_weight, given_weight, *rest):
+        total = dot(kept_ref[...], kept_weight[0], 1, 1)
+        total += dot(given_ref[...], given_weight[0], 1, 1)
+        rest[-1][...] = total.astype(bf16)
+
+    return pl.pallas_call(
+        kernel,
+        out_shape=jax.ShapeDtypeStruct((tokens, model_width // parts), bf16),
+        grid_spec=pltpu.PrefetchScalarGridSpec(
+            num_scalar_prefetch=1,
+            grid=(tiles,),
+            in_specs=[
+                pl.BlockSpec((tokens, width), lambda j, _: (0, 0)),
+                pl.BlockSpec((tokens, width), lambda j, _: (0, 0)),
+                pl.BlockSpec((1, TILE, width), lambda j, where: (where[0], part * tiles + j, 0)),
+                pl.BlockSpec((1, TILE, width), lambda j, where: (1 - where[0], part * tiles + j, 0)),
+            ]
+            + [UNREAD] * len(after),
+            out_specs=pl.BlockSpec((tokens, TILE), lambda j, _: (0, j)),
+        ),
+        compiler_params=ROOMY,
+        cost_estimate=taking(10),
+        name="feed_input",
+    )(low.reshape(1), kept, given, full, full, *after)
+
+
+def product(left, right, left_dim, right_dim, tile, after=()):
+    rows = left.shape[1 - left_dim]
+    width = right.shape[1 - right_dim]
+    turn = left_dim == 0 and right_dim == 1
+
+    def kernel(left_ref, right_ref, *rest):
+        value = turned(left_ref[...]) if turn else left_ref[...]
+        total = dot(value, right_ref[...], 1 if turn else left_dim, right_dim)
+        rest[-1][...] = total.astype(bf16)
+
+    if right_dim == 0:
+        right_spec = pl.BlockSpec((right.shape[0], tile), lambda j: (0, j))
+    else:
+        right_spec = pl.BlockSpec((tile, left.shape[left_dim]), lambda j: (j, 0))
+    return pl.pallas_call(
+        kernel,
+        out_shape=jax.ShapeDtypeStruct((rows, width), bf16),
+        grid=(width // tile,),
+        in_specs=[pl.BlockSpec(left.shape, lambda j: (0, 0)), right_spec] + [UNREAD] * len(after),
+        out_specs=pl.BlockSpec((rows, tile), lambda j: (0, j)),
+        compiler_params=ROOMY,
+        cost_estimate=taking(6),
+        name="product",
+    )(left, right, *after)
+
+
+def add_and_norm(activations, mine, came, gain, after=()):
+    count = len(mine)
+    rows, width = mine[0].shape
+
+    def kernel(act_ref, gain_ref, *refs):
+        residual_ref, normed_ref = refs[-2:]
+        for i in range(count):
+
+            @pl.when(pl.program_id(0) == i)
+            def _():
+                total = refs[i][...].astype(f32) + refs[count + i][...].astype(f32)
+                residual = act_ref[...].astype(f32) + total
+                inverse = lax.rsqrt(jnp.mean(residual * residual, -1, keepdims=True) + epsilon)
+                residual_ref[...] = residual
+                normed_ref[...] = (residual * inverse * gain_ref[...]).astype(bf16)
+
+    row_spec = pl.BlockSpec((rows, width), lambda i: (i, 0))
+    one_spec = pl.BlockSpec((rows, width), lambda i: (0, 0))
+    return pl.pallas_call(
+        kernel,
+        out_shape=(
+            jax.ShapeDtypeStruct(activations.shape, f32),
+            jax.ShapeDtypeStruct(activations.shape, bf16),
+        ),
+        grid=(count,),
+        in_specs=[row_spec, pl.BlockSpec((1, width), lambda i: (0, 0))]
+        + [one_spec] * (2 * count)
+        + [UNREAD] * len(after),
+        out_specs=(row_spec, row_spec),
+        compiler_params=ROOMY,
+        cost_estimate=taking(9),
+        name="add_and_norm",
+    )(activations, gain[None, :], *mine, *came, *after)
+
+
+def add_three(residual, mine, came, after=()):
+    tokens, width = residual.shape
+    rows = 128
+
+    def kernel(residual_ref, mine_ref, came_ref, *rest):
+        total = mine_ref[...].astype(f32) + came_ref[...].astype(f32)
+        rest[-1][...] = (residual_ref[...] + total).astype(bf16)
+
+    row_spec = pl.BlockSpec((rows, width), lambda i: (i, 0))
+    return pl.pallas_call(
+        kernel,
+        out_shape=jax.ShapeDtypeStruct((tokens, width), bf16),
+        grid=(tokens // rows,),
+        in_specs=[row_spec] * 3 + [UNREAD] * len(after),
+        out_specs=row_spec,
+        compiler_params=ROOMY,
+        cost_estimate=taking(5),
+        name="add_three",
+    )(residual, mine, came, *after)
+
+
+def norm_gradient(value, delta, gain, base):
+    inverse = lax.rsqrt(jnp.mean(value * value, -1, keepdims=True) + epsilon)
+    unit = value * inverse
+    scaled = delta * gain
+    total = base + inverse * (scaled - unit * jnp.mean(scaled * unit, -1, keepdims=True))
+    return total, jnp.sum(delta * unit, 0, keepdims=True)
+
+
+def add_term(term_ref, term):
+    @pl.when(pl.program_id(0) == 0)
+    def _():
+        term_ref[...] = term
+
+    @pl.when(pl.program_id(0) != 0)
+    def _():
+        term_ref[...] += term
+
+
+def norm_back(values, mine, came, gain, base, after=()):
+    count = len(mine)
+    tokens, width = values.shape
+    rows = 128
+
+    def kernel(value_ref, gain_ref, base_ref, *refs):
+        delta = jnp.concatenate(
+            [refs[i][...].astype(f32) + refs[count + i][...].astype(f32) for i in range(count)], 1
+        )
+        total, term = norm_gradient(
+            value_ref[...], delta, gain_ref[...], base_ref[...].astype(f32)
+        )
+        refs[-3][...] = total
+        refs[-1][...] = total.astype(bf16)
+        add_term(refs[-2], term)
+
+    row_spec = pl.BlockSpec((rows, width), lambda i: (i, 0))
+    part_spec = pl.BlockSpec((rows, width // count), lambda i: (i, 0))
+    line_spec = pl.BlockSpec((1, width), lambda i: (0, 0))
+    return pl.pallas_call(
+        kernel,
+        out_shape=(
+            jax.ShapeDtypeStruct((tokens, width), f32),
+            jax.ShapeDtypeStruct((1, width), f32),
+            jax.ShapeDtypeStruct((tokens, width), bf16),
+        ),
+        grid=(tokens // rows,),
+        in_specs=[row_spec, line_spec, row_spec]
+        + [part_spec] * (2 * count)
+        + [UNREAD] * len(after),
+        out_specs=(row_spec, line_spec, row_spec),
+        compiler_params=ROOMY,
+        cost_estimate=taking(12),
+        name="norm_back",
+    )(values, gain[None, :], base, *mine, *came, *after)
+
+
+def norm_back_rows(values, mine, came, term, gain, base, after=()):
+    count = len(mine)
+    tokens, width = values.shape
+    rows = 128
+    steps = mine[0].shape[0] // rows
+
+    def kernel(value_ref, term_ref, gain_ref, base_ref, *refs):
+        for i in range(count):
+
+            @pl.when(pl.program_id(0) // steps == i)
+            def _():
+                delta = refs[i][...].astype(f32) + refs[count + i][...].astype(f32)
+                total, gain_term = norm_gradient(
+                    value_ref[...].astype(f32),
+                    delta + term_ref[...],
+                    gain_ref[...],
+                    base_ref[...],
+                )
+                refs[-2][...] = total
+                add_term(refs[-1], gain_term)
+
+    row_spec = pl.BlockSpec((rows, width), lambda i: (i, 0))
+    line_spec = pl.BlockSpec((1, width), lambda i: (0, 0))
+
+    def part_spec(at):
+        return pl.BlockSpec(
+            (rows, width), lambda i: (jnp.clip(i - at * steps, 0, steps - 1), 0)
+        )
+
+    part_specs = [part_spec(i) for i in range(count)]
+    return pl.pallas_call(
+        kernel,
+        out_shape=(
+            jax.ShapeDtypeStruct((tokens, width), f32),
+            jax.ShapeDtypeStruct((1, width), f32),
+        ),
+        grid=(tokens // rows,),
+        in_specs=[row_spec, row_spec, line_spec, row_spec]
+        + part_specs * 2
+        + [UNREAD] * len(after),
+        out_specs=(row_spec, line_spec),
+        compiler_params=ROOMY,
+        cost_estimate=taking(13),
+        name="norm_back_rows",
+    )(values, term, gain[None, :], base, *mine, *came, *after)
 
 
 def block_bias(start_row, key_first, diagonal):
@@ -137,7 +480,8 @@
     return jnp.transpose(block.astype(f32)).astype(bf16)
 
 
-def attend_kernel(group, info, q_ref, k_ref, v_ref, start_ref, o_ref, lse_ref, acc, top):
+def attend_kernel(group, info, q_ref, k_ref, v_ref, start_ref, *rest):
+    o_ref, lse_ref, acc, top = rest[-4:]
     here, first = info[0], info[1]
     size = q_ref.shape[1]
 
@@ -170,7 +514,7 @@
         lse_ref[0, h : h + 1, :] = top[h] + jnp.log(total)
 
 
-def attend(info, query_t, keyval, start_row, kv_heads, seq):
+def attend(info, query_t, keyval, start_row, kv_heads, seq, after=()):
     blocks, kv_rows, _ = keyval.shape
     size = start_row.shape[1]
     group = query_t.shape[0] // HEAD // kv_heads
@@ -189,7 +533,8 @@
                 pl.BlockSpec((blocks, HEAD, size), lambda g, _: (0, g, seq)),
                 pl.BlockSpec((blocks, HEAD, size), lambda g, _: (0, kv_heads + g, seq)),
                 pl.BlockSpec((1, size), lambda g, _: (0, 0)),
-            ],
+            ]
+            + [UNREAD] * len(after),
             out_specs=(
                 pl.BlockSpec((rows, size), lambda g, _: (g, 0)),
                 pl.BlockSpec((1, group, size), lambda g, _: (g, 0, 0)),
@@ -200,19 +545,15 @@
             ],
         ),
         compiler_params=pltpu.CompilerParams(vmem_limit_bytes=48 * 2**20),
-        cost_estimate=pl.CostEstimate(
-            flops=2 * 2 * query_t.shape[0] * size * size * blocks * 4,
-            bytes_accessed=4 * query_t.shape[0] * size,
-            transcendentals=0,
-        ),
+        cost_estimate=taking(14),
         name="attend",
-    )(info, query_t, keyval, keyval, start_row)
+    )(info, query_t, keyval, keyval, start_row, *after)
 
 
 def attend_back_kernel(
-    group, info, q_ref, k_ref, v_ref, start_ref, d_ref, o_ref, lse_ref, cos_ref, sin_ref,
-    dq_ref, dk_ref, dv_ref, acc, inner,
+    group, info, q_ref, k_ref, v_ref, start_ref, d_ref, o_ref, lse_ref, cos_ref, sin_ref, *rest
 ):
+    dq_ref, dk_ref, dv_ref, acc, inner = rest[-5:]
     here, first = info[0], info[1]
     size = q_ref.shape[1]
     rows = [slice(h * HEAD, (h + 1) * HEAD) for h in range(group)]
@@ -270,7 +611,7 @@
 
 
 def attend_back(
-    info, query_t, keyval, start_row, delta_t, mixed_t, log_sums, cosine, sine, kv_heads, seq
+    info, query_t, keyval, start_row, delta_t, mixed_t, log_sums, cosine, sine, kv_heads, seq, after=()
 ):
     blocks = keyval.shape[0]
     size = start_row.shape[1]
@@ -294,7 +635,8 @@
                 pl.BlockSpec((1, group, size), lambda g, _: (g, 0, 0)),
                 pl.BlockSpec((HALF, size), lambda g, _: (0, seq)),
                 pl.BlockSpec((HALF, size), lambda g, _: (0, seq)),
-            ],
+            ]
+            + [UNREAD] * len(after),
             out_specs=(pl.BlockSpec((rows, size), lambda g, _: (g, 0)), kv_spec, kv_spec),
             scratch_shapes=[
                 pltpu.VMEM((rows, size), f32),
@@ -302,13 +644,9 @@
             ],
         ),
         compiler_params=pltpu.CompilerParams(vmem_limit_bytes=48 * 2**20),
-        cost_estimate=pl.CostEstimate(
-            flops=5 * 2 * query_t.shape[0] * size * size * blocks * 4,
-            bytes_accessed=8 * query_t.shape[0] * size,
-            transcendentals=0,
-        ),
+        cost_estimate=taking(16),
         name="attend_back",
-    )(info, query_t, keyval, keyval, start_row, delta_t, mixed_t, log_sums, cosine, sine)
+    )(info, query_t, keyval, keyval, start_row, delta_t, mixed_t, log_sums, cosine, sine, *after)
 
 
 def rotate_t(values, cosine, sine):
@@ -323,19 +661,30 @@
     return jnp.where(index == 0, when_zero, when_one)
 
 
-def block_products(lefts, rights, came, high, shards, left_rows, right_rows, left_cut):
+def block_products(
+    lefts, rights, came, high, shards, left_rows, right_rows, left_cut, half=None, after=()
+):
     cut_side, whole_side = (lefts, rights) if left_cut else (rights, lefts)
     whole_rows = right_rows if left_cut else left_rows
     tokens, model_width = cut_side[0].shape
-    part = model_width // shards // 2
+    if high is None:
+        part = model_width // shards
+        where_high = jnp.zeros((1,), jnp.int32)
+        cut_spec = pl.BlockSpec((tokens, part), lambda j, s, where: (0, s))
+    else:
+        part = model_width // shards // 2
+        where_high = high.reshape(1)
+        cut_spec = pl.BlockSpec((tokens, part), lambda j, s, where: (0, s * 2 + where[0]))
     whole = whole_side[0].shape[1 - whole_rows]
+    first = 0
+    if half is not None:
+        whole, first = whole // 2, half
     tile = whole // 2 if whole > 1408 else whole
     steps = whole // tile
-    cut_spec = pl.BlockSpec((tokens, part), lambda j, s, where: (0, s * 2 + where[0]))
     if whole_rows == 0:
-        whole_spec = pl.BlockSpec((tokens, tile), lambda j, s, where: (0, j))
+        whole_spec = pl.BlockSpec((tokens, tile), lambda j, s, where: (0, first + j))
     else:
-        whole_spec = pl.BlockSpec((tile, tokens), lambda j, s, where: (j, 0))
+        whole_spec = pl.BlockSpec((tile, tokens), lambda j, s, where: (first + j, 0))
     left_spec, right_spec = (cut_spec, whole_spec) if left_cut else (whole_spec, cut_spec)
     if left_cut:
         out_shape = (shards, part, whole)
@@ -358,17 +707,16 @@
         grid_spec=pltpu.PrefetchScalarGridSpec(
             num_scalar_prefetch=1,
             grid=(steps, shards),
-            in_specs=[left_spec] * 2 + [right_spec] * 2 + [out_spec] * len(extra),
+            in_specs=[left_spec] * 2
+            + [right_spec] * 2
+            + [out_spec] * len(extra)
+            + [UNREAD] * len(after),
             out_specs=out_spec,
         ),
         compiler_params=pltpu.CompilerParams(vmem_limit_bytes=56 * 2**20),
-        cost_estimate=pl.CostEstimate(
-            flops=4 * tokens * shards * part * whole,
-            bytes_accessed=4 * tokens * (shards * part + whole) + 2 * shards * part * whole,
-            transcendentals=0,
-        ),
+        cost_estimate=taking(9),
         name="block_products",
-    )(high.reshape(1), *lefts, *rights, *extra)
+    )(where_high, *lefts, *rights, *extra, *after)
 
 
 def column_half(values, which, shards):
@@ -377,9 +725,14 @@
     return lax.dynamic_slice_in_dim(values.reshape(tokens, shards, 2, part), which, 1, 2)[:, :, 0]
 
 
-def plain_products(lefts, rights, came, high, shards, left_rows, right_rows, left_cut):
+def plain_products(
+    lefts, rights, came, high, shards, left_rows, right_rows, left_cut, half=None, after=()
+):
     left = jnp.concatenate(lefts, left_rows)
     right = jnp.concatenate(rights, right_rows)
+    if half is not None:
+        size = right.shape[1] // 2
+        right = right[:, half * size : (half + 1) * size]
     if left_cut:
         total = jnp.einsum(
             "tsp,tn->spn" if right_rows == 0 else "tsp,nt->spn",
@@ -393,13 +746,27 @@
     return (total if came is None else total + came.astype(f32)).astype(bf16)
 
 
-def reduced(lefts, rights, high, shards, left_rows, right_rows, left_cut):
-    width = (lefts if left_cut else rights)[0].shape[1]
-    products = block_products if width // shards // 2 % 128 == 0 else plain_products
-    other = products(lefts, rights, None, 1 - high, shards, left_rows, right_rows, left_cut)
-    came = high_swap(other)
-    total = products(lefts, rights, came, high, shards, left_rows, right_rows, left_cut)
+def over_shard(total):
     return lax.psum_scatter(total, "shard", scatter_dimension=0, tiled=True)[0]
+
+
+class Reduced:
+    def __init__(self, lefts, rights, high, shards, left_rows, right_rows, left_cut, half=None):
+        width = (lefts if left_cut else rights)[0].shape[1]
+        self.products = block_products if width // shards // 2 % 128 == 0 else plain_products
+        self.sides = lefts, rights
+        self.high = high
+        self.rest = shards, left_rows, right_rows, left_cut, half
+
+    def send(self, after=(), swap_after=()):
+        self.other = self.products(*self.sides, None, 1 - self.high, *self.rest, after)
+        self.sent = tie(self.other, *swap_after)
+        self.came = high_swap(self.sent)
+
+    def add(self, after=(), sum_after=()):
+        self.total = self.products(*self.sides, self.came, self.high, *self.rest, after)
+        self.tied = tie(self.total, *sum_after)
+        return over_shard(self.tied)
 
 
 def halves(high, own, axis):
@@ -432,20 +799,36 @@
     low, high = ctx % 2, ctx // 2
 
     me = lax.axis_index("shard")
-    small = shards <= 4
-
-    def whole(weight, along_rows, direct):
-        pieces = fetch(weight, ctx, me, shards, direct and small)
-        return place(weight, pieces, ctx, me, shards, along_rows)
-
-    qkv_local = jnp.concatenate([query_weight, key_weight, value_weight], 1)
-    qkv_weight = whole(qkv_local, True, False)
-    gain_one = lax.all_gather(jnp.stack([attn_gain, ffn_gain]), "shard", axis=1, tiled=True)
-    gain_one, gain_two = gain_one[0].astype(f32), gain_one[1].astype(f32)
-    out_weight = whole(output_weight, False, False)
-    down_full = whole(down_weight, False, False)
-    gate_full = whole(gate_weight, True, False)
-    up_full = whole(up_weight, True, True)
+    where = (ctx, me, shards)
+
+    def apart(weight, *after):
+        if shards > 4:
+            return [others(gathered(weight, ctx), me)]
+        mine = quarter(weight, ctx)
+        mine = tie(mine, *after) if after else mine
+        return [lax.ppermute(mine, "shard", ring(shards, r))[None] for r in range(1, shards)]
+
+    gains = jnp.pad(jnp.stack([attn_gain, ffn_gain], 1), ((0, 0), (0, 126)))
+    qkv_local = jnp.concatenate([query_weight, key_weight, value_weight, gains], 1)
+    qkv_own = apart(qkv_local)
+
+    def later(weight, *after):
+        return lax.all_gather(tie(quarter(weight, ctx), *after), "shard", axis=0, tiled=False)
+
+    out_own = others(later(output_weight, *qkv_own), me)
+    gate_all = later(gate_weight, *qkv_own)
+    up_all = later(up_weight, *qkv_own)
+    down_all = later(down_weight, *qkv_own)
+    out_pieces = spread([out_own])
+    qkv_weight = place(qkv_local, spread(qkv_own), *where, True, [out_own])
+    gain_one = qkv_weight[:, -128].astype(f32)
+    gain_two = qkv_weight[:, -127].astype(f32)
+    keyval_weight = qkv_weight[:, query_cols:-128]
+    keyval_other = lax.ppermute(keyval_weight, "tp", SWAP_TP)
+    tp = lax.axis_index("tp")
+    keyval_weight = jnp.concatenate(
+        [pick(tp, keyval_weight, keyval_other), pick(tp, keyval_other, keyval_weight)], 1
+    )
 
     index = jnp.arange(seq_len, dtype=jnp.int32)[None, :]
     doc_start = jnp.zeros_like(segments)
@@ -466,127 +849,167 @@
     unit_one = inputs * inv_one
     normed_one = (unit_one * gain_one[None, :]).astype(bf16)
 
-    projected = dot(qkv_weight, normed_one, 0, 1)
+    projected = dot(qkv_weight[:, :-128], normed_one, 0, 1)
     query_t = (rotate_t(projected[:query_cols], cosine, sine) * HEAD ** (-0.5)).astype(bf16)
     key_t = rotate_t(projected[query_cols : query_cols + kv_width], cosine, sine).astype(bf16)
     value_t = projected[query_cols + kv_width :].astype(bf16)
-    keyval = lax.all_gather(jnp.concatenate([key_t, value_t], 0), "ctx", axis=0, tiled=False)
-
-    mixed, log_sums, residual, infos = [], [], [], []
+    keyval = jnp.concatenate([key_t, value_t], 0)[None]
+    came = low_swap(keyval)
+    keyval = jnp.concatenate([pick(low, keyval, came), pick(low, came, keyval)], 0)
+    keyval = tie(keyval, out_pieces[2][0])
+    came = high_swap(keyval)
+    keyval = jnp.concatenate([pick(high, keyval, came), pick(high, came, keyval)], 0)
+    out_weight = place(output_weight, out_pieces, *where, False, [query_t])
+    gate_own = others(tie(gate_all, came), me)
+    mixed, log_sums, infos, mine, came = [], [], [], [], []
+    last = [out_weight, gate_own, keyval_weight]
     for s in range(seq_here):
         infos.append(jnp.stack([ctx, first_block[s]]).astype(jnp.int32))
-        mixed_s, log_s = attend(infos[s], query_t, keyval, start_here[s : s + 1], kv_heads, s)
+        mixed_s, log_s = attend(
+            infos[s], query_t, keyval, start_here[s : s + 1], kv_heads, s, last + came[s - 2 : s - 1]
+        )
         mixed.append(mixed_s)
         log_sums.append(log_s)
-        residual.append(tp_sum(dot(mixed_s, out_weight, 0, 0)))
-    residual = inputs + jnp.concatenate(residual, 0)
+        mine.append(product(mixed_s, out_weight, 0, 0, 512, came[1:2]))
+        came.append(lax.ppermute(mine[s], "tp", SWAP_TP))
+        last = [mine[s]]
+        if s == 1:
+            up_own = others(tie(up_all, mine[s]), me)
+            last.append(up_own)
     mixed_t = jnp.concatenate(mixed, 1)
-
-    inv_two = lax.rsqrt(jnp.mean(residual * residual, -1, keepdims=True) + epsilon)
-    unit_two = residual * inv_two
-    normed_two = (unit_two * gain_two[None, :]).astype(bf16)
-    gate_proj = dot(normed_two, gate_full, 1, 0)
-    up_value = dot(normed_two, up_full, 1, 0)
-    sigmoid_gate = jax.nn.sigmoid(gate_proj)
-    silu_gate = gate_proj * sigmoid_gate
-    hidden = (silu_gate * up_value).astype(bf16)
-
-    hidden_delta = dot(grad_out, down_full, 1, 1)
-    gate_delta = (
-        hidden_delta * up_value * sigmoid_gate * (1.0 + gate_proj * (1.0 - sigmoid_gate))
-    ).astype(bf16)
-    up_delta = (hidden_delta * silu_gate).astype(bf16)
-    chunk = model_width // 4
-    parts = []
-    for i in range(4):
-        rows = slice(i * chunk, (i + 1) * chunk)
-        parts.append(tp_sum(dot(gate_delta, gate_full[rows], 1, 1) + dot(up_delta, up_full[rows], 1, 1)))
-    normed_two_delta = jnp.concatenate(parts, 1)
-    ffn_branch = tp_sum(dot(hidden, down_full, 1, 0))
-    block_out = (residual + ffn_branch).astype(bf16).reshape(activations.shape)
-
-    ffn_gain_term = jnp.sum(normed_two_delta * unit_two, 0)
-    scaled_two = normed_two_delta * gain_two[None, :]
-    residual_delta = grad_out.astype(f32) + inv_two * (
-        scaled_two - unit_two * jnp.mean(scaled_two * unit_two, -1, keepdims=True)
+    acts = activations.reshape(tokens, model_width)
+    gate_pieces = spread([gate_own], came[-1])
+    up_pieces = spread([up_own], came[-1])
+    down_own = others(tie(down_all, mine[-1]), me)
+    residual, normed_two = add_and_norm(acts, mine, came, gain_two, [gate_pieces[2][0], down_own])
+    hidden, gate_factor, up_factor, gate_up_full = feed_forward(
+        normed_two, (gate_weight, up_weight), (gate_pieces, up_pieces), *where
     )
-    residual_round = residual_delta.astype(bf16)
-
-    kept = pick(low, gate_delta, up_delta)
-    given = pick(low, up_delta, gate_delta)
+
+    hidden_pair = (hidden, low_swap(hidden))
+    cotangent_pair = (grad_out, low_swap(grad_out))
+    products = block_products if model_width // shards % 256 == 0 else plain_products
+    down_pieces = spread([down_own], hidden)
+    down_full = place(down_weight, down_pieces, *where, False, [hidden])
+    down_products = products(
+        hidden_pair, cotangent_pair, None, low, shards, 0, 0, False, None, [down_full]
+    )
+    down_sum = over_shard(down_products)
+    kept, given = feed_back(grad_out, down_full, gate_factor, up_factor, low, [down_products])
+
     normed_pair = (normed_two, low_swap(normed_two))
-    gate_up = reduced(normed_pair, (kept, low_swap(given)), high, shards, 0, 0, True)
-    gate_up = halves(high, gate_up, 0)
-    gate_up_other = low_swap(gate_up)
-    gate_grad = pick(low, gate_up, gate_up_other).astype(f32)
-    up_grad = pick(low, gate_up_other, gate_up).astype(f32)
-
-    part = hidden.shape[1] // 2
-    hidden_kept = lax.dynamic_slice_in_dim(hidden, low * part, part, 1)
-    hidden_given = lax.dynamic_slice_in_dim(hidden, (1 - low) * part, part, 1)
-    hidden_pair = (hidden_kept, low_swap(hidden_given))
-    cotangent_pair = (grad_out, low_swap(grad_out))
-    down = reduced(hidden_pair, cotangent_pair, high, shards, 0, 0, False)
-    down = halves(high, down, 1)
-    down_other = low_swap(down)
-    down_grad = jnp.concatenate([pick(low, down, down_other), pick(low, down_other, down)], 0)
-    down_grad = down_grad.astype(f32)
-
-    delta_t = dot(out_weight, residual_round, 1, 1).astype(bf16)
+    delta_pair = (kept, low_swap(given))
+    gate_up = [Reduced(normed_pair, delta_pair, high, shards, 0, 0, True, i) for i in range(2)]
+
+    chunks = 4
+    mine, came = [], []
+    last = []
+    for i in range(chunks):
+        mine.append(
+            feed_input(kept, given, gate_up_full, low, i, chunks, last + came[max(i - 2, 0) : i - 1])
+        )
+        came.append(lax.ppermute(mine[i], "tp", SWAP_TP))
+        last = [mine[i]]
+        if i % 2 == 0:
+            gate_up[i // 2].send(last, [gate_up[0].came] if i else [])
+            last = [gate_up[0].sent] if i == 0 else last
+    gate_up_first = gate_up[0].add([mine[-1], gate_up[1].sent], [down_sum])
+    ffn_mine = product(hidden, down_full, 1, 0, TILE, [gate_up[0].tied])
+    residual_delta, ffn_gain_term, residual_round = norm_back(
+        residual, mine, came, gain_two, grad_out, [ffn_mine]
+    )
+    delta_t = product(out_weight, residual_round, 1, 1, TILE)
+    ffn_came = lax.ppermute(ffn_mine, "tp", SWAP_TP)
 
     half_rows = query_cols // 2
     mixed_kept = lax.dynamic_slice_in_dim(mixed_t, low * half_rows, half_rows, 0)
     mixed_given = lax.dynamic_slice_in_dim(mixed_t, (1 - low) * half_rows, half_rows, 0)
     mixed_pair = (mixed_kept, low_swap(mixed_given))
     residual_pair = (residual_round, low_swap(residual_round))
-    output = reduced(mixed_pair, residual_pair, high, shards, 1, 0, False)
-    output = halves(high, output, 1)
-    output_other = low_swap(output)
-    output_grad = jnp.concatenate(
-        [pick(low, output, output_other), pick(low, output_other, output)], 0
-    ).astype(f32)
-
-    deltas, normed_one_delta = [], []
+    output = Reduced(mixed_pair, residual_pair, high, shards, 1, 0, False)
+
+    gate_up_second = gate_up[1].add([delta_t], [gate_up_first])
+    query_deltas, part_sums, mine, came = [], [], [], []
+    last = [gate_up[1].tied]
     for s in range(seq_here):
         query_delta, key_part, value_part = attend_back(
             infos[s], query_t, keyval, start_here[s : s + 1], delta_t, mixed[s], log_sums[s],
-            cosine, sine, kv_heads, s,
+            cosine, sine, kv_heads, s, last,
         )
-        part_sum = jnp.concatenate([key_part, value_part], 1).reshape(2, 2, 2 * kv_width, block_len)
-        sent = lax.dynamic_index_in_dim(part_sum, 1 - high, 0, False)
-        kept = lax.dynamic_index_in_dim(part_sum, high, 0, False)
-        kept = kept.astype(f32) + high_swap(sent).astype(f32)
-        sent = lax.dynamic_index_in_dim(kept, 1 - low, 0, False).astype(bf16)
-        kept = lax.dynamic_index_in_dim(kept, low, 0, False)
-        keyval_delta = kept + low_swap(sent).astype(f32)
-        cols = slice(s * block_len, (s + 1) * block_len)
-        key_delta = rotate_t(keyval_delta[:kv_width], cosine[:, cols], -sine[:, cols])
-        delta = jnp.concatenate(
-            [query_delta, key_delta.astype(bf16), keyval_delta[kv_width:].astype(bf16)], 0
-        )
-        deltas.append(delta)
-        normed_one_delta.append(tp_sum(dot(delta, qkv_weight, 0, 1)))
-    delta_all = jnp.concatenate(deltas, 1)
-    normed_one_delta = jnp.concatenate(normed_one_delta, 0)
-
-    attn_gain_term = jnp.sum(normed_one_delta * unit_one, 0)
-    scaled_one = normed_one_delta * gain_one[None, :]
-    input_grad = residual_delta + inv_one * (
-        scaled_one - unit_one * jnp.mean(scaled_one * unit_one, -1, keepdims=True)
+        query_deltas.append(query_delta)
+        part_sums.append(jnp.concatenate([key_part, value_part], 1))
+        mine.append(product(query_delta, qkv_weight[:, :query_cols], 0, 1, 512, came[s - 1 : s]))
+        came.append(lax.ppermute(mine[s], "tp", SWAP_TP))
+        last = [mine[s]]
+        if s == 0:
+            output.send(last, [gate_up[1].came])
+            last = [output.sent, ffn_came]
+        if s == 1:
+            output.total = output.products(*output.sides, output.came, high, *output.rest, last)
+            last = [output.total]
+    down_came = high_swap(tie(down_sum, output.came))
+
+    part_sum = jnp.concatenate(part_sums, 2).reshape(2, 2, 2 * kv_width, tokens)
+    sent = lax.dynamic_index_in_dim(part_sum, 1 - high, 0, False)
+    part_came = high_swap(sent)
+
+    normed_pair_one = (normed_one, low_swap(normed_one))
+
+    def products_of(delta, after):
+        half_rows = delta.shape[0] // 2
+        kept = lax.dynamic_slice_in_dim(delta, low * half_rows, half_rows, 0)
+        given = lax.dynamic_slice_in_dim(delta, (1 - low) * half_rows, half_rows, 0)
+        pair = (kept.T, low_swap(given).T)
+        return block_products(normed_pair_one, pair, None, None, shards, 0, 0, True, None, after)
+
+    output_tied = tie(output.total, gate_up_second)
+    query_products = products_of(jnp.concatenate(query_deltas, 1), [mine[-1], output_tied])
+    output_sum = over_shard(output_tied)
+    query_tied = tie(query_products, output_sum)
+    query_sum = over_shard(query_tied)
+
+    kept = lax.dynamic_index_in_dim(part_sum, high, 0, False)
+    kept = kept.astype(f32) + part_came.astype(f32)
+    sent = lax.dynamic_index_in_dim(kept, 1 - low, 0, False).astype(bf16)
+    kept = lax.dynamic_index_in_dim(kept, low, 0, False)
+    keyval_delta = kept + low_swap(sent).astype(f32)
+    key_delta = rotate_t(keyval_delta[:kv_width], cosine, -sine)
+    keyval_delta = jnp.concatenate(
+        [key_delta.astype(bf16), keyval_delta[kv_width:].astype(bf16)], 0
     )
-
-    half_rows = delta_all.shape[0] // 2
-    delta_kept = lax.dynamic_slice_in_dim(delta_all, low * half_rows, half_rows, 0)
-    delta_given = lax.dynamic_slice_in_dim(delta_all, (1 - low) * half_rows, half_rows, 0)
-    delta_pair = (delta_kept.T, low_swap(delta_given).T)
-    normed_pair_one = (normed_one, low_swap(normed_one))
-    qkv = reduced(normed_pair_one, delta_pair, high, shards, 0, 0, True)
-    qkv = halves(high, qkv, 0)
-    qkv_other = low_swap(qkv)
-    qkv_grad = jnp.concatenate([pick(low, qkv, qkv_other), pick(low, qkv_other, qkv)], 1)
-    qkv_grad = qkv_grad.astype(f32)
-
-    gain_terms = jnp.stack([attn_gain_term, ffn_gain_term])
+    keyval_came = lax.ppermute(keyval_delta, "tp", SWAP_TP)
+    keyval_both = jnp.concatenate(
+        [pick(tp, keyval_delta, keyval_came), pick(tp, keyval_came, keyval_delta)], 0
+    )
+    keyval_products = products_of(keyval_delta, [query_tied])
+    keyval_term = dot(keyval_both, keyval_weight, 0, 1)
+
+    block_out = add_three(residual, ffn_mine, ffn_came, [keyval_products])
+    block_out = block_out.reshape(activations.shape)
+    input_grad, attn_gain_term = norm_back_rows(
+        acts, mine, came, keyval_term, gain_one, residual_delta, [block_out]
+    )
+    keyval_sum = over_shard(tie(keyval_products, query_sum))
+
+    def two_sides(value):
+        other = low_swap(value)
+        return pick(low, value, other).astype(f32), pick(low, other, value).astype(f32)
+
+    down_sum = (down_sum.astype(f32) + tie(down_came, keyval_products).astype(f32)).astype(bf16)
+    down_grad = jnp.concatenate(two_sides(down_sum), 1)
+    first_gate, first_up = two_sides(halves(high, tie(gate_up_first, part_came), 0))
+    second_gate, second_up = two_sides(halves(high, tie(gate_up_second, part_came), 0))
+    gate_grad = jnp.concatenate([first_gate, second_gate], 1)
+    up_grad = jnp.concatenate([first_up, second_up], 1)
+    output_grad = jnp.concatenate(two_sides(halves(high, output_sum, 1)), 0)
+
+    def high_total(value):
+        return (value.astype(f32) + high_swap(value).astype(f32)).astype(bf16)
+
+    query_grad = jnp.concatenate(two_sides(high_total(query_sum)), 1)
+    key_grad, value_grad = two_sides(high_total(keyval_sum))
+
+    gain_terms = jnp.concatenate([attn_gain_term, ffn_gain_term], 0)
     gain_terms = gain_terms + low_swap(gain_terms)
     gain_terms = gain_terms + high_swap(gain_terms)
     gain_terms = gain_terms.reshape(2, shards, model_width // shards)
@@ -600,9 +1023,9 @@
     return (
         block_out,
         input_grad.reshape(activations.shape),
-        qkv_grad[:, :query_cols],
-        qkv_grad[:, query_cols : query_cols + kv_width],
-        qkv_grad[:, query_cols + kv_width :],
+        query_grad,
+        key_grad,
+        value_grad,
         output_grad,
         gate_grad,
         up_grad,

time: 1140 us -> 811 us (0.71); the launches traced: 1120 us -> 805 us
  waiting for transfers between devices: 504 us -> 222 us
  Pallas kernels: 185 us -> 351 us
  matrix products: 116 us -> 10.1 us
  starting transfers between devices: 120 us -> 76.8 us
  other arithmetic: 95.3 us -> 63 us
    pallas_call x0 -> x41, Pallas kernels: none -> 184 us  [the longest x8 53.5 us: product(): pl.pallas_call(kernel, out_shape=jax.ShapeDtypeStruct((rows, width), bf16...]
    ppermute x19, waiting for transfers between devices: 233 us -> 94.4 us  [high_swap(): return lax.ppermute(value, 'ctx', SWAP_HIGH)]
    ppermute x14 -> x16, waiting for transfers between devices: 229 us -> 109 us  [the longest x6 42.2 us: body(): came.append(lax.ppermute(mine[s], 'tp', SWAP_TP))]
    dot_general x20 -> x2, matrix products: 116 us -> 10.1 us  [dot(): lax.dot_general(left, right, (((left_dim,), (right_dim,)), ((), ())), pre...]
    all_gather x5 -> x4, waiting for transfers between devices: 40.9 us -> 6.97 us  [later(): lax.all_gather(tie(quarter(weight, ctx), *after), 'shard', axis=0, tiled=...]
    ppermute x30 -> x32, starting transfers between devices: 63.8 us -> 33.2 us  [low_swap(): return lax.ppermute(value, 'ctx', SWAP_LOW)]
    convert_element_type x7 -> x5, other arithmetic: 36.1 us -> 7.27 us  [the longest x1 2.87 us: body(): (down_sum.astype(f32) + tie(down_came, keyval_products).astype(f32)).asty...]
    pallas_call x5 -> x3, Pallas kernels: 42.5 us -> 22.8 us  [place(): pl.pallas_call(kernel, out_shape=jax.ShapeDtypeStruct(out_shape, weight.d...]
  transfers between devices with their start and end apart: 75 -> 80, of which waited for: 27 -> 28; matrix products, arithmetic and copies ran while one was open for 23% -> 13% of each run, Pallas kernels for 17% -> 42%
where the time goes in v2:
time: 811 us; the launch traced here: 805 us
  Pallas kernels  351 us (43%)
  waiting for transfers between devices  222 us (27%)
  starting transfers between devices  76.8 us (9%)
  local copies, waits for them, and re-layouts  66.9 us (8%)
  other arithmetic  63 us (8%)
  between operations  15.5 us (2%)
  matrix products  10.1 us (1%)
    ppermute x19, waiting for transfers between devices, high_swap(): return lax.ppermute(value, 'ctx', SWAP_HIGH)  94.4 us
    pallas_call x9, Pallas kernels, block_products(): pl.pallas_call(kernel, out_shape=jax.ShapeDtypeStruct(out_shape, bf16), g...  78.1 us
    pallas_call x8, Pallas kernels, product(): pl.pallas_call(kernel, out_shape=jax.ShapeDtypeStruct((rows, width), bf16...  53.5 us
    ppermute x6, waiting for transfers between devices, body(): came.append(lax.ppermute(mine[s], 'tp', SWAP_TP))  42.2 us
    pallas_call x4, Pallas kernels, feed_input(): pl.pallas_call(kernel, out_shape=jax.ShapeDtypeStruct((tokens, model_widt...  40.4 us
    pallas_call x3, Pallas kernels, attend_back(): pl.pallas_call(lambda *refs: attend_back_kernel(group, *refs), out_shape=...  35.7 us
    unnamed x192, local copies, waits for them, and re-layouts  33.9 us
    ppermute x32, starting transfers between devices, low_swap(): return lax.ppermute(value, 'ctx', SWAP_LOW)  33.2 us
  transfers between devices with their start and end apart: 80, of which 28 were waited for; matrix products, arithmetic and copies ran while one was open for 13% of the time, Pallas kernels for 42%

profile of v2, /device:TPU:1, one launch (start us, length us, event | category | flops | bytes accessed | tf_op | source)
XLA Modules:
  0.0 805.1 jit_solution(17099842617763803250)
XLA Ops:
  21.7 23.0 %collective-permute-done.1 = bf16[128,1408]{1,0:T(8,128)(2,1)S(1)} collective-permute-done((bf16[128,1408]{1,0:T(8,128)(2,1)S(1)}, bf16[128,1408]{1,0:T(8,128)(2,1)S(1)}, u32[]{:S(2)}, u32[]{:S(2)}) %collective-permute-start.1) | collective-permute-done | bytes 360480 | tf_op jit(solution)/shard_map/ppermute | solution.py:809
  110.7 11.6 %collective-permute-done.13.refs_1_.refs_2_ = bf16[3,256,512]{2,1,0:T(8,128)(2,1)S(1)} collective-permute-done((bf16[3,256,512]{2,1,0:T(8,128)(2,1)S(1)}, bf16[3,256,512]{2,1,0:T(8,128)(2,1)S(1)}, u32[]{:S(2)}, u32[]{:S(2)}) %collective-permute-start.13) | collective-permute-done | bytes 786464 | tf_op jit(solution)/shard_map/ppermute | solution.py:26
  134.1 7.6 collective-permute-done.14.refs_1_
  153.9 10.0 %attend.3 = (bf16[1024,256]{1,0:T(8,128)(2,1)S(1)}, f32[2,8,256]{2,1,0:T(8,128)S(1)}) custom-call(s32[2]{0:T(128)S(1)} %get-tuple-element.139.refs_0_, bf16[1024,768]{1,0:T(8,128)(2,1)S(1)} %bitcast.84, bf16[4,256,768]{2,1,0:T(8,128)(2,1)S(1)} %pad_maximum_fusion.4.refs_2_.refs_3_, bf16[4,256,768]{2,1,0:T(8,128)(2,1)S(1)} %pad_maximum_fusion.4.refs_2_.refs_3_, ...), custom_call_target="tpu_custom_call" | custom-call | flops 700000000 | bytes 2100000 | tf_op jit(solution)/shard_map/attend/pallas_call | solution.py:522
  172.6 10.0 %attend.4 = (bf16[1024,256]{1,0:T(8,128)(2,1)S(1)}, f32[2,8,256]{2,1,0:T(8,128)S(1)}) custom-call(s32[2]{0:T(128)S(1)} %get-tuple-element.140.refs_0_, bf16[1024,768]{1,0:T(8,128)(2,1)S(1)} %bitcast.85, bf16[4,256,768]{2,1,0:T(8,128)(2,1)S(1)} %pad_maximum_fusion.4.refs_2_.refs_3_, bf16[4,256,768]{2,1,0:T(8,128)(2,1)S(1)} %pad_maximum_fusion.4.refs_2_.refs_3_, ...), custom_call_target="tpu_custom_call" | custom-call | flops 700000000 | bytes 2100000 | tf_op jit(solution)/shard_map/attend/pallas_call | solution.py:522
  203.0 10.0 %attend.5 = (bf16[1024,256]{1,0:T(8,128)(2,1)S(1)}, f32[2,8,256]{2,1,0:T(8,128)S(1)}) custom-call(s32[2]{0:T(128)S(1)} %pad_add_fusion.3.refs_0_, bf16[1024,768]{1,0:T(8,128)(2,1)S(1)} %bitcast.86, bf16[4,256,768]{2,1,0:T(8,128)(2,1)S(1)} %pad_maximum_fusion.4.refs_2_.refs_3_, bf16[4,256,768]{2,1,0:T(8,128)(2,1)S(1)} %pad_maximum_fusion.4.refs_2_.refs_3_, ...), custom_call_target="tpu_custom_call" | custom-call | flops 700000000 | bytes 2100000 | tf_op jit(solution)/shard_map/attend/pallas_call | solution.py:522
  213.8 10.7 %collective-permute-done.19.rest_0_.refs_4_ = bf16[256,2048]{1,0:T(8,128)(2,1)S(1)} collective-permute-done((bf16[256,2048]{1,0:T(8,128)(2,1)S(1)}, bf16[256,2048]{1,0:T(8,128)(2,1)S(1)}, u32[]{:S(2)}, u32[]{:S(2)}) %collective-permute-start.19) | collective-permute-done | bytes 1048608 | tf_op jit(solution)/shard_map/ppermute | solution.py:874
  234.2 18.2 %collective-permute-done.20.refs_1_.refs_5_ = bf16[256,2048]{1,0:T(8,128)(2,1)} collective-permute-done((bf16[256,2048]{1,0:T(8,128)(2,1)}, bf16[256,2048]{1,0:T(8,128)(2,1)}, u32[]{:S(2)}, u32[]{:S(2)}) %collective-permute-start.20) | collective-permute-done | bytes 1048608 | tf_op jit(solution)/shard_map/ppermute | solution.py:874
  260.1 8.5 %add_and_norm.1 = (f32[768,2048]{1,0:T(8,128)}, bf16[768,2048]{1,0:T(8,128)(2,1)}) custom-call(bf16[768,2048]{1,0:T(8,128)(2,1)} %bitcast.90, f32[1,2048]{1,0:T(1,128)} %bitcast.151, bf16[256,2048]{1,0:T(8,128)(2,1)} %product.8.refs_5_.refs_0_, bf16[256,2048]{1,0:T(8,128)(2,1)} %product.9.refs_1_.refs_5_, bf16[256,2048]{1,0:T(8,128)(2,1)} %product.10.refs_1_.refs_2_, ...), custom_call_target="tpu_custom_call" | custom-call | flops 450000000 | bytes 1350000 | tf_op jit(solution)/shard_map/add_and_norm/pallas_call | solution.py:329
  268.7 28.9 %feed_forward.1 = (bf16[768,2816]{1,0:T(8,128)(2,1)}, bf16[768,2816]{1,0:T(8,128)(2,1)}, bf16[768,2816]{1,0:T(8,128)(2,1)}, bf16[2,2048,2816]{2,1,0:T(8,128)(2,1)}) custom-call(s32[2]{0:T(128)} %pad_add_fusion.where, bf16[768,2048]{1,0:T(8,128)(2,1)} %get-tuple-element.43.normed_ref.refs_0_, bf16[4,128,2816]{2,1,0:T(8,128)(2,1)} %bitcast.135, ...), custom_call_target="tpu_custom_call" | custom-call | flops 1450000000 | bytes 4350000 | tf_op jit(solution)/shard_map/feed_forward/pallas_call | solution.py:185
  298.9 9.4 %collective-permute-done.28.refs_0_ = bf16[3,704,512]{2,1,0:T(8,128)(2,1)} collective-permute-done((bf16[3,704,512]{2,1,0:T(8,128)(2,1)}, bf16[3,704,512]{2,1,0:T(8,128)(2,1)}, u32[]{:S(2)}, u32[]{:S(2)}) %collective-permute-start.28) | collective-permute-done | bytes 2162720 | tf_op jit(solution)/shard_map/ppermute | solution.py:26
  317.6 10.3 %place.5.refs_4_.down_ref.right_ref = bf16[2816,2048]{1,0:T(8,128)(2,1)} custom-call(s32[2]{0:T(128)} %pad_add_fusion.where, bf16[4,704,512]{2,1,0:T(8,128)(2,1)} %bitcast.134, bf16[3,704,512]{2,1,0:T(8,128)(2,1)} %pad_maximum_fusion.2.refs_7_.refs_0_, bf16[3,704,512]{2,1,0:T(8,128)(2,1)} %collective-permute-done.27.refs_1_, ...), custom_call_target="tpu_custom_call" | custom-call | flops 400000000 | bytes 1200000 | tf_op jit(solution)/shard_map/place/pallas_call | solution.py:130
  327.9 15.8 %block_products.9.rest_0_ = bf16[4,2816,256]{2,1,0:T(8,128)(2,1)} custom-call(s32[1]{0:T(128)} %bitcast.23.where, bf16[768,2816]{1,0:T(8,128)(2,1)} %get-tuple-element.44.refs_1_.refs_4_.refs_0_.left_ref, bf16[768,2816]{1,0:T(8,128)(2,1)} %collective-permute-done.31.refs_1_, bf16[768,2048]{1,0:T(8,128)(2,1)} %bitcast.24.refs_2_.grad_ref.base_ref, ...), custom_call_target="tpu_custom_call" | custom-call | flops 450000000 | bytes 1350000 | tf_op jit(solution)/shard_map/block_products/pallas_call | solution.py:704
  343.8 19.7 %feed_back.1 = (bf16[768,2816]{1,0:T(8,128)(2,1)}, bf16[768,2816]{1,0:T(8,128)(2,1)}) custom-call(s32[1]{0:T(128)} %bitcast.23.where, bf16[768,2048]{1,0:T(8,128)(2,1)} %bitcast.24.refs_2_.grad_ref.base_ref, bf16[2816,2048]{1,0:T(8,128)(2,1)} %place.5.refs_4_.down_ref.right_ref, bf16[768,2816]{1,0:T(8,128)(2,1)} %get-tuple-element.45.gate_ref, ...), custom_call_target="tpu_custom_call" | custom-call | flops 950000000 | bytes 2850000 | tf_op jit(solution)/shard_map/feed_back/pallas_call | solution.py:233
  364.0 10.1 %feed_input.4.refs_4_.refs_0_ = bf16[768,512]{1,0:T(8,128)(2,1)} custom-call(s32[1]{0:T(128)} %bitcast.23.where, bf16[768,2816]{1,0:T(8,128)(2,1)} %get-tuple-element.47.kept_ref.refs_2_, bf16[768,2816]{1,0:T(8,128)(2,1)} %get-tuple-element.48.given_ref, bf16[2,2048,2816]{2,1,0:T(8,128)(2,1)} %get-tuple-element.49.kept_weight.given_weight, ...), custom_call_target="tpu_custom_call" | custom-call | flops 500000000 | bytes 1500000 | tf_op jit(solution)/shard_map/feed_input/pallas_call | solution.py:264
  375.7 9.2 %block_products.10.refs_0_ = bf16[4,256,1408]{2,1,0:T(8,128)(2,1)} custom-call(s32[1]{0:T(128)} %bitcast.25.where, bf16[768,2048]{1,0:T(8,128)(2,1)} %get-tuple-element.43.normed_ref.refs_0_, bf16[768,2048]{1,0:T(8,128)(2,1)} %collective-permute-done.30.refs_1_, bf16[768,2816]{1,0:T(8,128)(2,1)} %get-tuple-element.47.kept_ref.refs_2_, ...), custom_call_target="tpu_custom_call" | custom-call | flops 450000000 | bytes 1350000 | tf_op jit(solution)/shard_map/block_products/pallas_call | solution.py:704
  386.2 10.1 %feed_input.5.rest_0_.refs_1_ = bf16[768,512]{1,0:T(8,128)(2,1)} custom-call(s32[1]{0:T(128)} %bitcast.23.where, bf16[768,2816]{1,0:T(8,128)(2,1)} %get-tuple-element.47.kept_ref.refs_2_, bf16[768,2816]{1,0:T(8,128)(2,1)} %get-tuple-element.48.given_ref, bf16[2,2048,2816]{2,1,0:T(8,128)(2,1)} %get-tuple-element.49.kept_weight.given_weight, ...), custom_call_target="tpu_custom_call" | custom-call | flops 500000000 | bytes 1500000 | tf_op jit(solution)/shard_map/feed_input/pallas_call | solution.py:264
  405.9 10.1 %feed_input.6.rest_0_.refs_4_.refs_2_ = bf16[768,512]{1,0:T(8,128)(2,1)} custom-call(s32[1]{0:T(128)} %bitcast.23.where, bf16[768,2816]{1,0:T(8,128)(2,1)} %get-tuple-element.47.kept_ref.refs_2_, bf16[768,2816]{1,0:T(8,128)(2,1)} %get-tuple-element.48.given_ref, bf16[2,2048,2816]{2,1,0:T(8,128)(2,1)} %get-tuple-element.49.kept_weight.given_weight, ...), custom_call_target="tpu_custom_call" | custom-call | flops 500000000 | bytes 1500000 | tf_op jit(solution)/shard_map/feed_input/pallas_call | solution.py:264
  415.9 9.2 %block_products.11.refs_0_ = bf16[4,256,1408]{2,1,0:T(8,128)(2,1)} custom-call(s32[1]{0:T(128)} %bitcast.25.where, bf16[768,2048]{1,0:T(8,128)(2,1)} %get-tuple-element.43.normed_ref.refs_0_, bf16[768,2048]{1,0:T(8,128)(2,1)} %collective-permute-done.30.refs_1_, bf16[768,2816]{1,0:T(8,128)(2,1)} %get-tuple-element.47.kept_ref.refs_2_, ...), custom_call_target="tpu_custom_call" | custom-call | flops 450000000 | bytes 1350000 | tf_op jit(solution)/shard_map/block_products/pallas_call | solution.py:704
  426.1 10.1 %feed_input.7.refs_5_.refs_3_ = bf16[768,512]{1,0:T(8,128)(2,1)} custom-call(s32[1]{0:T(128)} %bitcast.23.where, bf16[768,2816]{1,0:T(8,128)(2,1)} %get-tuple-element.47.kept_ref.refs_2_, bf16[768,2816]{1,0:T(8,128)(2,1)} %get-tuple-element.48.given_ref, bf16[2,2048,2816]{2,1,0:T(8,128)(2,1)} %get-tuple-element.49.kept_weight.given_weight, ...), custom_call_target="tpu_custom_call" | custom-call | flops 500000000 | bytes 1500000 | tf_op jit(solution)/shard_map/feed_input/pallas_call | solution.py:264
  436.2 12.7 %collective-permute-done.34.refs_1_.refs_4_ = bf16[4,256,1408]{2,1,0:T(8,128)(2,1)} collective-permute-done((bf16[4,256,1408]{2,1,0:T(8,128)(2,1)}, bf16[4,256,1408]{2,1,0:T(8,128)(2,1)}, u32[]{:S(2)}, u32[]{:S(2)}) %collective-permute-start.34) | collective-permute-done | bytes 2883616 | tf_op jit(solution)/shard_map/ppermute | solution.py:26
  448.9 9.7 %block_products.12.refs_0_ = bf16[4,256,1408]{2,1,0:T(8,128)(2,1)} custom-call(s32[1]{0:T(128)} %bitcast.22.where, bf16[768,2048]{1,0:T(8,128)(2,1)} %get-tuple-element.43.normed_ref.refs_0_, bf16[768,2048]{1,0:T(8,128)(2,1)} %collective-permute-done.30.refs_1_, bf16[768,2816]{1,0:T(8,128)(2,1)} %get-tuple-element.47.kept_ref.refs_2_, ...), custom_call_target="tpu_custom_call" | custom-call | flops 450000000 | bytes 1350000 | tf_op jit(solution)/shard_map/block_products/pallas_call | solution.py:704
  461.6 15.4 %product.11.refs_8_.mine_ref = bf16[768,2048]{1,0:T(8,128)(2,1)} custom-call(bf16[768,2816]{1,0:T(8,128)(2,1)} %get-tuple-element.44.refs_1_.refs_4_.refs_0_.left_ref, bf16[2816,2048]{1,0:T(8,128)(2,1)} %place.5.refs_4_.down_ref.right_ref, bf16[4,256,1408]{2,1,0:T(8,128)(2,1)} %tie.36.rest_0_), custom_call_target="tpu_custom_call" | custom-call | flops 300000000 | bytes 900000 | tf_op jit(solution)/shard_map/product/pallas_call | solution.py:299
  477.9 16.9 %collective-permute-done.40.refs_7_ = bf16[768,512]{1,0:T(8,128)(2,1)S(1)} collective-permute-done((bf16[768,512]{1,0:T(8,128)(2,1)}, bf16[768,512]{1,0:T(8,128)(2,1)S(1)}, u32[]{:S(2)}, u32[]{:S(2)}) %collective-permute-start.40) | collective-permute-done | bytes 786464 | tf_op jit(solution)/shard_map/ppermute | solution.py:911
  495.7 12.1 %norm_back.1 = (f32[768,2048]{1,0:T(8,128)}, f32[1,2048]{1,0:T(1,128)}, bf16[768,2048]{1,0:T(8,128)(2,1)}) custom-call(f32[768,2048]{1,0:T(8,128)} %get-tuple-element.42.value_ref.residual_ref, f32[1,2048]{1,0:T(1,128)} %bitcast.152, bf16[768,2048]{1,0:T(8,128)(2,1)} %bitcast.24.refs_2_.grad_ref.base_ref, bf16[768,512]{1,0:T(8,128)(2,1)} %feed_input.4.refs_4_.refs_0_, ...), custom_call_target="tpu_custom_call" | custom-call | flops 600000000 | bytes 1800000 | tf_op jit(solution)/shard_map/norm_back/pallas_call | solution.py:404
  523.4 9.7 %block_products.13.refs_0_ = bf16[4,256,1408]{2,1,0:T(8,128)(2,1)} custom-call(s32[1]{0:T(128)} %bitcast.22.where, bf16[768,2048]{1,0:T(8,128)(2,1)} %get-tuple-element.43.normed_ref.refs_0_, bf16[768,2048]{1,0:T(8,128)(2,1)} %collective-permute-done.30.refs_1_, bf16[768,2816]{1,0:T(8,128)(2,1)} %get-tuple-element.47.kept_ref.refs_2_, ...), custom_call_target="tpu_custom_call" | custom-call | flops 450000000 | bytes 1350000 | tf_op jit(solution)/shard_map/block_products/pallas_call | solution.py:704
  543.9 11.8 %attend_back.3 = (bf16[1024,256]{1,0:T(8,128)(2,1)S(1)}, bf16[4,128,256]{2,1,0:T(8,128)(2,1)S(1)}, bf16[4,128,256]{2,1,0:T(8,128)(2,1)S(1)}) custom-call(s32[2]{0:T(128)S(1)} %copy-done.36, bf16[1024,768]{1,0:T(8,128)(2,1)S(1)} %bitcast.87, bf16[4,256,768]{2,1,0:T(8,128)(2,1)S(1)} %pad_maximum_fusion.4.refs_2_.refs_3_, ...), custom_call_target="tpu_custom_call" | custom-call | flops 800000000 | bytes 2400000 | tf_op jit(solution)/shard_map/attend_back/pallas_call | solution.py:622
  570.7 9.4 %collective-permute-done.37.refs_11_.came_ref = bf16[768,2048]{1,0:T(8,128)(2,1)} collective-permute-done((bf16[768,2048]{1,0:T(8,128)(2,1)}, bf16[768,2048]{1,0:T(8,128)(2,1)}, u32[]{:S(2)}, u32[]{:S(2)}) %collective-permute-start.37) | collective-permute-done | bytes 3145760 | tf_op jit(solution)/shard_map/ppermute | solution.py:922
  582.5 11.8 %attend_back.4 = (bf16[1024,256]{1,0:T(8,128)(2,1)S(1)}, bf16[4,128,256]{2,1,0:T(8,128)(2,1)S(1)}, bf16[4,128,256]{2,1,0:T(8,128)(2,1)S(1)}) custom-call(s32[2]{0:T(128)S(1)} %copy-done.34, bf16[1024,768]{1,0:T(8,128)(2,1)S(1)} %bitcast.88, bf16[4,256,768]{2,1,0:T(8,128)(2,1)S(1)} %pad_maximum_fusion.4.refs_2_.refs_3_, ...), custom_call_target="tpu_custom_call" | custom-call | flops 800000000 | bytes 2400000 | tf_op jit(solution)/shard_map/attend_back/pallas_call | solution.py:622
  614.8 12.0 %attend_back.5 = (bf16[1024,256]{1,0:T(8,128)(2,1)S(1)}, bf16[4,128,256]{2,1,0:T(8,128)(2,1)S(1)}, bf16[4,128,256]{2,1,0:T(8,128)(2,1)S(1)}) custom-call(s32[2]{0:T(128)S(1)} %copy-done.38, bf16[1024,768]{1,0:T(8,128)(2,1)S(1)} %bitcast.89, bf16[4,256,768]{2,1,0:T(8,128)(2,1)S(1)} %pad_maximum_fusion.4.refs_2_.refs_3_, ...), custom_call_target="tpu_custom_call" | custom-call | flops 800000000 | bytes 2400000 | tf_op jit(solution)/shard_map/attend_back/pallas_call | solution.py:622
  630.8 16.4 %collective-permute-done.46.refs_1_ = bf16[2,256,768]{2,1,0:T(8,128)(2,1)S(1)} collective-permute-done((bf16[2,256,768]{2,1,0:T(8,128)(2,1)S(1)}, bf16[2,256,768]{2,1,0:T(8,128)(2,1)S(1)}, u32[]{:S(2)}, u32[]{:S(2)}) %collective-permute-start.46) | collective-permute-done | bytes 786464 | tf_op jit(solution)/shard_map/ppermute | solution.py:26
  724.0 13.5 %norm_back_rows.1 = (f32[768,2048]{1,0:T(8,128)}, f32[1,2048]{1,0:T(1,128)}) custom-call(bf16[768,2048]{1,0:T(8,128)(2,1)} %bitcast.91, f32[768,2048]{1,0:T(8,128)} %fusion.5.term_ref, f32[1,2048]{1,0:T(1,128)} %bitcast.150, f32[768,2048]{1,0:T(8,128)} %get-tuple-element.63.base_ref, bf16[256,2048]{1,0:T(8,128)(2,1)} %product.13.refs_4_.refs_0_, ...), custom_call_target="tpu_custom_call" | custom-call | flops 650000000 | bytes 1950000 | tf_op jit(solution)/shard_map/norm_back_rows/pallas_call | solution.py:452
  (494 shorter events, 385.5 us)
Async XLA Ops:
  7.2 74.8 %all-gather.9.cloned.1.call-start = ((), (), s32[]{:S(2)}) async-start(), calls=%async_computation.12 | async-start | bytes 1310720 | tf_op jit(solution)/shard_map/all_gather | solution.py:816
  14.6 30.1 %collective-permute-start.1 = (bf16[128,1408]{1,0:T(8,128)(2,1)S(1)}, bf16[128,1408]{1,0:T(8,128)(2,1)S(1)}, u32[]{:S(2)}, u32[]{:S(2)}) collective-permute-start(bf16[128,1408]{1,0:T(8,128)(2,1)S(1)} %constant_dynamic-slice_fusion.24), channel_id=1, source_target_pairs={{0,16},{8,24},{16,0},{24,8},{1,17},{9,25},{17,1},{25,9},{2,18},{10... | collective-permute-start | bytes 1081352 | tf_op jit(solution)/shard_map/ppermute | solution.py:809
  14.6 30.1 %collective-permute-start.2 = (bf16[128,1408]{1,0:T(8,128)(2,1)S(1)}, bf16[128,1408]{1,0:T(8,128)(2,1)S(1)}, u32[]{:S(2)}, u32[]{:S(2)}) collective-permute-start(bf16[128,1408]{1,0:T(8,128)(2,1)S(1)} %constant_dynamic-slice_fusion.24), channel_id=1, source_target_pairs={{0,8},{8,16},{16,24},{24,0},{1,9},{9,17},{17,25},{25,1},{2,10},{10... | collective-permute-start | bytes 1081352 | tf_op jit(solution)/shard_map/ppermute | solution.py:809
  45.6 103.8 %all-gather.11.cloned.1.call-start = ((), (), s32[]{:S(2)}) async-start(), calls=%async_computation.13 | async-start | bytes 3604480 | tf_op jit(solution)/shard_map/all_gather | solution.py:816
  47.7 147.6 %all-gather.13.cloned.1.call-start = ((), (), s32[]{:S(2)}) async-start(), calls=%async_computation.14 | async-start | bytes 3604480 | tf_op jit(solution)/shard_map/all_gather | solution.py:816
  50.0 206.5 %all-gather.15.cloned.1.call-start = ((), (), s32[]{:S(2)}) async-start(), calls=%async_computation.15 | async-start | bytes 3604480 | tf_op jit(solution)/shard_map/all_gather | solution.py:816
  82.0 376.7 %reduce-scatter.7.cloned.1.call-start = ((), (), s32[]{:S(2)}) async-start(), calls=%async_computation.6 | async-start | bytes 7208960 | tf_op jit(solution)/shard_map/reduce_scatter | solution.py:750
  104.4 38.2 %collective-permute-start.15 = (bf16[3,256,512]{2,1,0:T(8,128)(2,1)S(1)}, bf16[3,256,512]{2,1,0:T(8,128)(2,1)}, u32[]{:S(2)}, u32[]{:S(2)}) collective-permute-start(bf16[3,256,512]{2,1,0:T(8,128)(2,1)S(1)} %copy-done.53), channel_id=1, source_target_pairs={{0,2},{2,0},{4,6},{6,4},{1,3},{3,1},{5,7},{7,5},{8,10},{10,8},{12,... | collective-permute-start | bytes 2359304 | tf_op jit(solution)/shard_map/ppermute | solution.py:22
  152.6 99.7 %collective-permute-start.21 = (bf16[3,128,2816]{2,1,0:T(8,128)(2,1)}, bf16[3,128,2816]{2,1,0:T(8,128)(2,1)}, u32[]{:S(2)}, u32[]{:S(2)}) collective-permute-start(bf16[3,128,2816]{2,1,0:T(8,128)(2,1)} %pad_maximum_fusion.refs_6_.refs_1_), channel_id=1, source_target_pairs={{0,4},{4,0},{2,6},{6,2},{1,5},{5,1},{3,7},{7,3},{8,12},{12,8},{10,... | collective-permute-start | bytes 6488072 | tf_op jit(solution)/shard_map/ppermute | solution.py:26
  170.2 32.8 %collective-permute-start.18 = (bf16[256,2048]{1,0:T(8,128)(2,1)}, bf16[256,2048]{1,0:T(8,128)(2,1)}, u32[]{:S(2)}, u32[]{:S(2)}) collective-permute-start(bf16[256,2048]{1,0:T(8,128)(2,1)} %product.8.refs_5_.refs_0_), channel_id=1, source_target_pairs={{0,1},{1,0},{2,3},{3,2},{4,5},{5,4},{6,7},{7,6},{8,9},{9,8},{10,11... | collective-permute-start | bytes 3145736 | tf_op jit(solution)/shard_map/ppermute | solution.py:874
  198.6 57.8 %collective-permute-start.25 = (bf16[3,128,2816]{2,1,0:T(8,128)(2,1)}, bf16[3,128,2816]{2,1,0:T(8,128)(2,1)}, u32[]{:S(2)}, u32[]{:S(2)}) collective-permute-start(bf16[3,128,2816]{2,1,0:T(8,128)(2,1)} %pad_maximum_fusion.1.refs_6_), channel_id=1, source_target_pairs={{0,4},{4,0},{2,6},{6,2},{1,5},{5,1},{3,7},{7,3},{8,12},{12,8},{10,... | collective-permute-start | bytes 6488072 | tf_op jit(solution)/shard_map/ppermute | solution.py:26
  230.8 37.9 %collective-permute-start.22 = (bf16[3,128,2816]{2,1,0:T(8,128)(2,1)}, bf16[3,128,2816]{2,1,0:T(8,128)(2,1)}, u32[]{:S(2)}, u32[]{:S(2)}) collective-permute-start(bf16[3,128,2816]{2,1,0:T(8,128)(2,1)} %pad_maximum_fusion.refs_6_.refs_1_), channel_id=1, source_target_pairs={{0,2},{2,0},{4,6},{6,4},{1,3},{3,1},{5,7},{7,5},{8,10},{10,8},{12,... | collective-permute-start | bytes 6488072 | tf_op jit(solution)/shard_map/ppermute | solution.py:22
  234.2 34.5 %collective-permute-start.24 = (bf16[3,128,2816]{2,1,0:T(8,128)(2,1)}, bf16[3,128,2816]{2,1,0:T(8,128)(2,1)}, u32[]{:S(2)}, u32[]{:S(2)}) collective-permute-start(bf16[3,128,2816]{2,1,0:T(8,128)(2,1)} %pad_maximum_fusion.1.refs_6_), channel_id=1, source_target_pairs={{0,2},{2,0},{4,6},{6,4},{1,3},{3,1},{5,7},{7,5},{8,10},{10,8},{12,... | collective-permute-start | bytes 6488072 | tf_op jit(solution)/shard_map/ppermute | solution.py:22
  259.8 48.5 %collective-permute-start.28 = (bf16[3,704,512]{2,1,0:T(8,128)(2,1)}, bf16[3,704,512]{2,1,0:T(8,128)(2,1)}, u32[]{:S(2)}, u32[]{:S(2)}) collective-permute-start(bf16[3,704,512]{2,1,0:T(8,128)(2,1)} %pad_maximum_fusion.2.refs_7_.refs_0_), channel_id=1, source_target_pairs={{0,4},{4,0},{2,6},{6,2},{1,5},{5,1},{3,7},{7,3},{8,12},{12,8},{10,... | collective-permute-start | bytes 6488072 | tf_op jit(solution)/shard_map/ppermute | solution.py:26
  297.6 30.3 %collective-permute-start.31 = (bf16[768,2816]{1,0:T(8,128)(2,1)}, bf16[768,2816]{1,0:T(8,128)(2,1)}, u32[]{:S(2)}, u32[]{:S(2)}) collective-permute-start(bf16[768,2816]{1,0:T(8,128)(2,1)} %get-tuple-element.44.refs_1_.refs_4_.refs_0_.left_ref), channel_id=1, source_target_pairs={{0,2},{2,0},{4,6},{6,4},{1,3},{3,1},{5,7},{7,5},{8,10},{10,8},{12,... | collective-permute-start | bytes 12976136 | tf_op jit(solution)/shard_map/ppermute | solution.py:22
  298.4 29.5 %collective-permute-start.32 = (bf16[768,2048]{1,0:T(8,128)(2,1)}, bf16[768,2048]{1,0:T(8,128)(2,1)}, u32[]{:S(2)}, u32[]{:S(2)}) collective-permute-start(bf16[768,2048]{1,0:T(8,128)(2,1)} %bitcast.24.refs_2_.grad_ref.base_ref), channel_id=1, source_target_pairs={{0,2},{2,0},{4,6},{6,4},{1,3},{3,1},{5,7},{7,5},{8,10},{10,8},{12,... | collective-permute-start | bytes 9437192 | tf_op jit(solution)/shard_map/ppermute | solution.py:22
  343.7 189.4 %reduce-scatter.9.cloned.1.call-start = ((), (), s32[]{:S(2)}) async-start(), calls=%async_computation.7 | async-start | bytes 3604480 | tf_op jit(solution)/shard_map/reduce_scatter | solution.py:750
  384.9 64.0 %collective-permute-start.34 = (bf16[4,256,1408]{2,1,0:T(8,128)(2,1)}, bf16[4,256,1408]{2,1,0:T(8,128)(2,1)}, u32[]{:S(2)}, u32[]{:S(2)}) collective-permute-start(bf16[4,256,1408]{2,1,0:T(8,128)(2,1)} %tie.34.rest_0_), channel_id=1, source_target_pairs={{0,4},{4,0},{2,6},{6,2},{1,5},{5,1},{3,7},{7,3},{8,12},{12,8},{10,... | collective-permute-start | bytes 8650760 | tf_op jit(solution)/shard_map/ppermute | solution.py:26
  458.6 211.4 %reduce-scatter.11.cloned.1.call-start = ((), (), s32[]{:S(2)}) async-start(), calls=%async_computation.8 | async-start | bytes 3604480 | tf_op jit(solution)/shard_map/reduce_scatter | solution.py:750
  458.7 63.1 %collective-permute-start.41 = (bf16[4,256,1408]{2,1,0:T(8,128)(2,1)}, bf16[4,256,1408]{2,1,0:T(8,128)(2,1)S(1)}, u32[]{:S(2)}, u32[]{:S(2)}) collective-permute-start(bf16[4,256,1408]{2,1,0:T(8,128)(2,1)} %tie.35.refs_6_), channel_id=1, source_target_pairs={{0,4},{4,0},{2,6},{6,2},{1,5},{5,1},{3,7},{7,3},{8,12},{12,8},{10,... | collective-permute-start | bytes 8650760 | tf_op jit(solution)/shard_map/ppermute | solution.py:26
  460.1 34.7 %collective-permute-start.40 = (bf16[768,512]{1,0:T(8,128)(2,1)}, bf16[768,512]{1,0:T(8,128)(2,1)S(1)}, u32[]{:S(2)}, u32[]{:S(2)}) collective-permute-start(bf16[768,512]{1,0:T(8,128)(2,1)} %feed_input.7.refs_5_.refs_3_), channel_id=1, source_target_pairs={{0,1},{1,0},{2,3},{3,2},{4,5},{5,4},{6,7},{7,6},{8,9},{9,8},{10,11... | collective-permute-start | bytes 2359304 | tf_op jit(solution)/shard_map/ppermute | solution.py:911
  507.8 55.3 %collective-permute-start.43 = (bf16[768,2048]{1,0:T(8,128)(2,1)}, bf16[768,2048]{1,0:T(8,128)(2,1)}, u32[]{:S(2)}, u32[]{:S(2)}) collective-permute-start(bf16[768,2048]{1,0:T(8,128)(2,1)} %get-tuple-element.50.right_ref.refs_2_), channel_id=1, source_target_pairs={{0,2},{2,0},{4,6},{6,4},{1,3},{3,1},{5,7},{7,5},{8,10},{10,8},{12,... | collective-permute-start | bytes 9437192 | tf_op jit(solution)/shard_map/ppermute | solution.py:22
  510.2 70.0 %collective-permute-start.37 = (bf16[768,2048]{1,0:T(8,128)(2,1)}, bf16[768,2048]{1,0:T(8,128)(2,1)}, u32[]{:S(2)}, u32[]{:S(2)}) collective-permute-start(bf16[768,2048]{1,0:T(8,128)(2,1)} %product.11.refs_8_.mine_ref), channel_id=1, source_target_pairs={{0,1},{1,0},{2,3},{3,2},{4,5},{5,4},{6,7},{7,6},{8,9},{9,8},{10,11... | collective-permute-start | bytes 9437192 | tf_op jit(solution)/shard_map/ppermute | solution.py:922
  533.2 177.3 %reduce-scatter.13.cloned.1.call-start = ((), (), s32[]{:S(2)}) async-start(), calls=%async_computation.9 | async-start | bytes 1310720 | tf_op jit(solution)/shard_map/reduce_scatter | solution.py:750
  563.0 39.7 %collective-permute-start.45 = (bf16[256,2048]{1,0:T(8,128)(2,1)}, bf16[256,2048]{1,0:T(8,128)(2,1)}, u32[]{:S(2)}, u32[]{:S(2)}) collective-permute-start(bf16[256,2048]{1,0:T(8,128)(2,1)} %product.13.refs_4_.refs_0_), channel_id=1, source_target_pairs={{0,1},{1,0},{2,3},{3,2},{4,5},{5,4},{6,7},{7,6},{8,9},{9,8},{10,11... | collective-permute-start | bytes 3145736 | tf_op jit(solution)/shard_map/ppermute | solution.py:942
  569.3 38.5 %collective-permute-start.44 = (bf16[4,512,256]{2,1,0:T(8,128)(2,1)}, bf16[4,512,256]{2,1,0:T(8,128)(2,1)}, u32[]{:S(2)}, u32[]{:S(2)}) collective-permute-start(bf16[4,512,256]{2,1,0:T(8,128)(2,1)} %tie.38.refs_10_), channel_id=1, source_target_pairs={{0,4},{4,0},{2,6},{6,2},{1,5},{5,1},{3,7},{7,3},{8,12},{12,8},{10,... | collective-permute-start | bytes 3145736 | tf_op jit(solution)/shard_map/ppermute | solution.py:26
  653.3 49.8 %collective-permute-start.38 = (bf16[768,2048]{1,0:T(8,128)(2,1)}, bf16[768,2048]{1,0:T(8,128)(2,1)}, u32[]{:S(2)}, u32[]{:S(2)}) collective-permute-start(bf16[768,2048]{1,0:T(8,128)(2,1)} %copy-done.42), channel_id=1, source_target_pairs={{0,2},{2,0},{4,6},{6,4},{1,3},{3,1},{5,7},{7,5},{8,10},{10,8},{12,... | collective-permute-start | bytes 9437192 | tf_op jit(solution)/shard_map/ppermute | solution.py:22
  670.0 93.9 %reduce-scatter.15.cloned.1.call-start = ((), (), s32[]{:S(2)}) async-start(), calls=%async_computation.10 | async-start | bytes 2621440 | tf_op jit(solution)/shard_map/reduce_scatter | solution.py:750
  689.2 54.4 %collective-permute-start.63 = (bf16[2816,256]{1,0:T(8,128)(2,1)}, bf16[2816,256]{1,0:T(8,128)(2,1)}, u32[]{:S(2)}, u32[]{:S(2)}) collective-permute-start(bf16[2816,256]{1,0:T(8,128)(2,1)} %tie.44), channel_id=1, source_target_pairs={{0,4},{4,0},{2,6},{6,2},{1,5},{5,1},{3,7},{7,3},{8,12},{12,8},{10,... | collective-permute-start | bytes 4325384 | tf_op jit(solution)/shard_map/ppermute | solution.py:26
  691.0 33.0 %collective-permute-start.52 = (bf16[256,2048]{1,0:T(8,128)(2,1)}, bf16[256,2048]{1,0:T(8,128)(2,1)}, u32[]{:S(2)}, u32[]{:S(2)}) collective-permute-start(bf16[256,2048]{1,0:T(8,128)(2,1)} %product.15.refs_4_.refs_2_), channel_id=1, source_target_pairs={{0,1},{1,0},{2,3},{3,2},{4,5},{5,4},{6,7},{7,6},{8,9},{9,8},{10,11... | collective-permute-start | bytes 3145736 | tf_op jit(solution)/shard_map/ppermute | solution.py:942
  698.2 41.1 %collective-permute-start.61 = (bf16[256,1408]{1,0:T(8,128)(2,1)}, bf16[256,1408]{1,0:T(8,128)(2,1)}, u32[]{:S(2)}, u32[]{:S(2)}) collective-permute-start(bf16[256,1408]{1,0:T(8,128)(2,1)} %tie.43), channel_id=1, source_target_pairs={{0,4},{4,0},{2,6},{6,2},{1,5},{5,1},{3,7},{7,3},{8,12},{12,8},{10,... | collective-permute-start | bytes 2162696 | tf_op jit(solution)/shard_map/ppermute | solution.py:26
  710.5 77.6 %reduce-scatter.17.cloned.1.call-start = ((), (), s32[]{:S(2)}) async-start(), calls=%async_computation.11 | async-start | bytes 655360 | tf_op jit(solution)/shard_map/reduce_scatter | solution.py:750
  (144 other events, 1813.2 us)
Sparse Core Ops, SparseCore 0:
  45.7 29.7 all-gather.8
  77.0 58.7 all-gather.10
  137.4 57.8 all-gather.12
  196.7 57.7 all-gather.14
  343.9 100.3 reduce-scatter.6
  458.8 54.9 reduce-scatter.8
  533.3 55.7 reduce-scatter.10
  670.1 27.5 reduce-scatter.12
  710.6 46.9 reduce-scatter.14
  770.9 17.1 reduce-scatter.16

commit v3 on v2

--- a/solution.py
+++ b/solution.py
@@ -41,7 +41,7 @@
 
 
 def taking(microseconds):
-    return pl.CostEstimate(flops=int(microseconds * 0.05e9), bytes_accessed=int(microseconds * 0.15e6), transcendentals=0)
+    return pl.CostEstimate(flops=int(microseconds * 1e9), bytes_accessed=int(microseconds * 0.15e6), transcendentals=0)
 
 
 def tie(value, *after):
@@ -246,7 +246,7 @@
             out_specs=(token_spec, token_spec),
         ),
         compiler_params=ROOMY,
-        cost_estimate=taking(19),
+        cost_estimate=taking(5.7),
         name="feed_back",
     )(low.reshape(1), grad_out, down_full, gate_factor, up_factor, *after)
 
@@ -303,7 +303,7 @@
         in_specs=[pl.BlockSpec(left.shape, lambda j: (0, 0)), right_spec] + [UNREAD] * len(after),
         out_specs=pl.BlockSpec((rows, tile), lambda j: (0, j)),
         compiler_params=ROOMY,
-        cost_estimate=taking(6),
+        cost_estimate=taking(0.6),
         name="product",
     )(left, right, *after)
 
@@ -338,7 +338,7 @@
         + [UNREAD] * len(after),
         out_specs=(row_spec, row_spec),
         compiler_params=ROOMY,
-        cost_estimate=taking(9),
+        cost_estimate=taking(90),
         name="add_and_norm",
     )(activations, gain[None, :], *mine, *came, *after)
 
@@ -359,7 +359,7 @@
         in_specs=[row_spec] * 3 + [UNREAD] * len(after),
         out_specs=row_spec,
         compiler_params=ROOMY,
-        cost_estimate=taking(5),
+        cost_estimate=taking(0.15),
         name="add_three",
     )(residual, mine, came, *after)
 
@@ -644,7 +644,7 @@
             ],
         ),
         compiler_params=pltpu.CompilerParams(vmem_limit_bytes=48 * 2**20),
-        cost_estimate=taking(16),
+        cost_estimate=taking(160),
         name="attend_back",
     )(info, query_t, keyval, keyval, start_row, delta_t, mixed_t, log_sums, cosine, sine, *after)
 
@@ -750,6 +750,16 @@
     return lax.psum_scatter(total, "shard", scatter_dimension=0, tiled=True)[0]
 
 
+def directly_over_shard(total, me):
+    shards = total.shape[0]
+    result = lax.dynamic_index_in_dim(total, me, 0, False).astype(f32)
+    for k in range(1, shards):
+        block = lax.dynamic_index_in_dim(total, (me + k) % shards, 0, False)
+        came = lax.ppermute(block, "shard", [(i, (i + k) % shards) for i in range(shards)])
+        result = result + came.astype(f32)
+    return result.astype(bf16)
+
+
 class Reduced:
     def __init__(self, lefts, rights, high, shards, left_rows, right_rows, left_cut, half=None):
         width = (lefts if left_cut else rights)[0].shape[1]
@@ -769,8 +779,7 @@
         return over_shard(self.tied)
 
 
-def halves(high, own, axis):
-    came = high_swap(own)
+def halves(high, own, axis, came):
     return jnp.concatenate([pick(high, own, came), pick(high, came, own)], axis)
 
 
@@ -886,16 +895,17 @@
         normed_two, (gate_weight, up_weight), (gate_pieces, up_pieces), *where
     )
 
-    hidden_pair = (hidden, low_swap(hidden))
+    down_high = high_swap(down_own)
+    hidden = tie(hidden, down_high)
+    hidden_came = low_swap(hidden)
+    hidden_pair = (hidden, hidden_came)
     cotangent_pair = (grad_out, low_swap(grad_out))
     products = block_products if model_width // shards % 256 == 0 else plain_products
-    down_pieces = spread([down_own], hidden)
-    down_full = place(down_weight, down_pieces, *where, False, [hidden])
-    down_products = products(
-        hidden_pair, cotangent_pair, None, low, shards, 0, 0, False, None, [down_full]
-    )
+    down_products = products(hidden_pair, cotangent_pair, None, low, shards, 0, 0, False)
     down_sum = over_shard(down_products)
-    kept, given = feed_back(grad_out, down_full, gate_factor, up_factor, low, [down_products])
+    down_pieces = [down_own], [low_swap(down_own)], [down_high], [low_swap(down_high)]
+    down_full = place(down_weight, down_pieces, *where, False, [down_products])
+    kept, given = feed_back(grad_out, down_full, gate_factor, up_factor, low)
 
     normed_pair = (normed_two, low_swap(normed_two))
     delta_pair = (kept, low_swap(given))
@@ -913,13 +923,13 @@
         if i % 2 == 0:
             gate_up[i // 2].send(last, [gate_up[0].came] if i else [])
             last = [gate_up[0].sent] if i == 0 else last
-    gate_up_first = gate_up[0].add([mine[-1], gate_up[1].sent], [down_sum])
-    ffn_mine = product(hidden, down_full, 1, 0, TILE, [gate_up[0].tied])
+    ffn_mine = product(hidden, down_full, 1, 0, TILE, [mine[-1]])
+    gate_up_first = gate_up[0].add([ffn_mine, gate_up[1].sent, came[2]], [down_sum])
     residual_delta, ffn_gain_term, residual_round = norm_back(
-        residual, mine, came, gain_two, grad_out, [ffn_mine]
+        residual, mine, came, gain_two, grad_out, [ffn_mine, gate_up[0].tied]
     )
-    delta_t = product(out_weight, residual_round, 1, 1, TILE)
     ffn_came = lax.ppermute(ffn_mine, "tp", SWAP_TP)
+    delta_t = product(out_weight, residual_round, 1, 1, TILE, [])
 
     half_rows = query_cols // 2
     mixed_kept = lax.dynamic_slice_in_dim(mixed_t, low * half_rows, half_rows, 0)
@@ -928,9 +938,8 @@
     residual_pair = (residual_round, low_swap(residual_round))
     output = Reduced(mixed_pair, residual_pair, high, shards, 1, 0, False)
 
-    gate_up_second = gate_up[1].add([delta_t], [gate_up_first])
     query_deltas, part_sums, mine, came = [], [], [], []
-    last = [gate_up[1].tied]
+    last = []
     for s in range(seq_here):
         query_delta, key_part, value_part = attend_back(
             infos[s], query_t, keyval, start_here[s : s + 1], delta_t, mixed[s], log_sums[s],
@@ -938,16 +947,26 @@
         )
         query_deltas.append(query_delta)
         part_sums.append(jnp.concatenate([key_part, value_part], 1))
-        mine.append(product(query_delta, qkv_weight[:, :query_cols], 0, 1, 512, came[s - 1 : s]))
+        waits = []
+        if s == 0:
+            waits = []
+        if s == 1:
+            waits = []
+        if s == 2:
+            waits = []
+        mine.append(product(query_delta, qkv_weight[:, :query_cols], 0, 1, 512, waits))
         came.append(lax.ppermute(mine[s], "tp", SWAP_TP))
         last = [mine[s]]
         if s == 0:
             output.send(last, [gate_up[1].came])
-            last = [output.sent, ffn_came]
+            gate_up_second = gate_up[1].add([output.sent], [])
+            last = [output.sent, gate_up[1].tied, ffn_came]
         if s == 1:
             output.total = output.products(*output.sides, output.came, high, *output.rest, last)
-            last = [output.total]
-    down_came = high_swap(tie(down_sum, output.came))
+            output_tied = tie(output.total, gate_up_second)
+            down_came = high_swap(tie(down_sum, output.came))
+            first_came = high_swap(tie(gate_up_first, down_came))
+            last = [output.total, came[0], down_came, output_tied]
 
     part_sum = jnp.concatenate(part_sums, 2).reshape(2, 2, 2 * kv_width, tokens)
     sent = lax.dynamic_index_in_dim(part_sum, 1 - high, 0, False)
@@ -962,11 +981,10 @@
         pair = (kept.T, low_swap(given).T)
         return block_products(normed_pair_one, pair, None, None, shards, 0, 0, True, None, after)
 
-    output_tied = tie(output.total, gate_up_second)
-    query_products = products_of(jnp.concatenate(query_deltas, 1), [mine[-1], output_tied])
     output_sum = over_shard(output_tied)
-    query_tied = tie(query_products, output_sum)
-    query_sum = over_shard(query_tied)
+    query_products = products_of(jnp.concatenate(query_deltas, 1), [mine[-1], came[1]] + [output_sum])
+    part_came = tie(part_came, query_products)
+    query_sum = over_shard(query_products)
 
     kept = lax.dynamic_index_in_dim(part_sum, high, 0, False)
     kept = kept.astype(f32) + part_came.astype(f32)
@@ -981,15 +999,17 @@
     keyval_both = jnp.concatenate(
         [pick(tp, keyval_delta, keyval_came), pick(tp, keyval_came, keyval_delta)], 0
     )
-    keyval_products = products_of(keyval_delta, [query_tied])
+    keyval_products = products_of(keyval_delta, [query_products])
     keyval_term = dot(keyval_both, keyval_weight, 0, 1)
 
-    block_out = add_three(residual, ffn_mine, ffn_came, [keyval_products])
+    input_grad, attn_gain_term = norm_back_rows(
+        acts, mine, came, keyval_term, gain_one, residual_delta, [keyval_products]
+    )
+    block_out = add_three(residual, ffn_mine, ffn_came, [])
     block_out = block_out.reshape(activations.shape)
-    input_grad, attn_gain_term = norm_back_rows(
-        acts, mine, came, keyval_term, gain_one, residual_delta, [block_out]
-    )
-    keyval_sum = over_shard(tie(keyval_products, query_sum))
+    keyval_sum = directly_over_shard(keyval_products, me) if shards <= 4 else over_shard(keyval_products)
+
+    second_came = high_swap(tie(gate_up_second, part_came))
 
     def two_sides(value):
         other = low_swap(value)
@@ -997,11 +1017,11 @@
 
     down_sum = (down_sum.astype(f32) + tie(down_came, keyval_products).astype(f32)).astype(bf16)
     down_grad = jnp.concatenate(two_sides(down_sum), 1)
-    first_gate, first_up = two_sides(halves(high, tie(gate_up_first, part_came), 0))
-    second_gate, second_up = two_sides(halves(high, tie(gate_up_second, part_came), 0))
+    first_gate, first_up = two_sides(halves(high, gate_up_first, 0, first_came))
+    second_gate, second_up = two_sides(halves(high, gate_up_second, 0, second_came))
     gate_grad = jnp.concatenate([first_gate, second_gate], 1)
     up_grad = jnp.concatenate([first_up, second_up], 1)
-    output_grad = jnp.concatenate(two_sides(halves(high, output_sum, 1)), 0)
+    output_grad = jnp.concatenate(two_sides(halves(high, output_sum, 1, high_swap(output_sum))), 0)
 
     def high_total(value):
         return (value.astype(f32) + high_swap(value).astype(f32)).astype(bf16)

time: 811 us -> 812 us (level)
  waiting for transfers between devices: 222 us -> 202 us
  starting transfers between devices: 76.8 us -> 93.1 us
  local copies, waits for them, and re-layouts: 66.9 us -> 75.6 us
    ppermute x6, waiting for transfers between devices: 42.2 us -> 2.65 us  [body(): came.append(lax.ppermute(mine[s], 'tp', SWAP_TP))]
    all_gather x4, waiting for transfers between devices: 6.97 us -> 35.7 us  [later(): lax.all_gather(tie(quarter(weight, ctx), *after), 'shard', axis=0, tiled=...]
    ppermute x4, waiting for transfers between devices: 25 us -> 0.01 us  [body(): came.append(lax.ppermute(mine[i], 'tp', SWAP_TP))]
    ppermute x19, waiting for transfers between devices: 94.4 us -> 72.1 us  [high_swap(): return lax.ppermute(value, 'ctx', SWAP_HIGH)]
    ppermute x0 -> x3, waiting for transfers between devices: none -> 21.2 us  [directly_over_shard(): lax.ppermute(block, 'shard', [(i, (i + k) % shards) for i in range(shards)])]
    ppermute x19, starting transfers between devices: 23.7 us -> 38.2 us  [high_swap(): return lax.ppermute(value, 'ctx', SWAP_HIGH)]
    reduce_scatter x6 -> x5, waiting for transfers between devices: 2.86 us -> 14.9 us  [over_shard(): return lax.psum_scatter(total, 'shard', scatter_dimension=0, tiled=True)[0]]
    ppermute x1, waiting for transfers between devices: 9.45 us -> 0.46 us  [body(): ffn_came = lax.ppermute(ffn_mine, 'tp', SWAP_TP)]
  transfers between devices with their start and end apart: 80 -> 82, of which waited for: 28 -> 24; matrix products, arithmetic and copies ran while one was open for 13% -> 13% of each run, Pallas kernels for 42% -> 44%
where the time goes in v3:
time: 812 us; the launch traced here: 802 us
  Pallas kernels  350 us (43%)
  waiting for transfers between devices  202 us (25%)
  starting transfers between devices  93.1 us (11%)
  local copies, waits for them, and re-layouts  75.6 us (9%)
  other arithmetic  57.7 us (7%)
  between operations  15.4 us (2%)
  matrix products  8.85 us (1%)
    pallas_call x9, Pallas kernels, block_products(): pl.pallas_call(kernel, out_shape=jax.ShapeDtypeStruct(out_shape, bf16), g...  78 us
    ppermute x19, waiting for transfers between devices, high_swap(): return lax.ppermute(value, 'ctx', SWAP_HIGH)  72.1 us
    pallas_call x8, Pallas kernels, product(): pl.pallas_call(kernel, out_shape=jax.ShapeDtypeStruct((rows, width), bf16...  52.9 us
    pallas_call x4, Pallas kernels, feed_input(): pl.pallas_call(kernel, out_shape=jax.ShapeDtypeStruct((tokens, model_widt...  40.2 us
    unnamed x207, local copies, waits for them, and re-layouts  38.6 us
    ppermute x19, starting transfers between devices, high_swap(): return lax.ppermute(value, 'ctx', SWAP_HIGH)  38.2 us
    pallas_call x3, Pallas kernels, attend_back(): pl.pallas_call(lambda *refs: attend_back_kernel(group, *refs), out_shape=...  36.1 us
    all_gather x4, waiting for transfers between devices, later(): lax.all_gather(tie(quarter(weight, ctx), *after), 'shard', axis=0, tiled=...  35.7 us
  transfers between devices with their start and end apart: 82, of which 24 were waited for; matrix products, arithmetic and copies ran while one was open for 13% of the time, Pallas kernels for 44%

profile of v3, /device:TPU:1, one launch (start us, length us, event | category | flops | bytes accessed | tf_op | source)
XLA Modules:
  0.0 802.1 jit_solution(14155722060506652038)
XLA Ops:
  21.7 23.0 %collective-permute-done.1 = bf16[128,1408]{1,0:T(8,128)(2,1)S(1)} collective-permute-done((bf16[128,1408]{1,0:T(8,128)(2,1)S(1)}, bf16[128,1408]{1,0:T(8,128)(2,1)S(1)}, u32[]{:S(2)}, u32[]{:S(2)}) %collective-permute-start.1) | collective-permute-done | bytes 360480 | tf_op jit(solution)/shard_map/ppermute | solution.py:818
  111.1 12.0 %collective-permute-done.13.refs_1_.refs_2_ = bf16[3,256,512]{2,1,0:T(8,128)(2,1)S(1)} collective-permute-done((bf16[3,256,512]{2,1,0:T(8,128)(2,1)}, bf16[3,256,512]{2,1,0:T(8,128)(2,1)S(1)}, u32[]{:S(2)}, u32[]{:S(2)}) %collective-permute-start.13) | collective-permute-done | bytes 786464 | tf_op jit(solution)/shard_map/ppermute | solution.py:26
  133.1 9.5 %collective-permute-done.14.refs_1_ = bf16[2,256,768]{2,1,0:T(8,128)(2,1)S(1)} collective-permute-done((bf16[2,256,768]{2,1,0:T(8,128)(2,1)}, bf16[2,256,768]{2,1,0:T(8,128)(2,1)S(1)}, u32[]{:S(2)}, u32[]{:S(2)}) %collective-permute-start.14) | collective-permute-done | bytes 786464 | tf_op jit(solution)/shard_map/ppermute | solution.py:26
  155.4 10.0 %attend.3 = (bf16[1024,256]{1,0:T(8,128)(2,1)S(1)}, f32[2,8,256]{2,1,0:T(8,128)S(1)}) custom-call(s32[2]{0:T(128)S(1)} %get-tuple-element.142.refs_0_, bf16[1024,768]{1,0:T(8,128)(2,1)S(1)} %bitcast.95, bf16[4,256,768]{2,1,0:T(8,128)(2,1)S(1)} %copy-done.14, bf16[4,256,768]{2,1,0:T(8,128)(2,1)S(1)} %copy-done.14, s32[1,256]{1,0:T(1,128)S(1)} %get-tuple-element.137.refs_4_, ...), custom_call_target="tpu_custom_call" | custom-call | flops 14000000000 | bytes 2100000 | tf_op jit(solution)/shard_map/attend/pallas_call | solution.py:522
  174.1 10.0 %attend.4 = (bf16[1024,256]{1,0:T(8,128)(2,1)S(1)}, f32[2,8,256]{2,1,0:T(8,128)S(1)}) custom-call(s32[2]{0:T(128)S(1)} %get-tuple-element.143.refs_0_, bf16[1024,768]{1,0:T(8,128)(2,1)S(1)} %bitcast.96, bf16[4,256,768]{2,1,0:T(8,128)(2,1)S(1)} %copy-done.14, bf16[4,256,768]{2,1,0:T(8,128)(2,1)S(1)} %copy-done.14, s32[1,256]{1,0:T(1,128)S(1)} %get-tuple-element.138.refs_4_, ...), custom_call_target="tpu_custom_call" | custom-call | flops 14000000000 | bytes 2100000 | tf_op jit(solution)/shard_map/attend/pallas_call | solution.py:522
  203.8 10.0 %attend.5 = (bf16[1024,256]{1,0:T(8,128)(2,1)S(1)}, f32[2,8,256]{2,1,0:T(8,128)S(1)}) custom-call(s32[2]{0:T(128)S(1)} %pad_add_fusion.3.refs_0_, bf16[1024,768]{1,0:T(8,128)(2,1)S(1)} %bitcast.97, bf16[4,256,768]{2,1,0:T(8,128)(2,1)S(1)} %copy-done.15, bf16[4,256,768]{2,1,0:T(8,128)(2,1)S(1)} %copy-done.15, s32[1,256]{1,0:T(1,128)S(1)} %get-tuple-element.136.refs_4_, ...), custom_call_target="tpu_custom_call" | custom-call | flops 14000000000 | bytes 2100000 | tf_op jit(solution)/shard_map/attend/pallas_call | solution.py:522
  224.0 30.6 %all-gather.15.cloned.1.call-done = bf16[2816,512]{1,0:T(8,128)(2,1)} async-done(((bf16[704,512]{1,0:T(8,128)(2,1)}), bf16[2816,512]{1,0:T(8,128)(2,1)}) %all-gather.15.cloned.1.call-update) | async-done | bytes 2883600 | tf_op jit(solution)/shard_map/all_gather | solution.py:825
  259.0 8.6 %add_and_norm.1 = (f32[768,2048]{1,0:T(8,128)}, bf16[768,2048]{1,0:T(8,128)(2,1)}) custom-call(bf16[768,2048]{1,0:T(8,128)(2,1)} %bitcast.104, f32[1,2048]{1,0:T(1,128)} %bitcast.160, bf16[256,2048]{1,0:T(8,128)(2,1)} %product.8.refs_5_.refs_0_, bf16[256,2048]{1,0:T(8,128)(2,1)} %product.9.refs_1_.refs_5_, bf16[256,2048]{1,0:T(8,128)(2,1)} %product.10.refs_1_.refs_2_, ...), custom_call_target="tpu_custom_call" | custom-call | flops 89999998976 | bytes 13500000 | tf_op jit(solution)/shard_map/add_and_norm/pallas_call | solution.py:329
  268.9 28.7 %feed_forward.1 = (bf16[768,2816]{1,0:T(8,128)(2,1)}, bf16[768,2816]{1,0:T(8,128)(2,1)}, bf16[768,2816]{1,0:T(8,128)(2,1)}, bf16[2,2048,2816]{2,1,0:T(8,128)(2,1)}) custom-call(s32[2]{0:T(128)} %pad_add_fusion.where, bf16[768,2048]{1,0:T(8,128)(2,1)} %get-tuple-element.43.normed_ref.refs_0_, bf16[4,128,2816]{2,1,0:T(8,128)(2,1)} %bitcast.155, ...), custom_call_target="tpu_custom_call" | custom-call | flops 28999999488 | bytes 4350000 | tf_op jit(solution)/shard_map/feed_forward/pallas_call | solution.py:185
  307.8 16.3 %collective-permute-done.31.refs_3_ = bf16[768,2048]{1,0:T(8,128)(2,1)S(1)} collective-permute-done((bf16[768,2048]{1,0:T(8,128)(2,1)}, bf16[768,2048]{1,0:T(8,128)(2,1)S(1)}, u32[]{:S(2)}, u32[]{:S(2)}) %collective-permute-start.31) | collective-permute-done | bytes 3145760 | tf_op jit(solution)/shard_map/ppermute | solution.py:22
  327.9 15.8 %block_products.9.refs_4_ = bf16[4,2816,256]{2,1,0:T(8,128)(2,1)} custom-call(s32[1]{0:T(128)} %bitcast.22.where, bf16[768,2816]{1,0:T(8,128)(2,1)} %tie.32.refs_0_.left_ref, bf16[768,2816]{1,0:T(8,128)(2,1)} %copy-done.86, bf16[768,2048]{1,0:T(8,128)(2,1)} %bitcast.140, bf16[768,2048]{1,0:T(8,128)(2,1)} %copy-done.87), custom_call_target="tpu_custom_call" | custom-call | flops 8999999488 | bytes 1350000 | tf_op jit(solution)/shard_map/block_products/pallas_call | solution.py:704
  343.8 10.6 %place.5.down_ref.right_ref = bf16[2816,2048]{1,0:T(8,128)(2,1)} custom-call(s32[2]{0:T(128)} %pad_add_fusion.where, bf16[4,704,512]{2,1,0:T(8,128)(2,1)} %bitcast.157, bf16[3,704,512]{2,1,0:T(8,128)(2,1)} %copy-done.72, bf16[3,704,512]{2,1,0:T(8,128)(2,1)} %collective-permute-done.28.refs_1_, bf16[3,704,512]{2,1,0:T(8,128)(2,1)} %collective-permute-done.27.refs_1_.refs_2_, ...), custom_call_target="tpu_custom_call" | custom-call | flops 8000000000 | bytes 1200000 | tf_op jit(solution)/shard_map/place/pallas_call | solution.py:130
  354.4 19.2 %feed_back.1 = (bf16[768,2816]{1,0:T(8,128)(2,1)}, bf16[768,2816]{1,0:T(8,128)(2,1)}) custom-call(s32[1]{0:T(128)} %bitcast.22.where, bf16[768,2048]{1,0:T(8,128)(2,1)} %bitcast.141, bf16[2816,2048]{1,0:T(8,128)(2,1)} %place.5.down_ref.right_ref, bf16[768,2816]{1,0:T(8,128)(2,1)} %get-tuple-element.45.gate_ref, bf16[768,2816]{1,0:T(8,128)(2,1)} %get-tuple-element.46.up_ref), custom_call_target="tpu_custom_call" | custom-call | flops 5699999744 | bytes 855000 | tf_op jit(solution)/shard_map/feed_back/pallas_call | solution.py:233
  381.7 10.0 %feed_input.4.refs_4_.refs_0_ = bf16[768,512]{1,0:T(8,128)(2,1)} custom-call(s32[1]{0:T(128)} %bitcast.22.where, bf16[768,2816]{1,0:T(8,128)(2,1)} %get-tuple-element.47.kept_ref.refs_2_, bf16[768,2816]{1,0:T(8,128)(2,1)} %get-tuple-element.48.given_ref, bf16[2,2048,2816]{2,1,0:T(8,128)(2,1)} %get-tuple-element.49.kept_weight.given_weight, ...), custom_call_target="tpu_custom_call" | custom-call | flops 10000000000 | bytes 1500000 | tf_op jit(solution)/shard_map/feed_input/pallas_call | solution.py:264
  392.9 9.2 %block_products.10.refs_0_ = bf16[4,256,1408]{2,1,0:T(8,128)(2,1)} custom-call(s32[1]{0:T(128)} %bitcast.24.where, bf16[768,2048]{1,0:T(8,128)(2,1)} %get-tuple-element.43.normed_ref.refs_0_, bf16[768,2048]{1,0:T(8,128)(2,1)} %collective-permute-done.32.refs_1_, bf16[768,2816]{1,0:T(8,128)(2,1)} %get-tuple-element.47.kept_ref.refs_2_, ...), custom_call_target="tpu_custom_call" | custom-call | flops 8999999488 | bytes 1350000 | tf_op jit(solution)/shard_map/block_products/pallas_call | solution.py:704
  403.3 10.1 %feed_input.5.rest_0_.refs_1_ = bf16[768,512]{1,0:T(8,128)(2,1)} custom-call(s32[1]{0:T(128)} %bitcast.22.where, bf16[768,2816]{1,0:T(8,128)(2,1)} %get-tuple-element.47.kept_ref.refs_2_, bf16[768,2816]{1,0:T(8,128)(2,1)} %get-tuple-element.48.given_ref, bf16[2,2048,2816]{2,1,0:T(8,128)(2,1)} %get-tuple-element.49.kept_weight.given_weight, ...), custom_call_target="tpu_custom_call" | custom-call | flops 10000000000 | bytes 1500000 | tf_op jit(solution)/shard_map/feed_input/pallas_call | solution.py:264
  414.6 10.0 %feed_input.6.rest_0_.refs_4_.refs_2_ = bf16[768,512]{1,0:T(8,128)(2,1)} custom-call(s32[1]{0:T(128)} %bitcast.22.where, bf16[768,2816]{1,0:T(8,128)(2,1)} %get-tuple-element.47.kept_ref.refs_2_, bf16[768,2816]{1,0:T(8,128)(2,1)} %get-tuple-element.48.given_ref, bf16[2,2048,2816]{2,1,0:T(8,128)(2,1)} %get-tuple-element.49.kept_weight.given_weight, ...), custom_call_target="tpu_custom_call" | custom-call | flops 10000000000 | bytes 1500000 | tf_op jit(solution)/shard_map/feed_input/pallas_call | solution.py:264
  425.8 9.1 %block_products.11.refs_0_ = bf16[4,256,1408]{2,1,0:T(8,128)(2,1)} custom-call(s32[1]{0:T(128)} %bitcast.24.where, bf16[768,2048]{1,0:T(8,128)(2,1)} %get-tuple-element.43.normed_ref.refs_0_, bf16[768,2048]{1,0:T(8,128)(2,1)} %collective-permute-done.32.refs_1_, bf16[768,2816]{1,0:T(8,128)(2,1)} %get-tuple-element.47.kept_ref.refs_2_, ...), custom_call_target="tpu_custom_call" | custom-call | flops 8999999488 | bytes 1350000 | tf_op jit(solution)/shard_map/block_products/pallas_call | solution.py:704
  435.8 10.1 %feed_input.7.rest_0_.refs_3_ = bf16[768,512]{1,0:T(8,128)(2,1)} custom-call(s32[1]{0:T(128)} %bitcast.22.where, bf16[768,2816]{1,0:T(8,128)(2,1)} %get-tuple-element.47.kept_ref.refs_2_, bf16[768,2816]{1,0:T(8,128)(2,1)} %get-tuple-element.48.given_ref, bf16[2,2048,2816]{2,1,0:T(8,128)(2,1)} %get-tuple-element.49.kept_weight.given_weight, ...), custom_call_target="tpu_custom_call" | custom-call | flops 10000000000 | bytes 1500000 | tf_op jit(solution)/shard_map/feed_input/pallas_call | solution.py:264
  446.3 14.5 %product.11.mine_ref.refs_5_.refs_8_ = bf16[768,2048]{1,0:T(8,128)(2,1)} custom-call(bf16[768,2816]{1,0:T(8,128)(2,1)} %tie.32.refs_0_.left_ref, bf16[2816,2048]{1,0:T(8,128)(2,1)} %place.5.down_ref.right_ref, bf16[768,512]{1,0:T(8,128)(2,1)} %feed_input.7.rest_0_.refs_3_), custom_call_target="tpu_custom_call" | custom-call | flops 600000000 | bytes 90000 | tf_op jit(solution)/shard_map/product/pallas_call | solution.py:299
  468.2 9.9 %block_products.12.refs_0_ = bf16[4,256,1408]{2,1,0:T(8,128)(2,1)} custom-call(s32[1]{0:T(128)} %bitcast.26.where, bf16[768,2048]{1,0:T(8,128)(2,1)} %get-tuple-element.43.normed_ref.refs_0_, bf16[768,2048]{1,0:T(8,128)(2,1)} %collective-permute-done.32.refs_1_, bf16[768,2816]{1,0:T(8,128)(2,1)} %get-tuple-element.47.kept_ref.refs_2_, ...), custom_call_target="tpu_custom_call" | custom-call | flops 8999999488 | bytes 1350000 | tf_op jit(solution)/shard_map/block_products/pallas_call | solution.py:704
  479.0 12.1 %norm_back.1 = (f32[768,2048]{1,0:T(8,128)}, f32[1,2048]{1,0:T(1,128)}, bf16[768,2048]{1,0:T(8,128)(2,1)}) custom-call(f32[768,2048]{1,0:T(8,128)} %get-tuple-element.42.residual_ref.value_ref, f32[1,2048]{1,0:T(1,128)} %bitcast.161, bf16[768,2048]{1,0:T(8,128)(2,1)} %bitcast.142, bf16[768,512]{1,0:T(8,128)(2,1)} %feed_input.4.refs_4_.refs_0_, ...), custom_call_target="tpu_custom_call" | custom-call | flops 12000000000 | bytes 1800000 | tf_op jit(solution)/shard_map/norm_back/pallas_call | solution.py:404
  501.7 11.8 %attend_back.3 = (bf16[1024,256]{1,0:T(8,128)(2,1)S(1)}, bf16[4,128,256]{2,1,0:T(8,128)(2,1)S(1)}, bf16[4,128,256]{2,1,0:T(8,128)(2,1)S(1)}) custom-call(s32[2]{0:T(128)S(1)} %copy-done.41, bf16[1024,768]{1,0:T(8,128)(2,1)S(1)} %bitcast.98, bf16[4,256,768]{2,1,0:T(8,128)(2,1)S(1)} %copy-done.16, bf16[4,256,768]{2,1,0:T(8,128)(2,1)S(1)} %copy-done.16, ...), custom_call_target="tpu_custom_call" | custom-call | flops 160000000000 | bytes 24000000 | tf_op jit(solution)/shard_map/attend_back/pallas_call | solution.py:622
  533.2 7.4 add_three.1
  543.2 9.7 %block_products.14.refs_0_ = bf16[4,256,1408]{2,1,0:T(8,128)(2,1)} custom-call(s32[1]{0:T(128)} %bitcast.26.where, bf16[768,2048]{1,0:T(8,128)(2,1)} %get-tuple-element.43.normed_ref.refs_0_, bf16[768,2048]{1,0:T(8,128)(2,1)} %collective-permute-done.32.refs_1_, bf16[768,2816]{1,0:T(8,128)(2,1)} %get-tuple-element.47.kept_ref.refs_2_, ...), custom_call_target="tpu_custom_call" | custom-call | flops 8999999488 | bytes 1350000 | tf_op jit(solution)/shard_map/block_products/pallas_call | solution.py:704
  556.6 12.2 %attend_back.4 = (bf16[1024,256]{1,0:T(8,128)(2,1)S(1)}, bf16[4,128,256]{2,1,0:T(8,128)(2,1)S(1)}, bf16[4,128,256]{2,1,0:T(8,128)(2,1)S(1)}) custom-call(s32[2]{0:T(128)S(1)} %copy-done.39, bf16[1024,768]{1,0:T(8,128)(2,1)S(1)} %bitcast.99, bf16[4,256,768]{2,1,0:T(8,128)(2,1)S(1)} %copy-done.16, bf16[4,256,768]{2,1,0:T(8,128)(2,1)S(1)} %copy-done.16, ...), custom_call_target="tpu_custom_call" | custom-call | flops 160000000000 | bytes 24000000 | tf_op jit(solution)/shard_map/attend_back/pallas_call | solution.py:622
  587.7 10.6 %collective-permute-start.63 = (bf16[256,1408]{1,0:T(8,128)(2,1)}, bf16[256,1408]{1,0:T(8,128)(2,1)}, u32[]{:S(2)}, u32[]{:S(2)}) collective-permute-start(bf16[256,1408]{1,0:T(8,128)(2,1)} %tie.41), channel_id=1, source_target_pairs={{0,4},{4,0},{2,6},{6,2},{1,5},{5,1},{3,7},{7,3},{8,12},{12,8},{10,... | collective-permute-start | bytes 2162696 | tf_op jit(solution)/shard_map/ppermute | solution.py:26
  598.3 14.9 %reduce-scatter.8.cloned.1.call-done = bf16[1,256,1408]{2,1,0:T(8,128)(2,1)} async-done(((bf16[4,256,1408]{2,1,0:T(8,128)(2,1)}), bf16[1,256,1408]{2,1,0:T(8,128)(2,1)}) %reduce-scatter.8.cloned.1.call-update) | async-done | bytes 720912 | tf_op jit(solution)/shard_map/reduce_scatter | solution.py:750
  614.6 12.0 %attend_back.5 = (bf16[1024,256]{1,0:T(8,128)(2,1)S(1)}, bf16[4,128,256]{2,1,0:T(8,128)(2,1)S(1)}, bf16[4,128,256]{2,1,0:T(8,128)(2,1)S(1)}) custom-call(s32[2]{0:T(128)S(1)} %copy-done.44, bf16[1024,768]{1,0:T(8,128)(2,1)} %bitcast.94, bf16[4,256,768]{2,1,0:T(8,128)(2,1)} %pad_maximum_fusion.4.refs_2_.refs_3_, ...), custom_call_target="tpu_custom_call" | custom-call | flops 160000000000 | bytes 24000000 | tf_op jit(solution)/shard_map/attend_back/pallas_call | solution.py:622
  704.9 19.2 %collective-permute-done.57 = bf16[512,128]{1,0:T(8,128)(2,1)S(1)} collective-permute-done((bf16[512,128]{1,0:T(8,128)(2,1)}, bf16[512,128]{1,0:T(8,128)(2,1)S(1)}, u32[]{:S(2)}, u32[]{:S(2)}) %collective-permute-start.57) | collective-permute-done | bytes 131104 | tf_op jit(solution)/shard_map/ppermute | solution.py:758
  739.2 13.3 %norm_back_rows.1 = (f32[768,2048]{1,0:T(8,128)}, f32[1,2048]{1,0:T(1,128)}) custom-call(bf16[768,2048]{1,0:T(8,128)(2,1)} %bitcast.105, f32[768,2048]{1,0:T(8,128)} %fusion.5.term_ref, f32[1,2048]{1,0:T(1,128)} %bitcast.159, f32[768,2048]{1,0:T(8,128)} %get-tuple-element.63.base_ref, bf16[256,2048]{1,0:T(8,128)(2,1)} %product.13.refs_4_.refs_0_, ...), custom_call_target="tpu_custom_call" | custom-call | flops 12999999488 | bytes 1950000 | tf_op jit(solution)/shard_map/norm_back_rows/pallas_call | solution.py:452
  774.3 12.2 %collective-permute-done.54 = bf16[512,512]{1,0:T(8,128)(2,1)S(1)} collective-permute-done((bf16[512,512]{1,0:T(8,128)(2,1)}, bf16[512,512]{1,0:T(8,128)(2,1)S(1)}, u32[]{:S(2)}, u32[]{:S(2)}) %collective-permute-start.54) | collective-permute-done | bytes 524320 | tf_op jit(solution)/shard_map/ppermute | solution.py:26
  (515 shorter events, 364.0 us)
Async XLA Ops:
  7.2 75.5 %all-gather.9.cloned.1.call-start = ((), (), s32[]{:S(2)}) async-start(), calls=%async_computation.10 | async-start | bytes 1310720 | tf_op jit(solution)/shard_map/all_gather | solution.py:825
  45.6 105.2 %all-gather.11.cloned.1.call-start = ((), (), s32[]{:S(2)}) async-start(), calls=%async_computation.11 | async-start | bytes 3604480 | tf_op jit(solution)/shard_map/all_gather | solution.py:825
  47.7 147.6 %all-gather.13.cloned.1.call-start = ((), (), s32[]{:S(2)}) async-start(), calls=%async_computation.12 | async-start | bytes 3604480 | tf_op jit(solution)/shard_map/all_gather | solution.py:825
  50.0 204.6 %all-gather.15.cloned.1.call-start = ((), (), s32[]{:S(2)}) async-start(), calls=%async_computation.13 | async-start | bytes 3604480 | tf_op jit(solution)/shard_map/all_gather | solution.py:825
  82.6 395.5 %reduce-scatter.6.cloned.1.call-start = ((), (), s32[]{:S(2)}) async-start(), calls=%async_computation.5 | async-start | bytes 7208960 | tf_op jit(solution)/shard_map/reduce_scatter | solution.py:750
  104.9 39.1 %collective-permute-start.15 = (bf16[3,256,512]{2,1,0:T(8,128)(2,1)}, bf16[3,256,512]{2,1,0:T(8,128)(2,1)}, u32[]{:S(2)}, u32[]{:S(2)}) collective-permute-start(bf16[3,256,512]{2,1,0:T(8,128)(2,1)} %pad_maximum_fusion.8.refs_12_.refs_0_), channel_id=1, source_target_pairs={{0,2},{2,0},{4,6},{6,4},{1,3},{3,1},{5,7},{7,5},{8,10},{10,8},{12,... | collective-permute-start | bytes 2359304 | tf_op jit(solution)/shard_map/ppermute | solution.py:22
  154.0 103.8 %collective-permute-start.21 = (bf16[3,128,2816]{2,1,0:T(8,128)(2,1)}, bf16[3,128,2816]{2,1,0:T(8,128)(2,1)}, u32[]{:S(2)}, u32[]{:S(2)}) collective-permute-start(bf16[3,128,2816]{2,1,0:T(8,128)(2,1)} %pad_maximum_fusion.refs_6_.refs_1_), channel_id=1, source_target_pairs={{0,4},{4,0},{2,6},{6,2},{1,5},{5,1},{3,7},{7,3},{8,12},{12,8},{10,... | collective-permute-start | bytes 6488072 | tf_op jit(solution)/shard_map/ppermute | solution.py:26
  198.6 60.3 %collective-permute-start.25 = (bf16[3,128,2816]{2,1,0:T(8,128)(2,1)}, bf16[3,128,2816]{2,1,0:T(8,128)(2,1)}, u32[]{:S(2)}, u32[]{:S(2)}) collective-permute-start(bf16[3,128,2816]{2,1,0:T(8,128)(2,1)} %pad_maximum_fusion.1.refs_6_), channel_id=1, source_target_pairs={{0,4},{4,0},{2,6},{6,2},{1,5},{5,1},{3,7},{7,3},{8,12},{12,8},{10,... | collective-permute-start | bytes 6488072 | tf_op jit(solution)/shard_map/ppermute | solution.py:26
  223.5 44.0 %collective-permute-start.22 = (bf16[3,128,2816]{2,1,0:T(8,128)(2,1)}, bf16[3,128,2816]{2,1,0:T(8,128)(2,1)}, u32[]{:S(2)}, u32[]{:S(2)}) collective-permute-start(bf16[3,128,2816]{2,1,0:T(8,128)(2,1)} %pad_maximum_fusion.refs_6_.refs_1_), channel_id=1, source_target_pairs={{0,2},{2,0},{4,6},{6,4},{1,3},{3,1},{5,7},{7,5},{8,10},{10,8},{12,... | collective-permute-start | bytes 6488072 | tf_op jit(solution)/shard_map/ppermute | solution.py:22
  223.5 44.0 %collective-permute-start.24 = (bf16[3,128,2816]{2,1,0:T(8,128)(2,1)}, bf16[3,128,2816]{2,1,0:T(8,128)(2,1)}, u32[]{:S(2)}, u32[]{:S(2)}) collective-permute-start(bf16[3,128,2816]{2,1,0:T(8,128)(2,1)} %pad_maximum_fusion.1.refs_6_), channel_id=1, source_target_pairs={{0,2},{2,0},{4,6},{6,4},{1,3},{3,1},{5,7},{7,5},{8,10},{10,8},{12,... | collective-permute-start | bytes 6488072 | tf_op jit(solution)/shard_map/ppermute | solution.py:22
  256.6 48.0 %collective-permute-start.27 = (bf16[3,704,512]{2,1,0:T(8,128)(2,1)S(1)}, bf16[3,704,512]{2,1,0:T(8,128)(2,1)}, u32[]{:S(2)}, u32[]{:S(2)}) collective-permute-start(bf16[3,704,512]{2,1,0:T(8,128)(2,1)S(1)} %pad_maximum_fusion.2.refs_7_.refs_0_), channel_id=1, source_target_pairs={{0,4},{4,0},{2,6},{6,2},{1,5},{5,1},{3,7},{7,3},{8,12},{12,8},{10,... | collective-permute-start | bytes 6488072 | tf_op jit(solution)/shard_map/ppermute | solution.py:26
  306.2 37.6 %collective-permute-start.28 = (bf16[3,704,512]{2,1,0:T(8,128)(2,1)S(1)}, bf16[3,704,512]{2,1,0:T(8,128)(2,1)}, u32[]{:S(2)}, u32[]{:S(2)}) collective-permute-start(bf16[3,704,512]{2,1,0:T(8,128)(2,1)S(1)} %copy-done.73), channel_id=1, source_target_pairs={{0,2},{2,0},{4,6},{6,4},{1,3},{3,1},{5,7},{7,5},{8,10},{10,8},{12,... | collective-permute-start | bytes 6488072 | tf_op jit(solution)/shard_map/ppermute | solution.py:22
  307.8 36.0 %collective-permute-start.29 = (bf16[3,704,512]{2,1,0:T(8,128)(2,1)}, bf16[3,704,512]{2,1,0:T(8,128)(2,1)}, u32[]{:S(2)}, u32[]{:S(2)}) collective-permute-start(bf16[3,704,512]{2,1,0:T(8,128)(2,1)} %collective-permute-done.27.refs_1_.refs_2_), channel_id=1, source_target_pairs={{0,2},{2,0},{4,6},{6,4},{1,3},{3,1},{5,7},{7,5},{8,10},{10,8},{12,... | collective-permute-start | bytes 6488072 | tf_op jit(solution)/shard_map/ppermute | solution.py:22
  343.7 241.9 %reduce-scatter.14.cloned.1.call-start = ((), (), s32[]{:S(2)}) async-start(), calls=%async_computation.9 | async-start | bytes 3604480 | tf_op jit(solution)/shard_map/reduce_scatter | solution.py:750
  381.3 138.1 %collective-permute-start.40 = (bf16[512,768]{1,0:T(8,128)(2,1)}, bf16[512,768]{1,0:T(8,128)(2,1)}, u32[]{:S(2)}, u32[]{:S(2)}) collective-permute-start(bf16[512,768]{1,0:T(8,128)(2,1)} %get-tuple-element.95), channel_id=1, source_target_pairs={{0,2},{2,0},{4,6},{6,4},{1,3},{3,1},{5,7},{7,5},{8,10},{10,8},{12,... | collective-permute-start | bytes 2359304 | tf_op jit(solution)/shard_map/ppermute | solution.py:22
  402.1 64.0 %collective-permute-start.39 = (bf16[4,256,1408]{2,1,0:T(8,128)(2,1)}, bf16[4,256,1408]{2,1,0:T(8,128)(2,1)}, u32[]{:S(2)}, u32[]{:S(2)}) collective-permute-start(bf16[4,256,1408]{2,1,0:T(8,128)(2,1)} %tie.33.rest_0_), channel_id=1, source_target_pairs={{0,4},{4,0},{2,6},{6,2},{1,5},{5,1},{3,7},{7,3},{8,12},{12,8},{10,... | collective-permute-start | bytes 8650760 | tf_op jit(solution)/shard_map/ppermute | solution.py:26
  424.6 42.7 %collective-permute-start.37 = (bf16[768,512]{1,0:T(8,128)(2,1)}, bf16[768,512]{1,0:T(8,128)(2,1)S(1)}, u32[]{:S(2)}, u32[]{:S(2)}) collective-permute-start(bf16[768,512]{1,0:T(8,128)(2,1)} %feed_input.6.rest_0_.refs_4_.refs_2_), channel_id=1, source_target_pairs={{0,1},{1,0},{2,3},{3,2},{4,5},{5,4},{6,7},{7,6},{8,9},{9,8},{10,11... | collective-permute-start | bytes 2359304 | tf_op jit(solution)/shard_map/ppermute | solution.py:921
  460.8 72.4 %collective-permute-start.36 = (bf16[768,2048]{1,0:T(8,128)(2,1)}, bf16[768,2048]{1,0:T(8,128)(2,1)}, u32[]{:S(2)}, u32[]{:S(2)}) collective-permute-start(bf16[768,2048]{1,0:T(8,128)(2,1)} %product.11.mine_ref.refs_5_.refs_8_), channel_id=1, source_target_pairs={{0,1},{1,0},{2,3},{3,2},{4,5},{5,4},{6,7},{7,6},{8,9},{9,8},{10,11... | collective-permute-start | bytes 9437192 | tf_op jit(solution)/shard_map/ppermute | solution.py:931
  466.1 63.0 %collective-permute-start.42 = (bf16[4,256,1408]{2,1,0:T(8,128)(2,1)}, bf16[4,256,1408]{2,1,0:T(8,128)(2,1)}, u32[]{:S(2)}, u32[]{:S(2)}) collective-permute-start(bf16[4,256,1408]{2,1,0:T(8,128)(2,1)} %tie.34.refs_6_), channel_id=1, source_target_pairs={{0,4},{4,0},{2,6},{6,2},{1,5},{5,1},{3,7},{7,3},{8,12},{12,8},{10,... | collective-permute-start | bytes 8650760 | tf_op jit(solution)/shard_map/ppermute | solution.py:26
  500.2 113.0 %reduce-scatter.8.cloned.1.call-start = ((), (), s32[]{:S(2)}) async-start(), calls=%async_computation.6 | async-start | bytes 3604480 | tf_op jit(solution)/shard_map/reduce_scatter | solution.py:750
  530.3 119.8 %collective-permute-start.47 = (bf16[768,2048]{1,0:T(8,128)(2,1)}, bf16[768,2048]{1,0:T(8,128)(2,1)}, u32[]{:S(2)}, u32[]{:S(2)}) collective-permute-start(bf16[768,2048]{1,0:T(8,128)(2,1)} %copy-done.68), channel_id=1, source_target_pairs={{0,2},{2,0},{4,6},{6,4},{1,3},{3,1},{5,7},{7,5},{8,10},{10,8},{12,... | collective-permute-start | bytes 9437192 | tf_op jit(solution)/shard_map/ppermute | solution.py:22
  540.7 72.6 %collective-permute-start.44 = (bf16[256,2048]{1,0:T(8,128)(2,1)}, bf16[256,2048]{1,0:T(8,128)(2,1)}, u32[]{:S(2)}, u32[]{:S(2)}) collective-permute-start(bf16[256,2048]{1,0:T(8,128)(2,1)} %product.13.refs_4_.refs_0_), channel_id=1, source_target_pairs={{0,1},{1,0},{2,3},{3,2},{4,5},{5,4},{6,7},{7,6},{8,9},{9,8},{10,11... | collective-permute-start | bytes 3145736 | tf_op jit(solution)/shard_map/ppermute | solution.py:958
  553.0 97.1 %reduce-scatter.10.cloned.1.call-start = ((), (), s32[]{:S(2)}) async-start(), calls=%async_computation.7 | async-start | bytes 1310720 | tf_op jit(solution)/shard_map/reduce_scatter | solution.py:750
  576.5 73.7 %collective-permute-start.49 = (bf16[256,2048]{1,0:T(8,128)(2,1)}, bf16[256,2048]{1,0:T(8,128)(2,1)}, u32[]{:S(2)}, u32[]{:S(2)}) collective-permute-start(bf16[256,2048]{1,0:T(8,128)(2,1)} %product.14.refs_5_.refs_1_), channel_id=1, source_target_pairs={{0,1},{1,0},{2,3},{3,2},{4,5},{5,4},{6,7},{7,6},{8,9},{9,8},{10,11... | collective-permute-start | bytes 3145736 | tf_op jit(solution)/shard_map/ppermute | solution.py:958
  587.7 42.8 %collective-permute-start.63 = (bf16[256,1408]{1,0:T(8,128)(2,1)}, bf16[256,1408]{1,0:T(8,128)(2,1)}, u32[]{:S(2)}, u32[]{:S(2)}) collective-permute-start(bf16[256,1408]{1,0:T(8,128)(2,1)} %tie.41), channel_id=1, source_target_pairs={{0,4},{4,0},{2,6},{6,2},{1,5},{5,1},{3,7},{7,3},{8,12},{12,8},{10,... | collective-permute-start | bytes 2162696 | tf_op jit(solution)/shard_map/ppermute | solution.py:26
  613.2 159.8 %reduce-scatter.12.cloned.1.call-start = ((), (), s32[]{:S(2)}) async-start(), calls=%async_computation.8 | async-start | bytes 2621440 | tf_op jit(solution)/shard_map/reduce_scatter | solution.py:750
  633.8 37.0 %collective-permute-start.64 = (bf16[512,1408]{1,0:T(8,128)(2,1)}, bf16[512,1408]{1,0:T(8,128)(2,1)}, u32[]{:S(2)}, u32[]{:S(2)}) collective-permute-start(bf16[512,1408]{1,0:T(8,128)(2,1)} %pad_maximum_fusion.6), channel_id=1, source_target_pairs={{0,2},{2,0},{4,6},{6,4},{1,3},{3,1},{5,7},{7,5},{8,10},{10,8},{12,... | collective-permute-start | bytes 4325384 | tf_op jit(solution)/shard_map/ppermute | solution.py:22
  674.2 64.9 %collective-permute-start.52 = (bf16[256,2048]{1,0:T(8,128)(2,1)}, bf16[256,2048]{1,0:T(8,128)(2,1)}, u32[]{:S(2)}, u32[]{:S(2)}) collective-permute-start(bf16[256,2048]{1,0:T(8,128)(2,1)} %product.15.refs_4_.refs_2_), channel_id=1, source_target_pairs={{0,1},{1,0},{2,3},{3,2},{4,5},{5,4},{6,7},{7,6},{8,9},{9,8},{10,11... | collective-permute-start | bytes 3145736 | tf_op jit(solution)/shard_map/ppermute | solution.py:958
  676.4 50.2 %collective-permute-start.65 = (bf16[256,1408]{1,0:T(8,128)(2,1)}, bf16[256,1408]{1,0:T(8,128)(2,1)}, u32[]{:S(2)}, u32[]{:S(2)}) collective-permute-start(bf16[256,1408]{1,0:T(8,128)(2,1)} %tie.42), channel_id=1, source_target_pairs={{0,4},{4,0},{2,6},{6,2},{1,5},{5,1},{3,7},{7,3},{8,12},{12,8},{10,... | collective-permute-start | bytes 2162696 | tf_op jit(solution)/shard_map/ppermute | solution.py:26
  704.2 52.4 %collective-permute-start.62 = (bf16[512,512]{1,0:T(8,128)(2,1)S(1)}, bf16[512,512]{1,0:T(8,128)(2,1)S(1)}, u32[]{:S(2)}, u32[]{:S(2)}) collective-permute-start(bf16[512,512]{1,0:T(8,128)(2,1)S(1)} %copy-done.78), channel_id=1, source_target_pairs={{0,2},{2,0},{4,6},{6,4},{1,3},{3,1},{5,7},{7,5},{8,10},{10,8},{12,... | collective-permute-start | bytes 1572872 | tf_op jit(solution)/shard_map/ppermute | solution.py:22
  724.6 43.1 %collective-permute-start.67 = (bf16[2816,256]{1,0:T(8,128)(2,1)}, bf16[2816,256]{1,0:T(8,128)(2,1)}, u32[]{:S(2)}, u32[]{:S(2)}) collective-permute-start(bf16[2816,256]{1,0:T(8,128)(2,1)} %add_convert_fusion), channel_id=1, source_target_pairs={{0,2},{2,0},{4,6},{6,4},{1,3},{3,1},{5,7},{7,5},{8,10},{10,8},{12,... | collective-permute-start | bytes 4325384 | tf_op jit(solution)/shard_map/ppermute | solution.py:22
  726.6 36.9 %collective-permute-start.59 = (bf16[512,128]{1,0:T(8,128)(2,1)S(1)}, bf16[512,128]{1,0:T(8,128)(2,1)S(1)}, u32[]{:S(2)}, u32[]{:S(2)}) collective-permute-start(bf16[512,128]{1,0:T(8,128)(2,1)S(1)} %fusion.12), channel_id=1, source_target_pairs={{0,4},{4,0},{2,6},{6,2},{1,5},{5,1},{3,7},{7,3},{8,12},{12,8},{10,... | collective-permute-start | bytes 393224 | tf_op jit(solution)/shard_map/ppermute | solution.py:26
  (151 other events, 2138.7 us)
Sparse Core Ops, SparseCore 0:
  45.7 29.7 all-gather.8
  77.0 58.7 all-gather.10
  137.4 57.8 all-gather.12
  196.7 57.8 all-gather.14
  343.8 100.8 reduce-scatter.5
  500.3 53.9 reduce-scatter.13
  557.1 56.0 reduce-scatter.7
  616.1 26.9 reduce-scatter.9
  676.5 55.4 reduce-scatter.11

commit v4 on v3

--- a/solution.py
+++ b/solution.py
@@ -139,7 +139,7 @@
             out_specs=out_spec,
         ),
         compiler_params=pltpu.CompilerParams(vmem_limit_bytes=56 * 2**20),
-        cost_estimate=taking(8),
+        cost_estimate=taking(240),
         name="place",
     )(jnp.stack([ctx, me]), weight.reshape(4, rows, width), *sum(pieces, []), *after)
     return out.reshape(shards * height, width) if along_rows else out
@@ -277,7 +277,7 @@
             out_specs=pl.BlockSpec((tokens, TILE), lambda j, _: (0, j)),
         ),
         compiler_params=ROOMY,
-        cost_estimate=taking(10),
+        cost_estimate=taking(300),
         name="feed_input",
     )(low.reshape(1), kept, given, full, full, *after)
 
@@ -414,7 +414,7 @@
         + [UNREAD] * len(after),
         out_specs=(row_spec, line_spec, row_spec),
         compiler_params=ROOMY,
-        cost_estimate=taking(12),
+        cost_estimate=taking(360),
         name="norm_back",
     )(values, gain[None, :], base, *mine, *came, *after)
 
@@ -545,7 +545,7 @@
             ],
         ),
         compiler_params=pltpu.CompilerParams(vmem_limit_bytes=48 * 2**20),
-        cost_estimate=taking(14),
+        cost_estimate=taking(0.42),
         name="attend",
     )(info, query_t, keyval, keyval, start_row, *after)
 
@@ -871,7 +871,7 @@
     out_weight = place(output_weight, out_pieces, *where, False, [query_t])
     gate_own = others(tie(gate_all, came), me)
     mixed, log_sums, infos, mine, came = [], [], [], [], []
-    last = [out_weight, gate_own, keyval_weight]
+    last = [gate_own, keyval_weight]
     for s in range(seq_here):
         infos.append(jnp.stack([ctx, first_block[s]]).astype(jnp.int32))
         mixed_s, log_s = attend(
@@ -951,7 +951,7 @@
         if s == 0:
             waits = []
         if s == 1:
-            waits = []
+            waits = [came[0], ffn_came]
         if s == 2:
             waits = []
         mine.append(product(query_delta, qkv_weight[:, :query_cols], 0, 1, 512, waits))
@@ -966,7 +966,7 @@
             output_tied = tie(output.total, gate_up_second)
             down_came = high_swap(tie(down_sum, output.came))
             first_came = high_swap(tie(gate_up_first, down_came))
-            last = [output.total, came[0], down_came, output_tied]
+            last = [output.total, came[0], came[1], down_came] + [output_tied]
 
     part_sum = jnp.concatenate(part_sums, 2).reshape(2, 2, 2 * kv_width, tokens)
     sent = lax.dynamic_index_in_dim(part_sum, 1 - high, 0, False)
@@ -1003,7 +1003,7 @@
     keyval_term = dot(keyval_both, keyval_weight, 0, 1)
 
     input_grad, attn_gain_term = norm_back_rows(
-        acts, mine, came, keyval_term, gain_one, residual_delta, [keyval_products]
+        acts, mine, came, keyval_term, gain_one, residual_delta, [keyval_products, query_sum]
     )
     block_out = add_three(residual, ffn_mine, ffn_came, [])
     block_out = block_out.reshape(activations.shape)

time: 812 us -> 794 us (0.978)
  starting transfers between devices: 93.1 us -> 74.5 us
    ppermute x32, waiting for transfers between devices: 16.7 us -> 3.94 us  [low_swap(): return lax.ppermute(value, 'ctx', SWAP_LOW)]
    ppermute x19, waiting for transfers between devices: 72.1 us -> 81.2 us  [high_swap(): return lax.ppermute(value, 'ctx', SWAP_HIGH)]
    ppermute x19, starting transfers between devices: 38.2 us -> 29.6 us  [high_swap(): return lax.ppermute(value, 'ctx', SWAP_HIGH)]
    ppermute x6, waiting for transfers between devices: 2.65 us -> 11.1 us  [body(): came.append(lax.ppermute(mine[s], 'tp', SWAP_TP))]
    unnamed x207 -> x199, local copies, waits for them, and re-layouts: 38.6 us -> 37 us
  transfers between devices with their start and end apart: 82 -> 82, of which waited for: 24 -> 22; matrix products, arithmetic and copies ran while one was open for 13% -> 14% of each run, Pallas kernels for 44% -> 45%
where the time goes in v4:
time: 794 us; the launch traced here: 786 us
  Pallas kernels  350 us (44%)
  waiting for transfers between devices  202 us (25%)
  starting transfers between devices  74.5 us (9%)
  local copies, waits for them, and re-layouts  74.5 us (9%)
  other arithmetic  61.5 us (8%)
  between operations  15.4 us (2%)
  matrix products  8.91 us (1%)
    ppermute x19, waiting for transfers between devices, high_swap(): return lax.ppermute(value, 'ctx', SWAP_HIGH)  81.2 us
    pallas_call x9, Pallas kernels, block_products(): pl.pallas_call(kernel, out_shape=jax.ShapeDtypeStruct(out_shape, bf16), g...  77.8 us
    pallas_call x8, Pallas kernels, product(): pl.pallas_call(kernel, out_shape=jax.ShapeDtypeStruct((rows, width), bf16...  52.9 us
    pallas_call x4, Pallas kernels, feed_input(): pl.pallas_call(kernel, out_shape=jax.ShapeDtypeStruct((tokens, model_widt...  40.4 us
    unnamed x199, local copies, waits for them, and re-layouts  37 us
    pallas_call x3, Pallas kernels, attend_back(): pl.pallas_call(lambda *refs: attend_back_kernel(group, *refs), out_shape=...  36.2 us
    all_gather x4, waiting for transfers between devices, later(): lax.all_gather(tie(quarter(weight, ctx), *after), 'shard', axis=0, tiled=...  33.9 us
    pallas_call x3, Pallas kernels, attend(): pl.pallas_call(lambda *refs: attend_kernel(group, *refs), out_shape=(jax....  29.9 us
  transfers between devices with their start and end apart: 82, of which 22 were waited for; matrix products, arithmetic and copies ran while one was open for 14% of the time, Pallas kernels for 45%

profile of v4, /device:TPU:1, one launch (start us, length us, event | category | flops | bytes accessed | tf_op | source)
XLA Modules:
  0.0 786.3 jit_solution(10736768253360891209)
XLA Ops:
  21.7 23.0 %collective-permute-done.1 = bf16[128,1408]{1,0:T(8,128)(2,1)S(1)} collective-permute-done((bf16[128,1408]{1,0:T(8,128)(2,1)S(1)}, bf16[128,1408]{1,0:T(8,128)(2,1)S(1)}, u32[]{:S(2)}, u32[]{:S(2)}) %collective-permute-start.1) | collective-permute-done | bytes 360480 | tf_op jit(solution)/shard_map/ppermute | solution.py:818
  112.0 12.0 %collective-permute-done.13.refs_1_.refs_2_ = bf16[3,256,512]{2,1,0:T(8,128)(2,1)} collective-permute-done((bf16[3,256,512]{2,1,0:T(8,128)(2,1)}, bf16[3,256,512]{2,1,0:T(8,128)(2,1)}, u32[]{:S(2)}, u32[]{:S(2)}) %collective-permute-start.13) | collective-permute-done | bytes 786464 | tf_op jit(solution)/shard_map/ppermute | solution.py:26
  149.2 10.0 %attend.3 = (bf16[1024,256]{1,0:T(8,128)(2,1)S(1)}, f32[2,8,256]{2,1,0:T(8,128)S(1)}) custom-call(s32[2]{0:T(128)S(1)} %get-tuple-element.142.refs_0_, bf16[1024,768]{1,0:T(8,128)(2,1)S(1)} %bitcast.95, bf16[4,256,768]{2,1,0:T(8,128)(2,1)S(1)} %pad_maximum_fusion.4.refs_2_.refs_3_, bf16[4,256,768]{2,1,0:T(8,128)(2,1)S(1)} %pad_maximum_fusion.4.refs_2_.refs_3_, ...), custom_call_target="tpu_custom_call" | custom-call | flops 420000000 | bytes 63000 | tf_op jit(solution)/shard_map/attend/pallas_call | solution.py:522
  167.9 10.0 %attend.4 = (bf16[1024,256]{1,0:T(8,128)(2,1)S(1)}, f32[2,8,256]{2,1,0:T(8,128)S(1)}) custom-call(s32[2]{0:T(128)S(1)} %get-tuple-element.143.refs_0_, bf16[1024,768]{1,0:T(8,128)(2,1)S(1)} %bitcast.96, bf16[4,256,768]{2,1,0:T(8,128)(2,1)S(1)} %pad_maximum_fusion.4.refs_2_.refs_3_, bf16[4,256,768]{2,1,0:T(8,128)(2,1)S(1)} %pad_maximum_fusion.4.refs_2_.refs_3_, ...), custom_call_target="tpu_custom_call" | custom-call | flops 420000000 | bytes 63000 | tf_op jit(solution)/shard_map/attend/pallas_call | solution.py:522
  183.7 12.2 %all-gather.13.cloned.1.call-done = bf16[512,2816]{1,0:T(8,128)(2,1)} async-done(((bf16[128,2816]{1,0:T(8,128)(2,1)}), bf16[512,2816]{1,0:T(8,128)(2,1)}) %all-gather.13.cloned.1.call-update) | async-done | bytes 2883600 | tf_op jit(solution)/shard_map/all_gather | solution.py:825
  202.2 10.0 %attend.5 = (bf16[1024,256]{1,0:T(8,128)(2,1)S(1)}, f32[2,8,256]{2,1,0:T(8,128)S(1)}) custom-call(s32[2]{0:T(128)S(1)} %pad_add_fusion.3.refs_0_, bf16[1024,768]{1,0:T(8,128)(2,1)S(1)} %bitcast.97, bf16[4,256,768]{2,1,0:T(8,128)(2,1)S(1)} %pad_maximum_fusion.4.refs_2_.refs_3_, bf16[4,256,768]{2,1,0:T(8,128)(2,1)S(1)} %pad_maximum_fusion.4.refs_2_.refs_3_, ...), custom_call_target="tpu_custom_call" | custom-call | flops 420000000 | bytes 63000 | tf_op jit(solution)/shard_map/attend/pallas_call | solution.py:522
  213.0 11.1 %collective-permute-done.19.rest_0_.refs_4_ = bf16[256,2048]{1,0:T(8,128)(2,1)S(1)} collective-permute-done((bf16[256,2048]{1,0:T(8,128)(2,1)S(1)}, bf16[256,2048]{1,0:T(8,128)(2,1)S(1)}, u32[]{:S(2)}, u32[]{:S(2)}) %collective-permute-start.19) | collective-permute-done | bytes 1048608 | tf_op jit(solution)/shard_map/ppermute | solution.py:883
  233.5 21.7 %all-gather.15.cloned.1.call-done = bf16[2816,512]{1,0:T(8,128)(2,1)} async-done(((bf16[704,512]{1,0:T(8,128)(2,1)}), bf16[2816,512]{1,0:T(8,128)(2,1)}) %all-gather.15.cloned.1.call-update) | async-done | bytes 2883600 | tf_op jit(solution)/shard_map/all_gather | solution.py:825
  260.7 8.5 %add_and_norm.1 = (f32[768,2048]{1,0:T(8,128)}, bf16[768,2048]{1,0:T(8,128)(2,1)}) custom-call(bf16[768,2048]{1,0:T(8,128)(2,1)} %bitcast.104, f32[1,2048]{1,0:T(1,128)} %bitcast.161, bf16[256,2048]{1,0:T(8,128)(2,1)} %product.8.refs_5_.refs_0_, bf16[256,2048]{1,0:T(8,128)(2,1)} %product.9.refs_1_.refs_5_, bf16[256,2048]{1,0:T(8,128)(2,1)} %product.10.refs_1_.refs_2_, ...), custom_call_target="tpu_custom_call" | custom-call | flops 89999998976 | bytes 13500000 | tf_op jit(solution)/shard_map/add_and_norm/pallas_call | solution.py:329
  270.6 28.7 %feed_forward.1 = (bf16[768,2816]{1,0:T(8,128)(2,1)}, bf16[768,2816]{1,0:T(8,128)(2,1)}, bf16[768,2816]{1,0:T(8,128)(2,1)}, bf16[2,2048,2816]{2,1,0:T(8,128)(2,1)}) custom-call(s32[2]{0:T(128)} %pad_add_fusion.where, bf16[768,2048]{1,0:T(8,128)(2,1)} %get-tuple-element.43.normed_ref.refs_0_, bf16[4,128,2816]{2,1,0:T(8,128)(2,1)} %bitcast.156, ...), custom_call_target="tpu_custom_call" | custom-call | flops 28999999488 | bytes 4350000 | tf_op jit(solution)/shard_map/feed_forward/pallas_call | solution.py:185
  320.4 15.9 %block_products.9.refs_4_ = bf16[4,2816,256]{2,1,0:T(8,128)(2,1)} custom-call(s32[1]{0:T(128)} %bitcast.22.where, bf16[768,2816]{1,0:T(8,128)(2,1)} %tie.32.refs_0_.left_ref, bf16[768,2816]{1,0:T(8,128)(2,1)} %collective-permute-done.30.refs_1_, bf16[768,2048]{1,0:T(8,128)(2,1)} %bitcast.140, bf16[768,2048]{1,0:T(8,128)(2,1)} %collective-permute-done.31.refs_3_), custom_call_target="tpu_custom_call" | custom-call | flops 8999999488 | bytes 1350000 | tf_op jit(solution)/shard_map/block_products/pallas_call | solution.py:704
  336.4 10.6 %place.5.down_ref.right_ref = bf16[2816,2048]{1,0:T(8,128)(2,1)} custom-call(s32[2]{0:T(128)} %pad_add_fusion.where, bf16[4,704,512]{2,1,0:T(8,128)(2,1)} %bitcast.158, bf16[3,704,512]{2,1,0:T(8,128)(2,1)} %pad_maximum_fusion.2.refs_7_.refs_0_, bf16[3,704,512]{2,1,0:T(8,128)(2,1)} %collective-permute-done.28.refs_1_, ...), custom_call_target="tpu_custom_call" | custom-call | flops 240000008192 | bytes 36000000 | tf_op jit(solution)/shard_map/place/pallas_call | solution.py:130
  347.0 19.1 %feed_back.1 = (bf16[768,2816]{1,0:T(8,128)(2,1)}, bf16[768,2816]{1,0:T(8,128)(2,1)}) custom-call(s32[1]{0:T(128)} %bitcast.22.where, bf16[768,2048]{1,0:T(8,128)(2,1)} %bitcast.141, bf16[2816,2048]{1,0:T(8,128)(2,1)} %place.5.down_ref.right_ref, bf16[768,2816]{1,0:T(8,128)(2,1)} %get-tuple-element.45.gate_ref, bf16[768,2816]{1,0:T(8,128)(2,1)} %get-tuple-element.46.up_ref), custom_call_target="tpu_custom_call" | custom-call | flops 5699999744 | bytes 855000 | tf_op jit(solution)/shard_map/feed_back/pallas_call | solution.py:233
  366.2 10.1 %feed_input.4.refs_4_.refs_0_ = bf16[768,512]{1,0:T(8,128)(2,1)} custom-call(s32[1]{0:T(128)} %bitcast.22.where, bf16[768,2816]{1,0:T(8,128)(2,1)} %get-tuple-element.47.kept_ref.refs_2_, bf16[768,2816]{1,0:T(8,128)(2,1)} %get-tuple-element.48.given_ref, bf16[2,2048,2816]{2,1,0:T(8,128)(2,1)} %get-tuple-element.49.kept_weight.given_weight, ...), custom_call_target="tpu_custom_call" | custom-call | flops 299999985664 | bytes 45000000 | tf_op jit(solution)/shard_map/feed_input/pallas_call | solution.py:264
  377.5 9.2 %block_products.10.refs_0_ = bf16[4,256,1408]{2,1,0:T(8,128)(2,1)} custom-call(s32[1]{0:T(128)} %bitcast.24.where, bf16[768,2048]{1,0:T(8,128)(2,1)} %get-tuple-element.43.normed_ref.refs_0_, bf16[768,2048]{1,0:T(8,128)(2,1)} %collective-permute-done.32.refs_1_, bf16[768,2816]{1,0:T(8,128)(2,1)} %get-tuple-element.47.kept_ref.refs_2_, ...), custom_call_target="tpu_custom_call" | custom-call | flops 8999999488 | bytes 1350000 | tf_op jit(solution)/shard_map/block_products/pallas_call | solution.py:704
  386.7 10.2 %feed_input.5.rest_0_.refs_1_ = bf16[768,512]{1,0:T(8,128)(2,1)} custom-call(s32[1]{0:T(128)} %bitcast.22.where, bf16[768,2816]{1,0:T(8,128)(2,1)} %get-tuple-element.47.kept_ref.refs_2_, bf16[768,2816]{1,0:T(8,128)(2,1)} %get-tuple-element.48.given_ref, bf16[2,2048,2816]{2,1,0:T(8,128)(2,1)} %get-tuple-element.49.kept_weight.given_weight, ...), custom_call_target="tpu_custom_call" | custom-call | flops 299999985664 | bytes 45000000 | tf_op jit(solution)/shard_map/feed_input/pallas_call | solution.py:264
  398.3 10.0 %feed_input.6.rest_0_.refs_4_.refs_2_ = bf16[768,512]{1,0:T(8,128)(2,1)} custom-call(s32[1]{0:T(128)} %bitcast.22.where, bf16[768,2816]{1,0:T(8,128)(2,1)} %get-tuple-element.47.kept_ref.refs_2_, bf16[768,2816]{1,0:T(8,128)(2,1)} %get-tuple-element.48.given_ref, bf16[2,2048,2816]{2,1,0:T(8,128)(2,1)} %get-tuple-element.49.kept_weight.given_weight, ...), custom_call_target="tpu_custom_call" | custom-call | flops 299999985664 | bytes 45000000 | tf_op jit(solution)/shard_map/feed_input/pallas_call | solution.py:264
  409.6 9.2 %block_products.11.refs_0_ = bf16[4,256,1408]{2,1,0:T(8,128)(2,1)} custom-call(s32[1]{0:T(128)} %bitcast.24.where, bf16[768,2048]{1,0:T(8,128)(2,1)} %get-tuple-element.43.normed_ref.refs_0_, bf16[768,2048]{1,0:T(8,128)(2,1)} %collective-permute-done.32.refs_1_, bf16[768,2816]{1,0:T(8,128)(2,1)} %get-tuple-element.47.kept_ref.refs_2_, ...), custom_call_target="tpu_custom_call" | custom-call | flops 8999999488 | bytes 1350000 | tf_op jit(solution)/shard_map/block_products/pallas_call | solution.py:704
  418.7 10.2 %feed_input.7.rest_0_.refs_3_ = bf16[768,512]{1,0:T(8,128)(2,1)} custom-call(s32[1]{0:T(128)} %bitcast.22.where, bf16[768,2816]{1,0:T(8,128)(2,1)} %get-tuple-element.47.kept_ref.refs_2_, bf16[768,2816]{1,0:T(8,128)(2,1)} %get-tuple-element.48.given_ref, bf16[2,2048,2816]{2,1,0:T(8,128)(2,1)} %get-tuple-element.49.kept_weight.given_weight, ...), custom_call_target="tpu_custom_call" | custom-call | flops 299999985664 | bytes 45000000 | tf_op jit(solution)/shard_map/feed_input/pallas_call | solution.py:264
  429.1 14.6 %product.11.mine_ref.refs_5_.refs_8_ = bf16[768,2048]{1,0:T(8,128)(2,1)} custom-call(bf16[768,2816]{1,0:T(8,128)(2,1)} %tie.32.refs_0_.left_ref, bf16[2816,2048]{1,0:T(8,128)(2,1)} %place.5.down_ref.right_ref, bf16[768,512]{1,0:T(8,128)(2,1)} %feed_input.7.rest_0_.refs_3_), custom_call_target="tpu_custom_call" | custom-call | flops 600000000 | bytes 90000 | tf_op jit(solution)/shard_map/product/pallas_call | solution.py:299
  444.9 15.6 %collective-permute-done.39.refs_1_.refs_4_ = bf16[4,256,1408]{2,1,0:T(8,128)(2,1)} collective-permute-done((bf16[4,256,1408]{2,1,0:T(8,128)(2,1)}, bf16[4,256,1408]{2,1,0:T(8,128)(2,1)}, u32[]{:S(2)}, u32[]{:S(2)}) %collective-permute-start.39) | collective-permute-done | bytes 2883616 | tf_op jit(solution)/shard_map/ppermute | solution.py:26
  461.8 9.7 %block_products.12.refs_0_ = bf16[4,256,1408]{2,1,0:T(8,128)(2,1)} custom-call(s32[1]{0:T(128)} %bitcast.26.where, bf16[768,2048]{1,0:T(8,128)(2,1)} %get-tuple-element.43.normed_ref.refs_0_, bf16[768,2048]{1,0:T(8,128)(2,1)} %collective-permute-done.32.refs_1_, bf16[768,2816]{1,0:T(8,128)(2,1)} %get-tuple-element.47.kept_ref.refs_2_, ...), custom_call_target="tpu_custom_call" | custom-call | flops 8999999488 | bytes 1350000 | tf_op jit(solution)/shard_map/block_products/pallas_call | solution.py:704
  471.5 12.4 %norm_back.1 = (f32[768,2048]{1,0:T(8,128)}, f32[1,2048]{1,0:T(1,128)}, bf16[768,2048]{1,0:T(8,128)(2,1)}) custom-call(f32[768,2048]{1,0:T(8,128)} %get-tuple-element.42.residual_ref.value_ref, f32[1,2048]{1,0:T(1,128)} %bitcast.162, bf16[768,2048]{1,0:T(8,128)(2,1)} %bitcast.142, bf16[768,512]{1,0:T(8,128)(2,1)} %feed_input.4.refs_4_.refs_0_, ...), custom_call_target="tpu_custom_call" | custom-call | flops 359999995904 | bytes 54000000 | tf_op jit(solution)/shard_map/norm_back/pallas_call | solution.py:404
  494.3 11.8 %attend_back.3 = (bf16[1024,256]{1,0:T(8,128)(2,1)S(1)}, bf16[4,128,256]{2,1,0:T(8,128)(2,1)S(1)}, bf16[4,128,256]{2,1,0:T(8,128)(2,1)S(1)}) custom-call(s32[2]{0:T(128)S(1)} %copy-done.47, bf16[1024,768]{1,0:T(8,128)(2,1)S(1)} %bitcast.98, bf16[4,256,768]{2,1,0:T(8,128)(2,1)S(1)} %pad_maximum_fusion.4.refs_2_.refs_3_, ...), custom_call_target="tpu_custom_call" | custom-call | flops 160000000000 | bytes 24000000 | tf_op jit(solution)/shard_map/attend_back/pallas_call | solution.py:622
  532.1 9.7 %block_products.14.refs_0_ = bf16[4,256,1408]{2,1,0:T(8,128)(2,1)} custom-call(s32[1]{0:T(128)} %bitcast.26.where, bf16[768,2048]{1,0:T(8,128)(2,1)} %get-tuple-element.43.normed_ref.refs_0_, bf16[768,2048]{1,0:T(8,128)(2,1)} %collective-permute-done.32.refs_1_, bf16[768,2816]{1,0:T(8,128)(2,1)} %get-tuple-element.47.kept_ref.refs_2_, ...), custom_call_target="tpu_custom_call" | custom-call | flops 8999999488 | bytes 1350000 | tf_op jit(solution)/shard_map/block_products/pallas_call | solution.py:704
  541.9 9.7 %collective-permute-done.43.refs_4_.refs_1_ = bf16[4,512,256]{2,1,0:T(8,128)(2,1)} collective-permute-done((bf16[4,512,256]{2,1,0:T(8,128)(2,1)}, bf16[4,512,256]{2,1,0:T(8,128)(2,1)}, u32[]{:S(2)}, u32[]{:S(2)}) %collective-permute-start.43) | collective-permute-done | bytes 1048608 | tf_op jit(solution)/shard_map/ppermute | solution.py:26
  554.9 11.9 %attend_back.4 = (bf16[1024,256]{1,0:T(8,128)(2,1)S(1)}, bf16[4,128,256]{2,1,0:T(8,128)(2,1)S(1)}, bf16[4,128,256]{2,1,0:T(8,128)(2,1)S(1)}) custom-call(s32[2]{0:T(128)S(1)} %copy-done.45, bf16[1024,768]{1,0:T(8,128)(2,1)S(1)} %bitcast.99, bf16[4,256,768]{2,1,0:T(8,128)(2,1)S(1)} %pad_maximum_fusion.4.refs_2_.refs_3_, ...), custom_call_target="tpu_custom_call" | custom-call | flops 160000000000 | bytes 24000000 | tf_op jit(solution)/shard_map/attend_back/pallas_call | solution.py:622
  594.5 11.1 %reduce-scatter.8.cloned.1.call-done = bf16[1,256,1408]{2,1,0:T(8,128)(2,1)} async-done(((bf16[4,256,1408]{2,1,0:T(8,128)(2,1)}), bf16[1,256,1408]{2,1,0:T(8,128)(2,1)}) %reduce-scatter.8.cloned.1.call-update) | async-done | bytes 720912 | tf_op jit(solution)/shard_map/reduce_scatter | solution.py:750
  610.4 12.4 %attend_back.5 = (bf16[1024,256]{1,0:T(8,128)(2,1)S(1)}, bf16[4,128,256]{2,1,0:T(8,128)(2,1)S(1)}, bf16[4,128,256]{2,1,0:T(8,128)(2,1)S(1)}) custom-call(s32[2]{0:T(128)S(1)} %copy-done.49, bf16[1024,768]{1,0:T(8,128)(2,1)} %bitcast.94, bf16[4,256,768]{2,1,0:T(8,128)(2,1)} %copy-done, bf16[4,256,768]{2,1,0:T(8,128)(2,1)} %copy-done, ...), custom_call_target="tpu_custom_call" | custom-call | flops 160000000000 | bytes 24000000 | tf_op jit(solution)/shard_map/attend_back/pallas_call | solution.py:622
  699.2 16.6 %collective-permute-done.57 = bf16[512,128]{1,0:T(8,128)(2,1)} collective-permute-done((bf16[512,128]{1,0:T(8,128)(2,1)}, bf16[512,128]{1,0:T(8,128)(2,1)}, u32[]{:S(2)}, u32[]{:S(2)}) %collective-permute-start.57) | collective-permute-done | bytes 131104 | tf_op jit(solution)/shard_map/ppermute | solution.py:758
  738.4 13.3 %norm_back_rows.1 = (f32[768,2048]{1,0:T(8,128)}, f32[1,2048]{1,0:T(1,128)}) custom-call(bf16[768,2048]{1,0:T(8,128)(2,1)} %bitcast.105, f32[768,2048]{1,0:T(8,128)} %fusion.5.term_ref, f32[1,2048]{1,0:T(1,128)} %bitcast.160, f32[768,2048]{1,0:T(8,128)} %get-tuple-element.63.base_ref, bf16[256,2048]{1,0:T(8,128)(2,1)} %product.13.refs_4_.refs_0_, ...), custom_call_target="tpu_custom_call" | custom-call | flops 12999999488 | bytes 1950000 | tf_op jit(solution)/shard_map/norm_back_rows/pallas_call | solution.py:452
  761.1 10.8 %collective-permute-done.54 = bf16[512,512]{1,0:T(8,128)(2,1)} collective-permute-done((bf16[512,512]{1,0:T(8,128)(2,1)S(1)}, bf16[512,512]{1,0:T(8,128)(2,1)}, u32[]{:S(2)}, u32[]{:S(2)}) %collective-permute-start.54) | collective-permute-done | bytes 524320 | tf_op jit(solution)/shard_map/ppermute | solution.py:26
  (507 shorter events, 359.8 us)
Async XLA Ops:
  7.2 75.2 %all-gather.9.cloned.1.call-start = ((), (), s32[]{:S(2)}) async-start(), calls=%async_computation.10 | async-start | bytes 1310720 | tf_op jit(solution)/shard_map/all_gather | solution.py:825
  14.6 30.1 %collective-permute-start.2 = (bf16[128,1408]{1,0:T(8,128)(2,1)S(1)}, bf16[128,1408]{1,0:T(8,128)(2,1)S(1)}, u32[]{:S(2)}, u32[]{:S(2)}) collective-permute-start(bf16[128,1408]{1,0:T(8,128)(2,1)S(1)} %constant_dynamic-slice_fusion.25), channel_id=1, source_target_pairs={{0,8},{8,16},{16,24},{24,0},{1,9},{9,17},{17,25},{25,1},{2,10},{10... | collective-permute-start | bytes 1081352 | tf_op jit(solution)/shard_map/ppermute | solution.py:818
  45.6 98.4 %all-gather.11.cloned.1.call-start = ((), (), s32[]{:S(2)}) async-start(), calls=%async_computation.11 | async-start | bytes 3604480 | tf_op jit(solution)/shard_map/all_gather | solution.py:825
  47.7 148.2 %all-gather.13.cloned.1.call-start = ((), (), s32[]{:S(2)}) async-start(), calls=%async_computation.12 | async-start | bytes 3604480 | tf_op jit(solution)/shard_map/all_gather | solution.py:825
  50.0 205.2 %all-gather.15.cloned.1.call-start = ((), (), s32[]{:S(2)}) async-start(), calls=%async_computation.13 | async-start | bytes 3604480 | tf_op jit(solution)/shard_map/all_gather | solution.py:825
  82.3 389.2 %reduce-scatter.6.cloned.1.call-start = ((), (), s32[]{:S(2)}) async-start(), calls=%async_computation.5 | async-start | bytes 7208960 | tf_op jit(solution)/shard_map/reduce_scatter | solution.py:750
  147.9 111.7 %collective-permute-start.21 = (bf16[3,128,2816]{2,1,0:T(8,128)(2,1)}, bf16[3,128,2816]{2,1,0:T(8,128)(2,1)}, u32[]{:S(2)}, u32[]{:S(2)}) collective-permute-start(bf16[3,128,2816]{2,1,0:T(8,128)(2,1)} %pad_maximum_fusion.refs_5_.refs_1_), channel_id=1, source_target_pairs={{0,4},{4,0},{2,6},{6,2},{1,5},{5,1},{3,7},{7,3},{8,12},{12,8},{10,... | collective-permute-start | bytes 6488072 | tf_op jit(solution)/shard_map/ppermute | solution.py:26
  165.4 36.8 %collective-permute-start.18 = (bf16[256,2048]{1,0:T(8,128)(2,1)}, bf16[256,2048]{1,0:T(8,128)(2,1)}, u32[]{:S(2)}, u32[]{:S(2)}) collective-permute-start(bf16[256,2048]{1,0:T(8,128)(2,1)} %product.8.refs_5_.refs_0_), channel_id=1, source_target_pairs={{0,1},{1,0},{2,3},{3,2},{4,5},{5,4},{6,7},{7,6},{8,9},{9,8},{10,11... | collective-permute-start | bytes 3145736 | tf_op jit(solution)/shard_map/ppermute | solution.py:883
  199.2 61.5 %collective-permute-start.25 = (bf16[3,128,2816]{2,1,0:T(8,128)(2,1)}, bf16[3,128,2816]{2,1,0:T(8,128)(2,1)}, u32[]{:S(2)}, u32[]{:S(2)}) collective-permute-start(bf16[3,128,2816]{2,1,0:T(8,128)(2,1)} %pad_maximum_fusion.1.refs_6_), channel_id=1, source_target_pairs={{0,4},{4,0},{2,6},{6,2},{1,5},{5,1},{3,7},{7,3},{8,12},{12,8},{10,... | collective-permute-start | bytes 6488072 | tf_op jit(solution)/shard_map/ppermute | solution.py:26
  231.4 37.9 %collective-permute-start.22 = (bf16[3,128,2816]{2,1,0:T(8,128)(2,1)}, bf16[3,128,2816]{2,1,0:T(8,128)(2,1)}, u32[]{:S(2)}, u32[]{:S(2)}) collective-permute-start(bf16[3,128,2816]{2,1,0:T(8,128)(2,1)} %pad_maximum_fusion.refs_5_.refs_1_), channel_id=1, source_target_pairs={{0,2},{2,0},{4,6},{6,4},{1,3},{3,1},{5,7},{7,5},{8,10},{10,8},{12,... | collective-permute-start | bytes 6488072 | tf_op jit(solution)/shard_map/ppermute | solution.py:22
  233.5 35.8 %collective-permute-start.24 = (bf16[3,128,2816]{2,1,0:T(8,128)(2,1)}, bf16[3,128,2816]{2,1,0:T(8,128)(2,1)}, u32[]{:S(2)}, u32[]{:S(2)}) collective-permute-start(bf16[3,128,2816]{2,1,0:T(8,128)(2,1)} %pad_maximum_fusion.1.refs_6_), channel_id=1, source_target_pairs={{0,2},{2,0},{4,6},{6,4},{1,3},{3,1},{5,7},{7,5},{8,10},{10,8},{12,... | collective-permute-start | bytes 6488072 | tf_op jit(solution)/shard_map/ppermute | solution.py:22
  258.4 48.2 %collective-permute-start.27 = (bf16[3,704,512]{2,1,0:T(8,128)(2,1)}, bf16[3,704,512]{2,1,0:T(8,128)(2,1)}, u32[]{:S(2)}, u32[]{:S(2)}) collective-permute-start(bf16[3,704,512]{2,1,0:T(8,128)(2,1)} %pad_maximum_fusion.2.refs_7_.refs_0_), channel_id=1, source_target_pairs={{0,4},{4,0},{2,6},{6,2},{1,5},{5,1},{3,7},{7,3},{8,12},{12,8},{10,... | collective-permute-start | bytes 6488072 | tf_op jit(solution)/shard_map/ppermute | solution.py:26
  315.8 197.7 %collective-permute-start.40 = (bf16[512,768]{1,0:T(8,128)(2,1)}, bf16[512,768]{1,0:T(8,128)(2,1)}, u32[]{:S(2)}, u32[]{:S(2)}) collective-permute-start(bf16[512,768]{1,0:T(8,128)(2,1)} %get-tuple-element.95), channel_id=1, source_target_pairs={{0,2},{2,0},{4,6},{6,4},{1,3},{3,1},{5,7},{7,5},{8,10},{10,8},{12,... | collective-permute-start | bytes 2359304 | tf_op jit(solution)/shard_map/ppermute | solution.py:22
  320.0 57.5 %collective-permute-start.32 = (bf16[768,2048]{1,0:T(8,128)(2,1)}, bf16[768,2048]{1,0:T(8,128)(2,1)}, u32[]{:S(2)}, u32[]{:S(2)}) collective-permute-start(bf16[768,2048]{1,0:T(8,128)(2,1)} %get-tuple-element.43.normed_ref.refs_0_), channel_id=1, source_target_pairs={{0,2},{2,0},{4,6},{6,4},{1,3},{3,1},{5,7},{7,5},{8,10},{10,8},{12,... | collective-permute-start | bytes 9437192 | tf_op jit(solution)/shard_map/ppermute | solution.py:22
  336.3 255.7 %reduce-scatter.14.cloned.1.call-start = ((), (), s32[]{:S(2)}) async-start(), calls=%async_computation.9 | async-start | bytes 3604480 | tf_op jit(solution)/shard_map/reduce_scatter | solution.py:750
  396.9 63.7 %collective-permute-start.39 = (bf16[4,256,1408]{2,1,0:T(8,128)(2,1)}, bf16[4,256,1408]{2,1,0:T(8,128)(2,1)}, u32[]{:S(2)}, u32[]{:S(2)}) collective-permute-start(bf16[4,256,1408]{2,1,0:T(8,128)(2,1)} %tie.33.rest_0_), channel_id=1, source_target_pairs={{0,4},{4,0},{2,6},{6,2},{1,5},{5,1},{3,7},{7,3},{8,12},{12,8},{10,... | collective-permute-start | bytes 8650760 | tf_op jit(solution)/shard_map/ppermute | solution.py:26
  408.4 53.4 %collective-permute-start.37 = (bf16[768,512]{1,0:T(8,128)(2,1)}, bf16[768,512]{1,0:T(8,128)(2,1)}, u32[]{:S(2)}, u32[]{:S(2)}) collective-permute-start(bf16[768,512]{1,0:T(8,128)(2,1)} %feed_input.6.rest_0_.refs_4_.refs_2_), channel_id=1, source_target_pairs={{0,1},{1,0},{2,3},{3,2},{4,5},{5,4},{6,7},{7,6},{8,9},{9,8},{10,11... | collective-permute-start | bytes 2359304 | tf_op jit(solution)/shard_map/ppermute | solution.py:921
  428.9 42.6 %collective-permute-start.38 = (bf16[768,512]{1,0:T(8,128)(2,1)}, bf16[768,512]{1,0:T(8,128)(2,1)}, u32[]{:S(2)}, u32[]{:S(2)}) collective-permute-start(bf16[768,512]{1,0:T(8,128)(2,1)} %feed_input.7.rest_0_.refs_3_), channel_id=1, source_target_pairs={{0,1},{1,0},{2,3},{3,2},{4,5},{5,4},{6,7},{7,6},{8,9},{9,8},{10,11... | collective-permute-start | bytes 2359304 | tf_op jit(solution)/shard_map/ppermute | solution.py:921
  443.7 109.0 %collective-permute-start.36 = (bf16[768,2048]{1,0:T(8,128)(2,1)}, bf16[768,2048]{1,0:T(8,128)(2,1)}, u32[]{:S(2)}, u32[]{:S(2)}) collective-permute-start(bf16[768,2048]{1,0:T(8,128)(2,1)} %product.11.mine_ref.refs_5_.refs_8_), channel_id=1, source_target_pairs={{0,1},{1,0},{2,3},{3,2},{4,5},{5,4},{6,7},{7,6},{8,9},{9,8},{10,11... | collective-permute-start | bytes 9437192 | tf_op jit(solution)/shard_map/ppermute | solution.py:931
  460.6 62.8 %collective-permute-start.42 = (bf16[4,256,1408]{2,1,0:T(8,128)(2,1)}, bf16[4,256,1408]{2,1,0:T(8,128)(2,1)}, u32[]{:S(2)}, u32[]{:S(2)}) collective-permute-start(bf16[4,256,1408]{2,1,0:T(8,128)(2,1)} %tie.34.refs_6_), channel_id=1, source_target_pairs={{0,4},{4,0},{2,6},{6,2},{1,5},{5,1},{3,7},{7,3},{8,12},{12,8},{10,... | collective-permute-start | bytes 8650760 | tf_op jit(solution)/shard_map/ppermute | solution.py:26
  493.1 112.5 %reduce-scatter.8.cloned.1.call-start = ((), (), s32[]{:S(2)}) async-start(), calls=%async_computation.6 | async-start | bytes 3604480 | tf_op jit(solution)/shard_map/reduce_scatter | solution.py:750
  529.3 39.8 %collective-permute-start.44 = (bf16[256,2048]{1,0:T(8,128)(2,1)}, bf16[256,2048]{1,0:T(8,128)(2,1)}, u32[]{:S(2)}, u32[]{:S(2)}) collective-permute-start(bf16[256,2048]{1,0:T(8,128)(2,1)} %product.13.refs_4_.refs_0_), channel_id=1, source_target_pairs={{0,1},{1,0},{2,3},{3,2},{4,5},{5,4},{6,7},{7,6},{8,9},{9,8},{10,11... | collective-permute-start | bytes 3145736 | tf_op jit(solution)/shard_map/ppermute | solution.py:958
  541.9 105.8 %reduce-scatter.10.cloned.1.call-start = ((), (), s32[]{:S(2)}) async-start(), calls=%async_computation.7 | async-start | bytes 1310720 | tf_op jit(solution)/shard_map/reduce_scatter | solution.py:750
  551.6 42.4 %collective-permute-start.46 = (bf16[2816,256]{1,0:T(8,128)(2,1)}, bf16[2816,256]{1,0:T(8,128)(2,1)}, u32[]{:S(2)}, u32[]{:S(2)}) collective-permute-start(bf16[2816,256]{1,0:T(8,128)(2,1)} %tie.38), channel_id=1, source_target_pairs={{0,4},{4,0},{2,6},{6,2},{1,5},{5,1},{3,7},{7,3},{8,12},{12,8},{10,... | collective-permute-start | bytes 4325384 | tf_op jit(solution)/shard_map/ppermute | solution.py:26
  574.2 31.5 %collective-permute-start.45 = (bf16[256,2048]{1,0:T(8,128)(2,1)}, bf16[256,2048]{1,0:T(8,128)(2,1)S(1)}, u32[]{:S(2)}, u32[]{:S(2)}) collective-permute-start(bf16[256,2048]{1,0:T(8,128)(2,1)} %product.14.refs_5_.refs_1_), channel_id=1, source_target_pairs={{0,1},{1,0},{2,3},{3,2},{4,5},{5,4},{6,7},{7,6},{8,9},{9,8},{10,11... | collective-permute-start | bytes 3145736 | tf_op jit(solution)/shard_map/ppermute | solution.py:958
  574.4 73.3 %collective-permute-start.48 = (bf16[768,2048]{1,0:T(8,128)(2,1)}, bf16[768,2048]{1,0:T(8,128)(2,1)}, u32[]{:S(2)}, u32[]{:S(2)}) collective-permute-start(bf16[768,2048]{1,0:T(8,128)(2,1)} %copy-done.71), channel_id=1, source_target_pairs={{0,2},{2,0},{4,6},{6,4},{1,3},{3,1},{5,7},{7,5},{8,10},{10,8},{12,... | collective-permute-start | bytes 9437192 | tf_op jit(solution)/shard_map/ppermute | solution.py:22
  594.0 33.0 %collective-permute-start.63 = (bf16[256,1408]{1,0:T(8,128)(2,1)}, bf16[256,1408]{1,0:T(8,128)(2,1)}, u32[]{:S(2)}, u32[]{:S(2)}) collective-permute-start(bf16[256,1408]{1,0:T(8,128)(2,1)} %tie.41), channel_id=1, source_target_pairs={{0,4},{4,0},{2,6},{6,2},{1,5},{5,1},{3,7},{7,3},{8,12},{12,8},{10,... | collective-permute-start | bytes 2162696 | tf_op jit(solution)/shard_map/ppermute | solution.py:26
  605.7 132.7 %reduce-scatter.12.cloned.1.call-start = ((), (), s32[]{:S(2)}) async-start(), calls=%async_computation.8 | async-start | bytes 2621440 | tf_op jit(solution)/shard_map/reduce_scatter | solution.py:750
  629.6 37.2 %collective-permute-start.64 = (bf16[512,1408]{1,0:T(8,128)(2,1)}, bf16[512,1408]{1,0:T(8,128)(2,1)}, u32[]{:S(2)}, u32[]{:S(2)}) collective-permute-start(bf16[512,1408]{1,0:T(8,128)(2,1)} %pad_maximum_fusion.6), channel_id=1, source_target_pairs={{0,2},{2,0},{4,6},{6,4},{1,3},{3,1},{5,7},{7,5},{8,10},{10,8},{12,... | collective-permute-start | bytes 4325384 | tf_op jit(solution)/shard_map/ppermute | solution.py:22
  670.2 68.2 %collective-permute-start.52 = (bf16[256,2048]{1,0:T(8,128)(2,1)}, bf16[256,2048]{1,0:T(8,128)(2,1)}, u32[]{:S(2)}, u32[]{:S(2)}) collective-permute-start(bf16[256,2048]{1,0:T(8,128)(2,1)} %product.15.refs_4_.refs_2_), channel_id=1, source_target_pairs={{0,1},{1,0},{2,3},{3,2},{4,5},{5,4},{6,7},{7,6},{8,9},{9,8},{10,11... | collective-permute-start | bytes 3145736 | tf_op jit(solution)/shard_map/ppermute | solution.py:958
  672.3 46.3 %collective-permute-start.65 = (bf16[256,1408]{1,0:T(8,128)(2,1)}, bf16[256,1408]{1,0:T(8,128)(2,1)}, u32[]{:S(2)}, u32[]{:S(2)}) collective-permute-start(bf16[256,1408]{1,0:T(8,128)(2,1)} %tie.42), channel_id=1, source_target_pairs={{0,4},{4,0},{2,6},{6,2},{1,5},{5,1},{3,7},{7,3},{8,12},{12,8},{10,... | collective-permute-start | bytes 2162696 | tf_op jit(solution)/shard_map/ppermute | solution.py:26
  698.8 33.2 %collective-permute-start.62 = (bf16[512,512]{1,0:T(8,128)(2,1)S(1)}, bf16[512,512]{1,0:T(8,128)(2,1)S(1)}, u32[]{:S(2)}, u32[]{:S(2)}) collective-permute-start(bf16[512,512]{1,0:T(8,128)(2,1)S(1)} %copy-done.77), channel_id=1, source_target_pairs={{0,2},{2,0},{4,6},{6,4},{1,3},{3,1},{5,7},{7,5},{8,10},{10,8},{12,... | collective-permute-start | bytes 1572872 | tf_op jit(solution)/shard_map/ppermute | solution.py:22
  (147 other events, 2209.4 us)
Sparse Core Ops, SparseCore 0:
  45.7 29.9 all-gather.8
  77.8 58.5 all-gather.10
  138.0 57.8 all-gather.12
  197.3 57.8 all-gather.14
  336.4 100.6 reduce-scatter.5
  493.3 53.9 reduce-scatter.13
  549.6 56.0 reduce-scatter.7
  608.5 26.9 reduce-scatter.9
  672.4 51.0 reduce-scatter.11

commit v5 on v4

--- a/solution.py
+++ b/solution.py
@@ -750,13 +750,13 @@
     return lax.psum_scatter(total, "shard", scatter_dimension=0, tiled=True)[0]
 
 
-def directly_over_shard(total, me):
+def directly_over_shard(total, me, after):
     shards = total.shape[0]
     result = lax.dynamic_index_in_dim(total, me, 0, False).astype(f32)
     for k in range(1, shards):
         block = lax.dynamic_index_in_dim(total, (me + k) % shards, 0, False)
         came = lax.ppermute(block, "shard", [(i, (i + k) % shards) for i in range(shards)])
-        result = result + came.astype(f32)
+        result = result + tie(came, after).astype(f32)
     return result.astype(bf16)
 
 
@@ -966,7 +966,7 @@
             output_tied = tie(output.total, gate_up_second)
             down_came = high_swap(tie(down_sum, output.came))
             first_came = high_swap(tie(gate_up_first, down_came))
-            last = [output.total, came[0], came[1], down_came] + [output_tied]
+            last = [output.total, came[0], came[1], down_came]
 
     part_sum = jnp.concatenate(part_sums, 2).reshape(2, 2, 2 * kv_width, tokens)
     sent = lax.dynamic_index_in_dim(part_sum, 1 - high, 0, False)
@@ -1003,11 +1003,15 @@
     keyval_term = dot(keyval_both, keyval_weight, 0, 1)
 
     input_grad, attn_gain_term = norm_back_rows(
-        acts, mine, came, keyval_term, gain_one, residual_delta, [keyval_products, query_sum]
+        acts, mine, came, keyval_term, gain_one, residual_delta, [keyval_products]
     )
     block_out = add_three(residual, ffn_mine, ffn_came, [])
     block_out = block_out.reshape(activations.shape)
-    keyval_sum = directly_over_shard(keyval_products, me) if shards <= 4 else over_shard(keyval_products)
+    keyval_sum = (
+        directly_over_shard(keyval_products, me, input_grad)
+        if shards <= 4
+        else over_shard(keyval_products)
+    )
 
     second_came = high_swap(tie(gate_up_second, part_came))
 
@@ -1015,7 +1019,7 @@
         other = low_swap(value)
         return pick(low, value, other).astype(f32), pick(low, other, value).astype(f32)
 
-    down_sum = (down_sum.astype(f32) + tie(down_came, keyval_products).astype(f32)).astype(bf16)
+    down_sum = (down_sum.astype(f32) + tie(down_came, input_grad).astype(f32)).astype(bf16)
     down_grad = jnp.concatenate(two_sides(down_sum), 1)
     first_gate, first_up = two_sides(halves(high, gate_up_first, 0, first_came))
     second_gate, second_up = two_sides(halves(high, gate_up_second, 0, second_came))
@@ -1026,7 +1030,7 @@
     def high_total(value):
         return (value.astype(f32) + high_swap(value).astype(f32)).astype(bf16)
 
-    query_grad = jnp.concatenate(two_sides(high_total(query_sum)), 1)
+    query_grad = jnp.concatenate(two_sides(high_total(tie(query_sum, input_grad))), 1)
     key_grad, value_grad = two_sides(high_total(keyval_sum))
 
     gain_terms = jnp.concatenate([attn_gain_term, ffn_gain_term], 0)

time: 794 us -> 781 us (0.984)
  waiting for transfers between devices: 202 us -> 155 us
  starting transfers between devices: 74.5 us -> 98.7 us
  other arithmetic: 61.5 us -> 70.5 us
    ppermute x3, waiting for transfers between devices: 22.6 us -> 0.01 us  [directly_over_shard(): lax.ppermute(block, 'shard', [(i, (i + k) % shards) for i in range(shards)])]
    ppermute x19, starting transfers between devices: 29.6 us -> 44.5 us  [high_swap(): return lax.ppermute(value, 'ctx', SWAP_HIGH)]
    reduce_scatter x5, waiting for transfers between devices: 11.2 us -> 1.11 us  [over_shard(): return lax.psum_scatter(total, 'shard', scatter_dimension=0, tiled=True)[0]]
    unnamed x199 -> x211, local copies, waits for them, and re-layouts: 37 us -> 40.6 us
  transfers between devices with their start and end apart: 82 -> 82, of which waited for: 22 -> 20; matrix products, arithmetic and copies ran while one was open for 14% -> 15% of each run, Pallas kernels for 45% -> 45%
where the time goes in v5:
time: 781 us; the launch traced here: 776 us
  Pallas kernels  350 us (45%)
  waiting for transfers between devices  155 us (20%)
  starting transfers between devices  98.7 us (13%)
  local copies, waits for them, and re-layouts  78.1 us (10%)
  other arithmetic  70.5 us (9%)
  between operations  15.3 us (2%)
  matrix products  8.89 us (1%)
    pallas_call x9, Pallas kernels, block_products(): pl.pallas_call(kernel, out_shape=jax.ShapeDtypeStruct(out_shape, bf16), g...  78 us
    ppermute x19, waiting for transfers between devices, high_swap(): return lax.ppermute(value, 'ctx', SWAP_HIGH)  74.2 us
    pallas_call x8, Pallas kernels, product(): pl.pallas_call(kernel, out_shape=jax.ShapeDtypeStruct((rows, width), bf16...  52.9 us
    ppermute x19, starting transfers between devices, high_swap(): return lax.ppermute(value, 'ctx', SWAP_HIGH)  44.5 us
    unnamed x211, local copies, waits for them, and re-layouts  40.6 us
    pallas_call x4, Pallas kernels, feed_input(): pl.pallas_call(kernel, out_shape=jax.ShapeDtypeStruct((tokens, model_widt...  40.4 us
    pallas_call x3, Pallas kernels, attend_back(): pl.pallas_call(lambda *refs: attend_back_kernel(group, *refs), out_shape=...  36 us
    all_gather x4, waiting for transfers between devices, later(): lax.all_gather(tie(quarter(weight, ctx), *after), 'shard', axis=0, tiled=...  32.6 us
  transfers between devices with their start and end apart: 82, of which 20 were waited for; matrix products, arithmetic and copies ran while one was open for 15% of the time, Pallas kernels for 45%

profile of v5, /device:TPU:1, one launch (start us, length us, event | category | flops | bytes accessed | tf_op | source)
XLA Modules:
  0.0 776.5 jit_solution(4405825171615122783)
XLA Ops:
  21.7 23.0 %collective-permute-done.1 = bf16[128,1408]{1,0:T(8,128)(2,1)S(1)} collective-permute-done((bf16[128,1408]{1,0:T(8,128)(2,1)S(1)}, bf16[128,1408]{1,0:T(8,128)(2,1)S(1)}, u32[]{:S(2)}, u32[]{:S(2)}) %collective-permute-start.1) | collective-permute-done | bytes 360480 | tf_op jit(solution)/shard_map/ppermute | solution.py:818
  112.0 12.0 %collective-permute-done.13.refs_1_.refs_2_ = bf16[3,256,512]{2,1,0:T(8,128)(2,1)} collective-permute-done((bf16[3,256,512]{2,1,0:T(8,128)(2,1)}, bf16[3,256,512]{2,1,0:T(8,128)(2,1)}, u32[]{:S(2)}, u32[]{:S(2)}) %collective-permute-start.13) | collective-permute-done | bytes 786464 | tf_op jit(solution)/shard_map/ppermute | solution.py:26
  149.2 10.0 %attend.3 = (bf16[1024,256]{1,0:T(8,128)(2,1)S(1)}, f32[2,8,256]{2,1,0:T(8,128)S(1)}) custom-call(s32[2]{0:T(128)S(1)} %get-tuple-element.142.refs_0_, bf16[1024,768]{1,0:T(8,128)(2,1)S(1)} %bitcast.94, bf16[4,256,768]{2,1,0:T(8,128)(2,1)S(1)} %pad_maximum_fusion.4.refs_2_.refs_3_, bf16[4,256,768]{2,1,0:T(8,128)(2,1)S(1)} %pad_maximum_fusion.4.refs_2_.refs_3_, ...), custom_call_target="tpu_custom_call" | custom-call | flops 420000000 | bytes 63000 | tf_op jit(solution)/shard_map/attend/pallas_call | solution.py:522
  167.9 10.0 %attend.4 = (bf16[1024,256]{1,0:T(8,128)(2,1)S(1)}, f32[2,8,256]{2,1,0:T(8,128)S(1)}) custom-call(s32[2]{0:T(128)S(1)} %get-tuple-element.143.refs_0_, bf16[1024,768]{1,0:T(8,128)(2,1)S(1)} %bitcast.95, bf16[4,256,768]{2,1,0:T(8,128)(2,1)S(1)} %pad_maximum_fusion.4.refs_2_.refs_3_, bf16[4,256,768]{2,1,0:T(8,128)(2,1)S(1)} %pad_maximum_fusion.4.refs_2_.refs_3_, ...), custom_call_target="tpu_custom_call" | custom-call | flops 420000000 | bytes 63000 | tf_op jit(solution)/shard_map/attend/pallas_call | solution.py:522
  183.7 12.2 %all-gather.13.cloned.1.call-done = bf16[512,2816]{1,0:T(8,128)(2,1)} async-done(((bf16[128,2816]{1,0:T(8,128)(2,1)}), bf16[512,2816]{1,0:T(8,128)(2,1)}) %all-gather.13.cloned.1.call-update) | async-done | bytes 2883600 | tf_op jit(solution)/shard_map/all_gather | solution.py:825
  207.4 10.0 %attend.5 = (bf16[1024,256]{1,0:T(8,128)(2,1)S(1)}, f32[2,8,256]{2,1,0:T(8,128)S(1)}) custom-call(s32[2]{0:T(128)S(1)} %pad_add_fusion.3.refs_0_, bf16[1024,768]{1,0:T(8,128)(2,1)S(1)} %bitcast.96, bf16[4,256,768]{2,1,0:T(8,128)(2,1)S(1)} %pad_maximum_fusion.4.refs_2_.refs_3_, bf16[4,256,768]{2,1,0:T(8,128)(2,1)S(1)} %pad_maximum_fusion.4.refs_2_.refs_3_, ...), custom_call_target="tpu_custom_call" | custom-call | flops 420000000 | bytes 63000 | tf_op jit(solution)/shard_map/attend/pallas_call | solution.py:522
  218.2 8.9 %collective-permute-done.19.rest_0_.refs_4_ = bf16[256,2048]{1,0:T(8,128)(2,1)S(1)} collective-permute-done((bf16[256,2048]{1,0:T(8,128)(2,1)S(1)}, bf16[256,2048]{1,0:T(8,128)(2,1)S(1)}, u32[]{:S(2)}, u32[]{:S(2)}) %collective-permute-start.19) | collective-permute-done | bytes 1048608 | tf_op jit(solution)/shard_map/ppermute | solution.py:883
  234.9 20.3 %all-gather.15.cloned.1.call-done = bf16[2816,512]{1,0:T(8,128)(2,1)} async-done(((bf16[704,512]{1,0:T(8,128)(2,1)}), bf16[2816,512]{1,0:T(8,128)(2,1)}) %all-gather.15.cloned.1.call-update) | async-done | bytes 2883600 | tf_op jit(solution)/shard_map/all_gather | solution.py:825
  260.7 8.5 %add_and_norm.1 = (f32[768,2048]{1,0:T(8,128)}, bf16[768,2048]{1,0:T(8,128)(2,1)}) custom-call(bf16[768,2048]{1,0:T(8,128)(2,1)} %bitcast.104, f32[1,2048]{1,0:T(1,128)} %bitcast.160, bf16[256,2048]{1,0:T(8,128)(2,1)} %product.8.refs_5_.refs_0_, bf16[256,2048]{1,0:T(8,128)(2,1)} %product.9.refs_1_.refs_5_, bf16[256,2048]{1,0:T(8,128)(2,1)} %product.10.refs_1_.refs_2_, ...), custom_call_target="tpu_custom_call" | custom-call | flops 89999998976 | bytes 13500000 | tf_op jit(solution)/shard_map/add_and_norm/pallas_call | solution.py:329
  270.6 28.7 %feed_forward.1 = (bf16[768,2816]{1,0:T(8,128)(2,1)}, bf16[768,2816]{1,0:T(8,128)(2,1)}, bf16[768,2816]{1,0:T(8,128)(2,1)}, bf16[2,2048,2816]{2,1,0:T(8,128)(2,1)}) custom-call(s32[2]{0:T(128)} %pad_add_fusion.where, bf16[768,2048]{1,0:T(8,128)(2,1)} %get-tuple-element.43.normed_ref.refs_0_, bf16[4,128,2816]{2,1,0:T(8,128)(2,1)} %bitcast.155, ...), custom_call_target="tpu_custom_call" | custom-call | flops 28999999488 | bytes 4350000 | tf_op jit(solution)/shard_map/feed_forward/pallas_call | solution.py:185
  320.4 15.8 %block_products.9.refs_4_ = bf16[4,2816,256]{2,1,0:T(8,128)(2,1)} custom-call(s32[1]{0:T(128)} %bitcast.22.where, bf16[768,2816]{1,0:T(8,128)(2,1)} %tie.36.refs_0_.left_ref, bf16[768,2816]{1,0:T(8,128)(2,1)} %collective-permute-done.30.refs_1_, bf16[768,2048]{1,0:T(8,128)(2,1)} %bitcast.140, bf16[768,2048]{1,0:T(8,128)(2,1)} %collective-permute-done.31.refs_3_), custom_call_target="tpu_custom_call" | custom-call | flops 8999999488 | bytes 1350000 | tf_op jit(solution)/shard_map/block_products/pallas_call | solution.py:704
  336.4 10.6 %place.5.down_ref.right_ref = bf16[2816,2048]{1,0:T(8,128)(2,1)} custom-call(s32[2]{0:T(128)} %pad_add_fusion.where, bf16[4,704,512]{2,1,0:T(8,128)(2,1)} %bitcast.157, bf16[3,704,512]{2,1,0:T(8,128)(2,1)} %pad_maximum_fusion.2.refs_7_.refs_0_, bf16[3,704,512]{2,1,0:T(8,128)(2,1)} %collective-permute-done.28.refs_1_, ...), custom_call_target="tpu_custom_call" | custom-call | flops 240000008192 | bytes 36000000 | tf_op jit(solution)/shard_map/place/pallas_call | solution.py:130
  347.0 19.2 %feed_back.1 = (bf16[768,2816]{1,0:T(8,128)(2,1)}, bf16[768,2816]{1,0:T(8,128)(2,1)}) custom-call(s32[1]{0:T(128)} %bitcast.22.where, bf16[768,2048]{1,0:T(8,128)(2,1)} %bitcast.141, bf16[2816,2048]{1,0:T(8,128)(2,1)} %place.5.down_ref.right_ref, bf16[768,2816]{1,0:T(8,128)(2,1)} %get-tuple-element.45.gate_ref, bf16[768,2816]{1,0:T(8,128)(2,1)} %get-tuple-element.46.up_ref), custom_call_target="tpu_custom_call" | custom-call | flops 5699999744 | bytes 855000 | tf_op jit(solution)/shard_map/feed_back/pallas_call | solution.py:233
  366.4 10.1 %feed_input.4.refs_4_.refs_0_ = bf16[768,512]{1,0:T(8,128)(2,1)} custom-call(s32[1]{0:T(128)} %bitcast.22.where, bf16[768,2816]{1,0:T(8,128)(2,1)} %get-tuple-element.47.kept_ref.refs_2_, bf16[768,2816]{1,0:T(8,128)(2,1)} %get-tuple-element.48.given_ref, bf16[2,2048,2816]{2,1,0:T(8,128)(2,1)} %get-tuple-element.49.kept_weight.given_weight, ...), custom_call_target="tpu_custom_call" | custom-call | flops 299999985664 | bytes 45000000 | tf_op jit(solution)/shard_map/feed_input/pallas_call | solution.py:264
  377.6 9.2 %block_products.10.refs_0_ = bf16[4,256,1408]{2,1,0:T(8,128)(2,1)} custom-call(s32[1]{0:T(128)} %bitcast.24.where, bf16[768,2048]{1,0:T(8,128)(2,1)} %get-tuple-element.43.normed_ref.refs_0_, bf16[768,2048]{1,0:T(8,128)(2,1)} %collective-permute-done.32.refs_1_, bf16[768,2816]{1,0:T(8,128)(2,1)} %get-tuple-element.47.kept_ref.refs_2_, ...), custom_call_target="tpu_custom_call" | custom-call | flops 8999999488 | bytes 1350000 | tf_op jit(solution)/shard_map/block_products/pallas_call | solution.py:704
  386.8 10.2 %feed_input.5.rest_0_.refs_1_ = bf16[768,512]{1,0:T(8,128)(2,1)} custom-call(s32[1]{0:T(128)} %bitcast.22.where, bf16[768,2816]{1,0:T(8,128)(2,1)} %get-tuple-element.47.kept_ref.refs_2_, bf16[768,2816]{1,0:T(8,128)(2,1)} %get-tuple-element.48.given_ref, bf16[2,2048,2816]{2,1,0:T(8,128)(2,1)} %get-tuple-element.49.kept_weight.given_weight, ...), custom_call_target="tpu_custom_call" | custom-call | flops 299999985664 | bytes 45000000 | tf_op jit(solution)/shard_map/feed_input/pallas_call | solution.py:264
  398.4 10.0 %feed_input.6.rest_0_.refs_4_.refs_2_ = bf16[768,512]{1,0:T(8,128)(2,1)} custom-call(s32[1]{0:T(128)} %bitcast.22.where, bf16[768,2816]{1,0:T(8,128)(2,1)} %get-tuple-element.47.kept_ref.refs_2_, bf16[768,2816]{1,0:T(8,128)(2,1)} %get-tuple-element.48.given_ref, bf16[2,2048,2816]{2,1,0:T(8,128)(2,1)} %get-tuple-element.49.kept_weight.given_weight, ...), custom_call_target="tpu_custom_call" | custom-call | flops 299999985664 | bytes 45000000 | tf_op jit(solution)/shard_map/feed_input/pallas_call | solution.py:264
  409.7 9.2 %block_products.11.refs_0_ = bf16[4,256,1408]{2,1,0:T(8,128)(2,1)} custom-call(s32[1]{0:T(128)} %bitcast.24.where, bf16[768,2048]{1,0:T(8,128)(2,1)} %get-tuple-element.43.normed_ref.refs_0_, bf16[768,2048]{1,0:T(8,128)(2,1)} %collective-permute-done.32.refs_1_, bf16[768,2816]{1,0:T(8,128)(2,1)} %get-tuple-element.47.kept_ref.refs_2_, ...), custom_call_target="tpu_custom_call" | custom-call | flops 8999999488 | bytes 1350000 | tf_op jit(solution)/shard_map/block_products/pallas_call | solution.py:704
  418.8 10.2 %feed_input.7.rest_0_.refs_3_ = bf16[768,512]{1,0:T(8,128)(2,1)} custom-call(s32[1]{0:T(128)} %bitcast.22.where, bf16[768,2816]{1,0:T(8,128)(2,1)} %get-tuple-element.47.kept_ref.refs_2_, bf16[768,2816]{1,0:T(8,128)(2,1)} %get-tuple-element.48.given_ref, bf16[2,2048,2816]{2,1,0:T(8,128)(2,1)} %get-tuple-element.49.kept_weight.given_weight, ...), custom_call_target="tpu_custom_call" | custom-call | flops 299999985664 | bytes 45000000 | tf_op jit(solution)/shard_map/feed_input/pallas_call | solution.py:264
  429.2 14.6 %product.11.mine_ref.refs_5_.refs_8_ = bf16[768,2048]{1,0:T(8,128)(2,1)} custom-call(bf16[768,2816]{1,0:T(8,128)(2,1)} %tie.36.refs_0_.left_ref, bf16[2816,2048]{1,0:T(8,128)(2,1)} %place.5.down_ref.right_ref, bf16[768,512]{1,0:T(8,128)(2,1)} %feed_input.7.rest_0_.refs_3_), custom_call_target="tpu_custom_call" | custom-call | flops 600000000 | bytes 90000 | tf_op jit(solution)/shard_map/product/pallas_call | solution.py:299
  445.0 15.7 %collective-permute-done.39.refs_1_.refs_4_ = bf16[4,256,1408]{2,1,0:T(8,128)(2,1)} collective-permute-done((bf16[4,256,1408]{2,1,0:T(8,128)(2,1)}, bf16[4,256,1408]{2,1,0:T(8,128)(2,1)}, u32[]{:S(2)}, u32[]{:S(2)}) %collective-permute-start.39) | collective-permute-done | bytes 2883616 | tf_op jit(solution)/shard_map/ppermute | solution.py:26
  461.9 9.7 %block_products.12.refs_0_ = bf16[4,256,1408]{2,1,0:T(8,128)(2,1)} custom-call(s32[1]{0:T(128)} %bitcast.26.where, bf16[768,2048]{1,0:T(8,128)(2,1)} %get-tuple-element.43.normed_ref.refs_0_, bf16[768,2048]{1,0:T(8,128)(2,1)} %collective-permute-done.32.refs_1_, bf16[768,2816]{1,0:T(8,128)(2,1)} %get-tuple-element.47.kept_ref.refs_2_, ...), custom_call_target="tpu_custom_call" | custom-call | flops 8999999488 | bytes 1350000 | tf_op jit(solution)/shard_map/block_products/pallas_call | solution.py:704
  471.6 12.4 %norm_back.1 = (f32[768,2048]{1,0:T(8,128)}, f32[1,2048]{1,0:T(1,128)}, bf16[768,2048]{1,0:T(8,128)(2,1)}) custom-call(f32[768,2048]{1,0:T(8,128)} %get-tuple-element.42.residual_ref.value_ref, f32[1,2048]{1,0:T(1,128)} %bitcast.161, bf16[768,2048]{1,0:T(8,128)(2,1)} %bitcast.142, bf16[768,512]{1,0:T(8,128)(2,1)} %feed_input.4.refs_4_.refs_0_, ...), custom_call_target="tpu_custom_call" | custom-call | flops 359999995904 | bytes 54000000 | tf_op jit(solution)/shard_map/norm_back/pallas_call | solution.py:404
  494.4 11.8 %attend_back.3 = (bf16[1024,256]{1,0:T(8,128)(2,1)S(1)}, bf16[4,128,256]{2,1,0:T(8,128)(2,1)S(1)}, bf16[4,128,256]{2,1,0:T(8,128)(2,1)S(1)}) custom-call(s32[2]{0:T(128)S(1)} %copy-done.46, bf16[1024,768]{1,0:T(8,128)(2,1)S(1)} %bitcast.97, bf16[4,256,768]{2,1,0:T(8,128)(2,1)S(1)} %pad_maximum_fusion.4.refs_2_.refs_3_, ...), custom_call_target="tpu_custom_call" | custom-call | flops 160000000000 | bytes 24000000 | tf_op jit(solution)/shard_map/attend_back/pallas_call | solution.py:622
  532.2 9.7 %block_products.14.refs_0_ = bf16[4,256,1408]{2,1,0:T(8,128)(2,1)} custom-call(s32[1]{0:T(128)} %bitcast.26.where, bf16[768,2048]{1,0:T(8,128)(2,1)} %get-tuple-element.43.normed_ref.refs_0_, bf16[768,2048]{1,0:T(8,128)(2,1)} %collective-permute-done.32.refs_1_, bf16[768,2816]{1,0:T(8,128)(2,1)} %get-tuple-element.47.kept_ref.refs_2_, ...), custom_call_target="tpu_custom_call" | custom-call | flops 8999999488 | bytes 1350000 | tf_op jit(solution)/shard_map/block_products/pallas_call | solution.py:704
  542.1 9.7 %collective-permute-done.43.refs_4_.refs_1_ = bf16[4,512,256]{2,1,0:T(8,128)(2,1)} collective-permute-done((bf16[4,512,256]{2,1,0:T(8,128)(2,1)}, bf16[4,512,256]{2,1,0:T(8,128)(2,1)}, u32[]{:S(2)}, u32[]{:S(2)}) %collective-permute-start.43) | collective-permute-done | bytes 1048608 | tf_op jit(solution)/shard_map/ppermute | solution.py:26
  555.1 11.9 %attend_back.4 = (bf16[1024,256]{1,0:T(8,128)(2,1)S(1)}, bf16[4,128,256]{2,1,0:T(8,128)(2,1)S(1)}, bf16[4,128,256]{2,1,0:T(8,128)(2,1)S(1)}) custom-call(s32[2]{0:T(128)S(1)} %copy-done.44, bf16[1024,768]{1,0:T(8,128)(2,1)S(1)} %bitcast.98, bf16[4,256,768]{2,1,0:T(8,128)(2,1)S(1)} %pad_maximum_fusion.4.refs_2_.refs_3_, ...), custom_call_target="tpu_custom_call" | custom-call | flops 160000000000 | bytes 24000000 | tf_op jit(solution)/shard_map/attend_back/pallas_call | solution.py:622
  574.5 7.6 add_three.1
  594.2 10.4 %collective-permute-start.63 = (bf16[256,1408]{1,0:T(8,128)(2,1)}, bf16[256,1408]{1,0:T(8,128)(2,1)}, u32[]{:S(2)}, u32[]{:S(2)}) collective-permute-start(bf16[256,1408]{1,0:T(8,128)(2,1)} %tie.49), channel_id=1, source_target_pairs={{0,4},{4,0},{2,6},{6,2},{1,5},{5,1},{3,7},{7,3},{8,12},{12,8},{10,... | collective-permute-start | bytes 2162696 | tf_op jit(solution)/shard_map/ppermute | solution.py:26
  609.3 12.2 %attend_back.5 = (bf16[1024,256]{1,0:T(8,128)(2,1)S(1)}, bf16[4,128,256]{2,1,0:T(8,128)(2,1)S(1)}, bf16[4,128,256]{2,1,0:T(8,128)(2,1)S(1)}) custom-call(s32[2]{0:T(128)S(1)} %copy-done.48, bf16[1024,768]{1,0:T(8,128)(2,1)} %bitcast.93, bf16[4,256,768]{2,1,0:T(8,128)(2,1)} %copy-done, bf16[4,256,768]{2,1,0:T(8,128)(2,1)} %copy-done, ...), custom_call_target="tpu_custom_call" | custom-call | flops 160000000000 | bytes 24000000 | tf_op jit(solution)/shard_map/attend_back/pallas_call | solution.py:622
  646.7 7.4 block_products.16.refs_1_.refs_4_
  703.6 13.6 %norm_back_rows.1 = (f32[768,2048]{1,0:T(8,128)}, f32[1,2048]{1,0:T(1,128)}) custom-call(bf16[768,2048]{1,0:T(8,128)(2,1)} %bitcast.105, f32[768,2048]{1,0:T(8,128)} %fusion.5.term_ref, f32[1,2048]{1,0:T(1,128)} %bitcast.159, f32[768,2048]{1,0:T(8,128)} %get-tuple-element.63.base_ref, bf16[256,2048]{1,0:T(8,128)(2,1)} %product.13.refs_4_.refs_0_, ...), custom_call_target="tpu_custom_call" | custom-call | flops 12999999488 | bytes 1950000 | tf_op jit(solution)/shard_map/norm_back_rows/pallas_call | solution.py:452
  (523 shorter events, 366.4 us)
Async XLA Ops:
  7.2 75.2 %all-gather.9.cloned.1.call-start = ((), (), s32[]{:S(2)}) async-start(), calls=%async_computation.10 | async-start | bytes 1310720 | tf_op jit(solution)/shard_map/all_gather | solution.py:825
  45.6 98.4 %all-gather.11.cloned.1.call-start = ((), (), s32[]{:S(2)}) async-start(), calls=%async_computation.11 | async-start | bytes 3604480 | tf_op jit(solution)/shard_map/all_gather | solution.py:825
  47.7 148.2 %all-gather.13.cloned.1.call-start = ((), (), s32[]{:S(2)}) async-start(), calls=%async_computation.12 | async-start | bytes 3604480 | tf_op jit(solution)/shard_map/all_gather | solution.py:825
  49.9 205.3 %all-gather.15.cloned.1.call-start = ((), (), s32[]{:S(2)}) async-start(), calls=%async_computation.13 | async-start | bytes 3604480 | tf_op jit(solution)/shard_map/all_gather | solution.py:825
  82.4 389.3 %reduce-scatter.6.cloned.1.call-start = ((), (), s32[]{:S(2)}) async-start(), calls=%async_computation.5 | async-start | bytes 7208960 | tf_op jit(solution)/shard_map/reduce_scatter | solution.py:750
  147.9 111.7 %collective-permute-start.21 = (bf16[3,128,2816]{2,1,0:T(8,128)(2,1)}, bf16[3,128,2816]{2,1,0:T(8,128)(2,1)}, u32[]{:S(2)}, u32[]{:S(2)}) collective-permute-start(bf16[3,128,2816]{2,1,0:T(8,128)(2,1)} %pad_maximum_fusion.refs_5_.refs_1_), channel_id=1, source_target_pairs={{0,4},{4,0},{2,6},{6,2},{1,5},{5,1},{3,7},{7,3},{8,12},{12,8},{10,... | collective-permute-start | bytes 6488072 | tf_op jit(solution)/shard_map/ppermute | solution.py:26
  165.4 42.0 %collective-permute-start.18 = (bf16[256,2048]{1,0:T(8,128)(2,1)}, bf16[256,2048]{1,0:T(8,128)(2,1)}, u32[]{:S(2)}, u32[]{:S(2)}) collective-permute-start(bf16[256,2048]{1,0:T(8,128)(2,1)} %product.8.refs_5_.refs_0_), channel_id=1, source_target_pairs={{0,1},{1,0},{2,3},{3,2},{4,5},{5,4},{6,7},{7,6},{8,9},{9,8},{10,11... | collective-permute-start | bytes 3145736 | tf_op jit(solution)/shard_map/ppermute | solution.py:883
  199.2 61.5 %collective-permute-start.25 = (bf16[3,128,2816]{2,1,0:T(8,128)(2,1)}, bf16[3,128,2816]{2,1,0:T(8,128)(2,1)}, u32[]{:S(2)}, u32[]{:S(2)}) collective-permute-start(bf16[3,128,2816]{2,1,0:T(8,128)(2,1)} %pad_maximum_fusion.1.refs_6_), channel_id=1, source_target_pairs={{0,4},{4,0},{2,6},{6,2},{1,5},{5,1},{3,7},{7,3},{8,12},{12,8},{10,... | collective-permute-start | bytes 6488072 | tf_op jit(solution)/shard_map/ppermute | solution.py:26
  234.4 34.9 %collective-permute-start.22 = (bf16[3,128,2816]{2,1,0:T(8,128)(2,1)}, bf16[3,128,2816]{2,1,0:T(8,128)(2,1)}, u32[]{:S(2)}, u32[]{:S(2)}) collective-permute-start(bf16[3,128,2816]{2,1,0:T(8,128)(2,1)} %pad_maximum_fusion.refs_5_.refs_1_), channel_id=1, source_target_pairs={{0,2},{2,0},{4,6},{6,4},{1,3},{3,1},{5,7},{7,5},{8,10},{10,8},{12,... | collective-permute-start | bytes 6488072 | tf_op jit(solution)/shard_map/ppermute | solution.py:22
  234.4 34.9 %collective-permute-start.24 = (bf16[3,128,2816]{2,1,0:T(8,128)(2,1)}, bf16[3,128,2816]{2,1,0:T(8,128)(2,1)}, u32[]{:S(2)}, u32[]{:S(2)}) collective-permute-start(bf16[3,128,2816]{2,1,0:T(8,128)(2,1)} %pad_maximum_fusion.1.refs_6_), channel_id=1, source_target_pairs={{0,2},{2,0},{4,6},{6,4},{1,3},{3,1},{5,7},{7,5},{8,10},{10,8},{12,... | collective-permute-start | bytes 6488072 | tf_op jit(solution)/shard_map/ppermute | solution.py:22
  258.5 48.2 %collective-permute-start.27 = (bf16[3,704,512]{2,1,0:T(8,128)(2,1)}, bf16[3,704,512]{2,1,0:T(8,128)(2,1)}, u32[]{:S(2)}, u32[]{:S(2)}) collective-permute-start(bf16[3,704,512]{2,1,0:T(8,128)(2,1)} %pad_maximum_fusion.2.refs_7_.refs_0_), channel_id=1, source_target_pairs={{0,4},{4,0},{2,6},{6,2},{1,5},{5,1},{3,7},{7,3},{8,12},{12,8},{10,... | collective-permute-start | bytes 6488072 | tf_op jit(solution)/shard_map/ppermute | solution.py:26
  315.9 197.7 %collective-permute-start.40 = (bf16[512,768]{1,0:T(8,128)(2,1)}, bf16[512,768]{1,0:T(8,128)(2,1)}, u32[]{:S(2)}, u32[]{:S(2)}) collective-permute-start(bf16[512,768]{1,0:T(8,128)(2,1)} %get-tuple-element.95), channel_id=1, source_target_pairs={{0,2},{2,0},{4,6},{6,4},{1,3},{3,1},{5,7},{7,5},{8,10},{10,8},{12,... | collective-permute-start | bytes 2359304 | tf_op jit(solution)/shard_map/ppermute | solution.py:22
  320.1 57.6 %collective-permute-start.32 = (bf16[768,2048]{1,0:T(8,128)(2,1)}, bf16[768,2048]{1,0:T(8,128)(2,1)}, u32[]{:S(2)}, u32[]{:S(2)}) collective-permute-start(bf16[768,2048]{1,0:T(8,128)(2,1)} %get-tuple-element.43.normed_ref.refs_0_), channel_id=1, source_target_pairs={{0,2},{2,0},{4,6},{6,4},{1,3},{3,1},{5,7},{7,5},{8,10},{10,8},{12,... | collective-permute-start | bytes 9437192 | tf_op jit(solution)/shard_map/ppermute | solution.py:22
  336.3 255.8 %reduce-scatter.14.cloned.1.call-start = ((), (), s32[]{:S(2)}) async-start(), calls=%async_computation.9 | async-start | bytes 3604480 | tf_op jit(solution)/shard_map/reduce_scatter | solution.py:750
  397.0 63.7 %collective-permute-start.39 = (bf16[4,256,1408]{2,1,0:T(8,128)(2,1)}, bf16[4,256,1408]{2,1,0:T(8,128)(2,1)}, u32[]{:S(2)}, u32[]{:S(2)}) collective-permute-start(bf16[4,256,1408]{2,1,0:T(8,128)(2,1)} %tie.37.rest_0_), channel_id=1, source_target_pairs={{0,4},{4,0},{2,6},{6,2},{1,5},{5,1},{3,7},{7,3},{8,12},{12,8},{10,... | collective-permute-start | bytes 8650760 | tf_op jit(solution)/shard_map/ppermute | solution.py:26
  408.4 53.5 %collective-permute-start.37 = (bf16[768,512]{1,0:T(8,128)(2,1)}, bf16[768,512]{1,0:T(8,128)(2,1)}, u32[]{:S(2)}, u32[]{:S(2)}) collective-permute-start(bf16[768,512]{1,0:T(8,128)(2,1)} %feed_input.6.rest_0_.refs_4_.refs_2_), channel_id=1, source_target_pairs={{0,1},{1,0},{2,3},{3,2},{4,5},{5,4},{6,7},{7,6},{8,9},{9,8},{10,11... | collective-permute-start | bytes 2359304 | tf_op jit(solution)/shard_map/ppermute | solution.py:921
  429.0 42.7 %collective-permute-start.38 = (bf16[768,512]{1,0:T(8,128)(2,1)}, bf16[768,512]{1,0:T(8,128)(2,1)}, u32[]{:S(2)}, u32[]{:S(2)}) collective-permute-start(bf16[768,512]{1,0:T(8,128)(2,1)} %feed_input.7.rest_0_.refs_3_), channel_id=1, source_target_pairs={{0,1},{1,0},{2,3},{3,2},{4,5},{5,4},{6,7},{7,6},{8,9},{9,8},{10,11... | collective-permute-start | bytes 2359304 | tf_op jit(solution)/shard_map/ppermute | solution.py:921
  443.8 109.0 %collective-permute-start.36 = (bf16[768,2048]{1,0:T(8,128)(2,1)}, bf16[768,2048]{1,0:T(8,128)(2,1)}, u32[]{:S(2)}, u32[]{:S(2)}) collective-permute-start(bf16[768,2048]{1,0:T(8,128)(2,1)} %product.11.mine_ref.refs_5_.refs_8_), channel_id=1, source_target_pairs={{0,1},{1,0},{2,3},{3,2},{4,5},{5,4},{6,7},{7,6},{8,9},{9,8},{10,11... | collective-permute-start | bytes 9437192 | tf_op jit(solution)/shard_map/ppermute | solution.py:931
  460.7 62.8 %collective-permute-start.42 = (bf16[4,256,1408]{2,1,0:T(8,128)(2,1)}, bf16[4,256,1408]{2,1,0:T(8,128)(2,1)}, u32[]{:S(2)}, u32[]{:S(2)}) collective-permute-start(bf16[4,256,1408]{2,1,0:T(8,128)(2,1)} %tie.38.refs_6_), channel_id=1, source_target_pairs={{0,4},{4,0},{2,6},{6,2},{1,5},{5,1},{3,7},{7,3},{8,12},{12,8},{10,... | collective-permute-start | bytes 8650760 | tf_op jit(solution)/shard_map/ppermute | solution.py:26
  493.3 112.4 %reduce-scatter.8.cloned.1.call-start = ((), (), s32[]{:S(2)}) async-start(), calls=%async_computation.6 | async-start | bytes 3604480 | tf_op jit(solution)/shard_map/reduce_scatter | solution.py:750
  529.4 39.9 %collective-permute-start.44 = (bf16[256,2048]{1,0:T(8,128)(2,1)}, bf16[256,2048]{1,0:T(8,128)(2,1)}, u32[]{:S(2)}, u32[]{:S(2)}) collective-permute-start(bf16[256,2048]{1,0:T(8,128)(2,1)} %product.13.refs_4_.refs_0_), channel_id=1, source_target_pairs={{0,1},{1,0},{2,3},{3,2},{4,5},{5,4},{6,7},{7,6},{8,9},{9,8},{10,11... | collective-permute-start | bytes 3145736 | tf_op jit(solution)/shard_map/ppermute | solution.py:958
  542.0 104.6 %reduce-scatter.10.cloned.1.call-start = ((), (), s32[]{:S(2)}) async-start(), calls=%async_computation.7 | async-start | bytes 1310720 | tf_op jit(solution)/shard_map/reduce_scatter | solution.py:750
  551.8 42.4 %collective-permute-start.46 = (bf16[2816,256]{1,0:T(8,128)(2,1)}, bf16[2816,256]{1,0:T(8,128)(2,1)}, u32[]{:S(2)}, u32[]{:S(2)}) collective-permute-start(bf16[2816,256]{1,0:T(8,128)(2,1)} %tie.42), channel_id=1, source_target_pairs={{0,4},{4,0},{2,6},{6,2},{1,5},{5,1},{3,7},{7,3},{8,12},{12,8},{10,... | collective-permute-start | bytes 4325384 | tf_op jit(solution)/shard_map/ppermute | solution.py:26
  574.4 31.4 %collective-permute-start.45 = (bf16[256,2048]{1,0:T(8,128)(2,1)}, bf16[256,2048]{1,0:T(8,128)(2,1)S(1)}, u32[]{:S(2)}, u32[]{:S(2)}) collective-permute-start(bf16[256,2048]{1,0:T(8,128)(2,1)} %product.14.refs_5_.refs_1_), channel_id=1, source_target_pairs={{0,1},{1,0},{2,3},{3,2},{4,5},{5,4},{6,7},{7,6},{8,9},{9,8},{10,11... | collective-permute-start | bytes 3145736 | tf_op jit(solution)/shard_map/ppermute | solution.py:958
  574.5 72.1 %collective-permute-start.48 = (bf16[768,2048]{1,0:T(8,128)(2,1)}, bf16[768,2048]{1,0:T(8,128)(2,1)}, u32[]{:S(2)}, u32[]{:S(2)}) collective-permute-start(bf16[768,2048]{1,0:T(8,128)(2,1)} %copy-done.72), channel_id=1, source_target_pairs={{0,2},{2,0},{4,6},{6,4},{1,3},{3,1},{5,7},{7,5},{8,10},{10,8},{12,... | collective-permute-start | bytes 9437192 | tf_op jit(solution)/shard_map/ppermute | solution.py:22
  594.2 31.4 %collective-permute-start.63 = (bf16[256,1408]{1,0:T(8,128)(2,1)}, bf16[256,1408]{1,0:T(8,128)(2,1)}, u32[]{:S(2)}, u32[]{:S(2)}) collective-permute-start(bf16[256,1408]{1,0:T(8,128)(2,1)} %tie.49), channel_id=1, source_target_pairs={{0,4},{4,0},{2,6},{6,2},{1,5},{5,1},{3,7},{7,3},{8,12},{12,8},{10,... | collective-permute-start | bytes 2162696 | tf_op jit(solution)/shard_map/ppermute | solution.py:26
  605.7 142.7 %reduce-scatter.12.cloned.1.call-start = ((), (), s32[]{:S(2)}) async-start(), calls=%async_computation.8 | async-start | bytes 2621440 | tf_op jit(solution)/shard_map/reduce_scatter | solution.py:750
  628.1 36.8 %collective-permute-start.64 = (bf16[512,1408]{1,0:T(8,128)(2,1)}, bf16[512,1408]{1,0:T(8,128)(2,1)}, u32[]{:S(2)}, u32[]{:S(2)}) collective-permute-start(bf16[512,1408]{1,0:T(8,128)(2,1)} %pad_maximum_fusion.6), channel_id=1, source_target_pairs={{0,2},{2,0},{4,6},{6,4},{1,3},{3,1},{5,7},{7,5},{8,10},{10,8},{12,... | collective-permute-start | bytes 4325384 | tf_op jit(solution)/shard_map/ppermute | solution.py:22
  645.5 57.0 %collective-permute-start.52 = (bf16[256,2048]{1,0:T(8,128)(2,1)}, bf16[256,2048]{1,0:T(8,128)(2,1)}, u32[]{:S(2)}, u32[]{:S(2)}) collective-permute-start(bf16[256,2048]{1,0:T(8,128)(2,1)} %product.15.refs_4_.refs_2_), channel_id=1, source_target_pairs={{0,1},{1,0},{2,3},{3,2},{4,5},{5,4},{6,7},{7,6},{8,9},{9,8},{10,11... | collective-permute-start | bytes 3145736 | tf_op jit(solution)/shard_map/ppermute | solution.py:958
  675.5 52.4 %collective-permute-start.62 = (bf16[512,512]{1,0:T(8,128)(2,1)}, bf16[512,512]{1,0:T(8,128)(2,1)}, u32[]{:S(2)}, u32[]{:S(2)}) collective-permute-start(bf16[512,512]{1,0:T(8,128)(2,1)} %pad_maximum_fusion.10), channel_id=1, source_target_pairs={{0,2},{2,0},{4,6},{6,4},{1,3},{3,1},{5,7},{7,5},{8,10},{10,8},{12,... | collective-permute-start | bytes 1572872 | tf_op jit(solution)/shard_map/ppermute | solution.py:22
  685.2 32.0 %collective-permute-start.58 = (bf16[512,128]{1,0:T(8,128)(2,1)S(1)}, bf16[512,128]{1,0:T(8,128)(2,1)S(1)}, u32[]{:S(2)}, u32[]{:S(2)}) collective-permute-start(bf16[512,128]{1,0:T(8,128)(2,1)S(1)} %get-tuple-element.121), channel_id=1, source_target_pairs={{0,24},{8,0},{16,8},{24,16},{1,25},{9,1},{17,9},{25,17},{2,26},{10... | collective-permute-start | bytes 393224 | tf_op jit(solution)/shard_map/ppermute | solution.py:758
  702.4 42.5 %collective-permute-start.66 = (bf16[512,1408]{1,0:T(8,128)(2,1)}, bf16[512,1408]{1,0:T(8,128)(2,1)}, u32[]{:S(2)}, u32[]{:S(2)}) collective-permute-start(bf16[512,1408]{1,0:T(8,128)(2,1)} %pad_maximum_fusion.7), channel_id=1, source_target_pairs={{0,2},{2,0},{4,6},{6,4},{1,3},{3,1},{5,7},{7,5},{8,10},{10,8},{12,... | collective-permute-start | bytes 4325384 | tf_op jit(solution)/shard_map/ppermute | solution.py:22
  (153 other events, 2201.9 us)
Sparse Core Ops, SparseCore 0:
  45.7 29.8 all-gather.8
  77.7 58.6 all-gather.10
  138.0 57.8 all-gather.12
  197.3 57.8 all-gather.14
  336.4 100.5 reduce-scatter.5
  493.4 53.9 reduce-scatter.13
  549.6 56.0 reduce-scatter.7
  608.6 27.0 reduce-scatter.9
  669.4 56.9 reduce-scatter.11
